TPU v7x, 256 devices: a whole 4x4x8 slice. The times are simulated.
256 devices in a mesh: ia: 8 (over x, core), ja: 32 (over y, z).
Axes of the slice: x: 4, y: 4, z: 8, core: 2. Of those that a mesh axis runs over, the one named last changes fastest.
Arguments:
- state: float32 [12, 65536], P(None, 'ja'), may hold values from -6 to 6
- mass: float32 [65536], P('ja'), may hold values from 0.2 to 5
- elapsed: float32 [65536], P('ja'), may hold values from 0.05 to 0.5
- active_ids: int32 [16384], P('ia'), may hold values from 0 to 65535, as said below
- active_count: int32 [8], replicated, may hold values from 256 to 2048, as said below
Outputs:
- new_state: float32 [12, 65536], P(None, 'ja')
- active_force: float32 [6, 16384], P(None, 'ia')
Inputs may be any that keep to these rules, and one draw needn't show every extreme that they name: `active_ids`: all entries are distinct star numbers. `active_count`: one list in every draw is full.
All inputs are finite; a program needn't handle non-finite values.
Results may differ from a plain program's by a relative error of at most 0.000047.
Values sent between devices are 32-bit elements; how exact they have to be, the bound alone decides.
No kernel may reach another device: no remote copies, remote signals or barrier semaphores. Data moves between devices by JAX's collectives and lax.ppermute only.
A program may use at most 64 MiB of HBM per device.

v0:
```python
import jax
import jax.numpy as jnp
from jax import lax
from jax.sharding import PartitionSpec as P

softening_square = 0.01


def predict(state, elapsed):
    position = state[0:3]
    velocity = state[3:6]
    accel_old = state[6:9]
    jerk_old = state[9:12]
    half = elapsed * elapsed * 0.5
    sixth = half * elapsed / 3.0
    new_pos = position + velocity * elapsed + accel_old * half + jerk_old * sixth
    new_vel = velocity + accel_old * elapsed + jerk_old * half
    return (new_pos, new_vel)


def pair_terms(target_pos, target_vel, source_pos, source_vel, source_mass, scale):
    separation = source_pos[:, None, :] - target_pos[:, :, None]
    relative = source_vel[:, None, :] - target_vel[:, :, None]
    square = jnp.sum(separation * separation, axis=0) + softening_square
    inverse = 1.0 / jnp.sqrt(square)
    weight = source_mass[None, :] * inverse * inverse * inverse * scale
    radial = 3.0 * jnp.sum(separation * relative, axis=0) / square
    accel_sum = jnp.sum(weight[None] * separation, axis=2)
    jerk_sum = jnp.sum(weight[None] * (relative - radial[None] * separation), axis=2)
    return jnp.concatenate([accel_sum, jerk_sum], axis=0)


def correct(old, step_time, force):
    position = old[0:3]
    velocity = old[3:6]
    accel_old = old[6:9]
    jerk_old = old[9:12]
    accel_new = force[0:3]
    jerk_new = force[3:6]
    half = step_time * 0.5
    twelfth = step_time * step_time / 12.0
    vel_new = velocity + (accel_old + accel_new) * half + (jerk_old - jerk_new) * twelfth
    pos_new = position + (velocity + vel_new) * half + (accel_old - accel_new) * twelfth
    return jnp.concatenate([pos_new, vel_new, accel_new, jerk_new], axis=0)


def body(state, mass, elapsed, active_ids, active_count):
    star_dev = state.shape[1]
    capacity = active_ids.shape[0]
    groups_ia = lax.axis_size("ia")
    my_list = lax.axis_index("ia")
    my_field = lax.axis_index("ja")
    tile_rows = 128
    scale = 1.0 / (star_dev * lax.axis_size("ja"))
    every_slot = jnp.arange(groups_ia * capacity, dtype=jnp.int32)
    slot_counts = jnp.repeat(active_count, capacity)
    position_in = jnp.arange(capacity, dtype=jnp.int32)
    live = active_count[my_list]
    local = active_ids - my_field * star_dev
    owned = (local >= 0) & (local < star_dev) & (position_in < live)
    extended = jnp.concatenate([state, elapsed[None]], axis=0)
    picked = jnp.take(extended, jnp.clip(local, 0, star_dev - 1), axis=1)
    picked = jnp.where(owned[None], picked, 0.0)
    record = lax.psum(picked, "ja")
    old = record[0:12]
    step_time = record[12]
    act_pos, act_vel = predict(old, step_time)
    pred_pos, pred_vel = predict(state, elapsed)

    def add_tile(turn, running):
        begin = turn * tile_rows
        tile_pos = lax.dynamic_slice_in_dim(act_pos, begin, tile_rows, 1)
        tile_vel = lax.dynamic_slice_in_dim(act_vel, begin, tile_rows, 1)
        terms = pair_terms(tile_pos, tile_vel, pred_pos, pred_vel, mass, scale)
        return lax.dynamic_update_slice_in_dim(running, terms, begin, 1)

    count_tiles = (live + tile_rows - 1) // tile_rows
    partial_force = lax.fori_loop(0, count_tiles, add_tile, jnp.zeros((6, capacity), jnp.float32))
    force = lax.psum(partial_force, "ja")
    fresh = correct(old, step_time, force)
    gathered, gathered_ids = (
        lax.all_gather(fresh, "ia", axis=1, tiled=True),
        lax.all_gather(active_ids, "ia", axis=0, tiled=True),
    )
    valid_back = every_slot % capacity < slot_counts
    active_force = jnp.where((position_in < live)[None], force, 0.0)
    local_back = gathered_ids - my_field * star_dev
    keep = valid_back & (local_back >= 0) & (local_back < star_dev)
    target = jnp.where(keep, local_back, star_dev).astype(jnp.int32)
    new_state = state.at[:, target].set(gathered, mode="drop")
    return (new_state, active_force)


def solution(mesh):
    placed = (P(None, "ja"), P("ja"), P("ja"), P("ia"), P())
    return jax.shard_map(
        body, mesh=mesh, in_specs=placed, out_specs=(P(None, "ja"), P(None, "ia")), check_vma=False
    )
```

profile of v0, /device:TPU:1, one launch (start us, length us, event | category | flops | bytes accessed | tf_op | source)
XLA Modules:
  0.0 394.3 jit_solution(12631693500377681800)
XLA Ops:
  7.3 1.3 dynamic_slice.9
  8.6 0.7 fusion.12
  9.3 1.4 compare_and_fusion
  10.7 0.9 pad_maximum_fusion
  12.0 5.5 %gather_fusion = f32[2048,13]{1,0:T(8,128)S(1)} fusion(f32[13,2048]{0,1:T(8,128)S(1)} %copy.76, s32[2048]{0:T(1024)S(1)} %fusion.12), kind=kCustom, calls=%fused_computation | custom fusion | bytes 221184 | tf_op jit(solution)/shard_map/jit(_take)/gather | solution.py:62
  17.8 0.7 select_bitcast_fusion
  19.3 15.8 %all_gather.6 = s32[16384]{0:T(1024)S(1)} all-gather(s32[2048]{0:T(1024)S(1)} %copy-done.4), channel_id=1, replica_groups=mesh['ia'=8,'ja'=32] {'ia'}, dimensions={0}, use_global_device_ids=true | all-gather | bytes 73728 | tf_op jit(solution)/shard_map/all_gather | solution.py:83
  36.3 123.2 %all-reduce.2.cloned.1.call-done = f32[13,2048]{1,0:T(8,128)} async-done(((f32[13,2048]{1,0:T(8,128)}), f32[13,2048]{1,0:T(8,128)}) %all-reduce.2.cloned.1.call-update) | async-done | bytes 106512 | tf_op jit(solution)/shard_map/psum | solution.py:64
  159.5 0.9 broadcast_multiply_fusion
  160.3 1.0 multiply_add_fusion.1
  161.4 39.0 %while.10 = (s32[]{:T(128)}, f32[6,2048]{1,0:T(8,128)S(1)}, s32[]{:T(128)}, f32[3,2048]{1,0:T(4,128)S(1)}, f32[3,2048]{1,0:T(4,128)S(1)}, /*index=5*/f32[2048]{0...) while((s32[]{:T(128)}, f32[6,2048]{1,0:T(8,128)S(1)}, ...), condition=%wide.region_6.7_spmd, body=%wide.region_1.0_spmd.sunk | while | flops 12320774 | bytes 8518827 | solution.py:78
  161.4 0.8 fusion.16
  162.6 1.2 fusion.17
  163.9 0.8 fusion.16
  165.1 1.2 fusion.17
  166.3 0.8 fusion.16
  167.5 1.2 fusion.17
  168.8 0.8 fusion.16
  169.9 1.2 fusion.17
  171.2 0.8 fusion.16
  172.4 1.2 fusion.17
  173.6 0.8 fusion.16
  174.8 1.2 fusion.17
  176.1 0.8 fusion.16
  177.3 1.2 fusion.17
  178.5 0.8 fusion.16
  179.7 1.2 fusion.17
  180.9 0.8 fusion.16
  182.1 1.2 fusion.17
  183.4 0.8 fusion.16
  184.6 1.2 fusion.17
  185.8 0.8 fusion.16
  187.0 1.2 fusion.17
  188.2 0.8 fusion.16
  189.4 1.2 fusion.17
  190.7 0.8 fusion.16
  191.9 1.2 fusion.17
  193.1 0.8 fusion.16
  194.3 1.2 fusion.17
  195.5 0.8 fusion.16
  196.7 1.2 fusion.17
  198.0 0.8 fusion.16
  199.2 1.2 fusion.17
  200.4 113.2 %psum.15 = f32[6,2048]{1,0:T(8,128)S(1)} all-reduce(f32[6,2048]{1,0:T(8,128)S(1)} %get-tuple-element.45), channel_id=1, replica_groups=mesh['ia'=8,'ja'=32] {'ja'}, use_global_device_ids=true, to_apply=%region_7.8 | all-reduce | flops 12288 | bytes 98304 | tf_op jit(solution)/shard_map/psum | solution.py:79
  314.3 26.4 %all_gather.7 = f32[12,16384]{1,0:T(8,128)S(1)} all-gather(f32[12,2048]{1,0:T(8,128)S(1)} %pad_maximum_fusion.1), channel_id=1, replica_groups=mesh['ia'=8,'ja'=32] {'ia'}, dimensions={1}, use_global_device_ids=true | all-gather | bytes 884736 | tf_op jit(solution)/shard_map/all_gather | solution.py:82
  340.8 4.6 %copy.79 = f32[16384,12]{1,0:T(8,128)} copy(f32[16384,12]{0,1:T(8,128)S(1)} %bitcast.14) | data formatting | bytes 1572864 | tf_op jit(solution)/shard_map/all_gather | solution.py:82
  345.4 41.1 %scatter_fusion = f32[12,2048]{0,1:T(8,128)S(1)} fusion(f32[12,2048]{0,1:T(8,128)S(1)} %copy.78, s32[16384]{0:T(1024)S(1)} %compare_select_fusion, f32[16384,12]{1,0:T(8,128)} %copy.79), kind=kCustom, calls=%fused_computation.1 | custom fusion | bytes 2424832 | tf_op jit(solution)/shard_map/scatter | solution.py:90
  386.5 1.0 copy.80
  (75 shorter events, 8.9 us)
Async XLA Ops:
  7.2 12.1 %copy-start.5 = (s32[8]{0:T(128)S(1)}, s32[8]{0:T(128)}, u32[]{:S(2)}) copy-start(s32[8]{0:T(128)} %param.11) | copy-start | bytes 100
  7.2 12.1 %copy-start.4 = (s32[2048]{0:T(1024)S(1)}, s32[2048]{0:T(1024)}, u32[]{:S(2)}) copy-start(s32[2048]{0:T(1024)} %param.10) | copy-start | bytes 24580
  7.2 27.9 %copy-start = (f32[12,2048]{1,0:T(8,128)S(1)}, f32[12,2048]{1,0:T(8,128)}, u32[]{:S(2)}) copy-start(f32[12,2048]{1,0:T(8,128)} %param.7) | copy-start | bytes 294916
  7.2 12.0 %copy-start.3 = (f32[2048]{0:T(1024)S(1)}, f32[2048]{0:T(1024)}, u32[]{:S(2)}) copy-start(f32[2048]{0:T(1024)} %param.9) | copy-start | bytes 24580
  7.2 152.2 %all-reduce.2.cloned.1.call-start = ((), (), s32[]{:S(2)}) async-start(), calls=%async_computation | async-start | bytes 262144 | tf_op jit(solution)/shard_map/psum | solution.py:64
  11.6 149.8 %copy-start.2 = (f32[2048]{0:T(1024)S(1)}, f32[2048]{0:T(1024)}, u32[]{:S(2)}) copy-start(f32[2048]{0:T(1024)} %param.8) | copy-start | bytes 24580
  161.4 152.8 %copy-start.1 = (f32[13,2048]{1,0:T(8,128)S(1)}, f32[13,2048]{1,0:T(8,128)}, u32[]{:S(2)}) copy-start(f32[13,2048]{1,0:T(8,128)} %all-reduce.2.cloned.1.call-done) | copy-start | bytes 319492
Sparse Core Ops, SparseCore 0:
  18.6 140.7 all-reduce.1
where the time goes:
time: 394 us
  blocking collectives  155 us (39%)
  waiting for transfers between devices  123 us (31%)
  local copies, waits for them, and re-layouts  54.8 us (14%)
  other arithmetic  45.2 us (11%)
  between operations  14.9 us (4%)
    psum x1, waiting for transfers between devices, body(): record = lax.psum(picked, 'ja')  123 us
    psum x1, blocking collectives, body(): force = lax.psum(partial_force, 'ja')  113 us
    scatter x1, local copies, waits for them, and re-layouts, body(): new_state = state.at[:, target].set(gathered, mode='drop')  41.1 us
    all_gather x1, blocking collectives, body(): lax.all_gather(fresh, 'ia', axis=1, tiled=True)  26.4 us
    reduce_sum x16, other arithmetic, pair_terms(): accel_sum = jnp.sum(weight[None] * separation, axis=2)  18.9 us
    all_gather x1, blocking collectives, body(): lax.all_gather(active_ids, 'ia', axis=0, tiled=True)  15.8 us
    reduce_sum x16, other arithmetic, pair_terms(): square = jnp.sum(separation * separation, axis=0) + softening_square  13.2 us
  transfers between devices with their start and end apart: 1, of which 1 were waited for; matrix products, arithmetic and copies ran while one was open for 0% of the time, Pallas kernels for 0%

commit v1 on v0

v1 whole, which is shorter than its diff:
```python
import jax
import jax.numpy as jnp
from jax import lax
from jax.experimental import pallas as pl
from jax.experimental.pallas import tpu as pltpu
from jax.sharding import Mesh, PartitionSpec as P

F32 = jnp.float32
I32 = jnp.int32
softening_square = 0.01
LISTS = 8
CAP = 2048
SHARD = 2048
GROUPS = 64
LANES = 128
BLOCKS = 128
SMEM = pl.BlockSpec(memory_space=pltpu.SMEM)
VMEM = pl.BlockSpec(memory_space=pltpu.VMEM)


def take(tile, index):
    return jnp.take_along_axis(tile, index, axis=1, mode="promise_in_bounds")


def list_offsets(counts_ref):
    offsets = [jnp.int32(0)]
    for i in range(LISTS):
        offsets.append(offsets[-1] + counts_ref[i])
    return offsets[:LISTS], offsets[LISTS]


def group_size(live):
    return lax.shift_right_logical(live + (GROUPS - 1), 6)


def split_position(position, size):
    group = jnp.floor((position.astype(F32) + 0.5) / size.astype(F32)).astype(I32)
    lane = position - group * size
    return group * 2 + (lane >> 7), lane & 127


def pack_kernel(state_ref, mass_ref, elapsed_ref, ids_ref, out_ref):
    eighth = lax.axis_index("x") * 2 + lax.axis_index("c")
    part = pl.ds(pl.multiple_of(eighth * 256, 256), 256)
    piece = pl.ds(pl.multiple_of(lax.axis_index("z") * 256, 256), 256)
    old = state_ref[:, part]
    step = elapsed_ref[:, part]
    half = step * step * 0.5
    sixth = half * step / 3.0
    pos = old[0:3] + old[3:6] * step + old[6:9] * half + old[9:12] * sixth
    vel = old[3:6] + old[6:9] * step + old[9:12] * half
    mass = mass_ref[:, part] * (1.0 / 65536.0)
    ids = ids_ref[:, piece].astype(F32)
    rows = jnp.concatenate([pos, vel, mass, ids], axis=0)
    both = jnp.concatenate([rows[:, :LANES], rows[:, LANES:]], axis=0)
    for peer in range(32):
        out_ref[peer] = both


def extract_kernel(counts_ref, slab_ref, out_ref):
    offsets, live = list_offsets(counts_ref)
    size = group_size(live)
    group = lax.axis_index("c") * 32 + lax.axis_index("x") * 8 + lax.axis_index("z")
    my_y = lax.axis_index("y")
    sub = lax.broadcasted_iota(I32, (8, LANES), 0)
    column = lax.broadcasted_iota(I32, (8, LANES), 1)

    def one_half(half):
        lane = column + half * LANES
        position = group * size + lane
        valid = (lane < size) & (position < live)
        which = jnp.zeros((8, LANES), I32)
        base = jnp.zeros((8, LANES), I32)
        for i in range(1, LISTS):
            after = position >= offsets[i]
            which = jnp.where(after, i, which)
            base = jnp.where(after, offsets[i], base)
        slot = jnp.where(valid, position - base, 0)
        block = (which & 1) * 64 + (which >> 1) * 16 + (slot >> 8) * 2 + ((slot >> 7) & 1)
        within = slot & 127
        found = jnp.zeros((8, LANES), F32)
        for v in range(16):
            tile = slab_ref[pl.ds(7 + 64 * v, 8, stride=8), :]
            found = jnp.where(block == v * 8 + sub, take(tile, within), found)
        star = jnp.broadcast_to(jnp.sum(found, axis=0, keepdims=True), (8, LANES)).astype(I32)
        mine = valid & ((star >> 14) == my_y)
        place = ((star >> 8) & 1) * 64 + ((star >> 9) & 3) * 16 + ((star >> 11) & 7) * 2 + ((star >> 7) & 1)
        place = jnp.where(mine, place, -1)
        inside = star & 127

        def step(turn, acc):
            for k in range(16):
                b = turn * 16 + k
                tile = slab_ref[pl.ds(pl.multiple_of(b * 8, 8), 8), :]
                acc = jnp.where(place == b, take(tile, inside), acc)
            return acc

        picked = lax.fori_loop(0, BLOCKS // 16, step, jnp.zeros((8, LANES), F32))
        out_ref[half * 8 : half * 8 + 8, :] = jnp.where(sub < 6, picked, 0.0)

    one_half(0)
    out_ref[8:16, :] = jnp.zeros((8, LANES), F32)

    @pl.when(size > LANES)
    def _():
        one_half(1)


def inverse_kernel(counts_ref, slab_ref, block_ref, lane_ref):
    offsets, live = list_offsets(counts_ref)
    size = group_size(live)
    shard = lax.axis_index("y") * 8 + lax.axis_index("z")
    wide = 2 * LANES
    row16 = lax.broadcasted_iota(I32, (16, wide), 0)
    row128 = lax.broadcasted_iota(I32, (LANES, wide), 0)
    column = lax.broadcasted_iota(I32, (1, wide), 1)
    total = jnp.zeros((32, LANES), F32)
    for i in range(LISTS):
        first = ((i & 1) * 32 + (i >> 1) * 8) * 16

        def step(turn, acc):
            row = first + turn * 16
            ids = jnp.concatenate(
                [slab_ref[pl.ds(row + 7, 1), :], slab_ref[pl.ds(row + 15, 1), :]], axis=1
            ).astype(I32)
            slot = turn * wide + column
            mine = (slot < counts_ref[i]) & ((ids >> 11) == shard)
            high = jnp.where(mine, (ids >> 7) & 15, -1)
            low = ids & 127
            mark = offsets[i] + slot + 1
            here = row16 == high
            left = jnp.concatenate(
                [
                    jnp.where(here, (mark >> 7).astype(F32), 0.0),
                    jnp.where(here, (mark & 127).astype(F32), 0.0),
                ],
                axis=0,
            ).astype(jnp.bfloat16)
            right = jnp.where(row128 == low, 1.0, 0.0).astype(jnp.bfloat16)
            return acc + lax.dot_general(
                left, right, (((1,), (1,)), ((), ())), preferred_element_type=F32
            )

        total = lax.fori_loop(0, (counts_ref[i] + (wide - 1)) >> 8, step, total)
    position = (total[0:16] * 128.0 + total[16:32]).astype(I32) - 1
    block, lane = split_position(position, size)
    block_ref[...] = jnp.where(position >= 0, block, -1)
    lane_ref[...] = jnp.where(position >= 0, lane, 0)


def pair_kernel(counts_ref, own_ref, one_ref, two_ref, three_ref, slab_ref, out_ref, target_ref, sum_ref):
    _, live = list_offsets(counts_ref)
    size = group_size(live)
    targets = own_ref[...] + one_ref[...] + two_ref[...] + three_ref[...]
    pad = jnp.zeros((LANES - 8, LANES), F32)
    for half in range(2):
        rows = jnp.concatenate([targets[half * 8 : half * 8 + 8], pad], axis=0)
        target_ref[half * LANES : (half + 1) * LANES, :] = rows.T
    sum_ref[...] = jnp.zeros_like(sum_ref)
    column = lax.broadcasted_iota(I32, (16, LANES), 1)
    zero = jnp.zeros((16, LANES), F32)

    def tile_of_targets(turn, carry):
        begin = pl.multiple_of(turn * 16, 16)
        mine = target_ref[pl.ds(begin, 16), :]
        tx, ty, tz, ux, uy, uz = [jnp.broadcast_to(mine[:, k : k + 1], (16, LANES)) for k in range(6)]

        def block(b, acc):
            ax, ay, az, jx, jy, jz = acc
            source = slab_ref[pl.ds(pl.multiple_of(b * 8, 8), 8), :]
            sx, sy, sz, vx, vy, vz, mass = [source[k : k + 1] for k in range(7)]
            rx = sx - tx
            ry = sy - ty
            rz = sz - tz
            wx = vx - ux
            wy = vy - uy
            wz = vz - uz
            square = (rx * rx + softening_square) + ry * ry + rz * rz
            dot = rx * wx + ry * wy + rz * wz
            inverse = lax.rsqrt(square)
            inverse2 = inverse * inverse
            weight = (mass * inverse) * inverse2
            radial = (3.0 * dot) * inverse2
            return (
                ax + weight * rx,
                ay + weight * ry,
                az + weight * rz,
                jx + weight * (wx - radial * rx),
                jy + weight * (wy - radial * ry),
                jz + weight * (wz - radial * rz),
            )

        def blocks(turn8, acc):
            for k in range(8):
                acc = block(turn8 * 8 + k, acc)
            return acc

        acc = lax.fori_loop(0, BLOCKS // 8, blocks, (zero,) * 6)
        result = zero
        for k in range(6):
            result = jnp.where(column == k, jnp.sum(acc[k], axis=1, keepdims=True), result)
        sum_ref[pl.ds(begin, 16), :] = result
        return carry

    lax.fori_loop(0, (size + 15) >> 4, tile_of_targets, 0)
    for half in range(2):
        out_ref[half * 8 : half * 8 + 8, :] = sum_ref[half * LANES : (half + 1) * LANES, :].T[0:8]


def finish_kernel(counts_ref, block_ref, lane_ref, force_ref, state_ref, elapsed_ref, new_ref, active_ref):
    offsets, live = list_offsets(counts_ref)
    size = group_size(live)
    halves = jnp.where(size > LANES, 2, 1)
    my_list = lax.axis_index("x") * 2 + lax.axis_index("c")
    count = counts_ref[my_list]
    start = jnp.int32(0)
    for i in range(LISTS):
        start = jnp.where(my_list == i, offsets[i], start)
    row = lax.broadcasted_iota(I32, (8, LANES), 1)

    def gather(blocks, lanes):
        blocks = [jnp.broadcast_to(b, (8, LANES)) for b in blocks]
        lanes = [jnp.broadcast_to(b, (8, LANES)) for b in lanes]

        def step(turn, acc):
            acc = list(acc)
            for k in range(8):
                b = (turn * 8 + k) * (3 - halves)
                tile = force_ref[pl.ds(pl.multiple_of(b * 8, 8), 8), :]
                for n in range(len(acc)):
                    acc[n] = jnp.where(blocks[n] == b, take(tile, lanes[n]), acc[n])
            return tuple(acc)

        zero = jnp.zeros((8, LANES), F32)
        return lax.fori_loop(0, 8 * halves, step, (zero,) * len(blocks))

    for quarter in range(4):
        blocks = [block_ref[quarter * 4 + k : quarter * 4 + k + 1, :] for k in range(4)]
        lanes = [lane_ref[quarter * 4 + k : quarter * 4 + k + 1, :] for k in range(4)]
        found = gather(blocks, lanes)
        for k in range(4):
            part = slice((quarter * 4 + k) * LANES, (quarter * 4 + k + 1) * LANES)
            old = state_ref[:, part]
            step_time = elapsed_ref[:, part]
            force = found[k]
            half = step_time * 0.5
            twelfth = step_time * step_time / 12.0
            vel = old[3:6] + (old[6:9] + force[0:3]) * half + (old[9:12] - force[3:6]) * twelfth
            pos = old[0:3] + (old[3:6] + vel) * half + (old[6:9] - force[0:3]) * twelfth
            fresh = jnp.concatenate([pos, vel, force[0:6]], axis=0)
            new_ref[:, part] = jnp.where(blocks[k] >= 0, fresh, old)

    for quarter in range(4):
        span = slice(quarter * 512, quarter * 512 + 512)
        active_ref[:, span] = jnp.zeros((6, 512), F32)

        @pl.when(quarter * 512 < count)
        def _():
            blocks, lanes = [], []
            for k in range(4):
                slot = row + (quarter * 4 + k) * LANES
                b, lane = split_position(start + slot, size)
                blocks.append(jnp.where(slot < count, b, -1))
                lanes.append(lane)
            found = gather(blocks, lanes)
            for k in range(4):
                part = slice((quarter * 4 + k) * LANES, (quarter * 4 + k + 1) * LANES)
                active_ref[:, part] = found[k][0:6]


def exchange_y(part):
    return [lax.ppermute(part, "y", [(i, (i + k) % 4) for i in range(4)]) for k in range(1, 4)]


def spread(part):
    part = lax.all_to_all(part, ("x", "z"), 0, 0)
    return lax.all_gather(part, "c").reshape(1024, LANES)


def body(state, mass, elapsed, active_ids, active_count):
    mass = mass.reshape(1, SHARD)
    elapsed = elapsed.reshape(1, SHARD)
    ids = active_ids.reshape(1, CAP)
    packed = pl.pallas_call(
        pack_kernel,
        out_shape=jax.ShapeDtypeStruct((32, 16, LANES), F32),
        in_specs=[VMEM] * 4,
        out_specs=VMEM,
        name="pack",
    )(state, mass, elapsed, ids)
    slab = spread(packed)
    own = pl.pallas_call(
        extract_kernel,
        out_shape=jax.ShapeDtypeStruct((16, LANES), F32),
        in_specs=[SMEM, VMEM],
        out_specs=VMEM,
        name="extract",
    )(active_count, slab)
    others = exchange_y(own)
    blocks, lanes = pl.pallas_call(
        inverse_kernel,
        out_shape=[jax.ShapeDtypeStruct((16, LANES), I32)] * 2,
        in_specs=[SMEM, VMEM],
        out_specs=[VMEM, VMEM],
        name="inverse",
    )(active_count, slab)
    partial = pl.pallas_call(
        pair_kernel,
        out_shape=jax.ShapeDtypeStruct((16, LANES), F32),
        in_specs=[SMEM] + [VMEM] * 5,
        out_specs=VMEM,
        scratch_shapes=[pltpu.VMEM((256, LANES), F32), pltpu.VMEM((256, LANES), F32)],
        name="pairs",
    )(active_count, own, *others, slab)
    more = exchange_y(partial)
    force = partial + more[0] + more[1] + more[2]
    forces = spread(jnp.broadcast_to(force[None], (32, 16, LANES)))
    return pl.pallas_call(
        finish_kernel,
        out_shape=[
            jax.ShapeDtypeStruct((12, SHARD), F32),
            jax.ShapeDtypeStruct((6, CAP), F32),
        ],
        in_specs=[SMEM] + [VMEM] * 5,
        out_specs=[VMEM, VMEM],
        name="finish",
    )(active_count, blocks, lanes, forces, state, elapsed)


def solution(mesh):
    fine = Mesh(mesh.devices.reshape(4, 2, 4, 8), ("x", "c", "y", "z"))
    placed = (P(None, ("y", "z")), P(("y", "z")), P(("y", "z")), P(("x", "c")), P())
    return jax.shard_map(
        body,
        mesh=fine,
        in_specs=placed,
        out_specs=(P(None, ("y", "z")), P(None, ("x", "c"))),
        check_vma=False,
    )
```

time: 394 us -> 88.7 us (0.23)
  blocking collectives: 155 us -> 33.9 us
  waiting for transfers between devices: 123 us -> 10.4 us
  local copies, waits for them, and re-layouts: 54.8 us -> 1.82 us
  other arithmetic: 45.2 us -> 0.7 us
  Pallas kernels: 0 us -> 30.9 us
  between operations: 14.9 us -> 0.65 us
  starting transfers between devices: 0.04 us -> 9.92 us
    psum x1 -> x0, waiting for transfers between devices: 123 us -> none  [body(): record = lax.psum(picked, 'ja')]
    psum x1 -> x0, blocking collectives: 113 us -> none  [body(): force = lax.psum(partial_force, 'ja')]
    scatter x1 -> x0, local copies, waits for them, and re-layouts: 41.1 us -> none  [body(): new_state = state.at[:, target].set(gathered, mode='drop')]
    reduce_sum x32 -> x0, other arithmetic: 32.1 us -> none  [the longest x16 18.9 us: pair_terms(): accel_sum = jnp.sum(weight[None] * separation, axis=2)]
    pallas_call x0 -> x5, Pallas kernels: none -> 30.9 us  [the longest x1 11.8 us: body(): pl.pallas_call(pair_kernel, out_shape=jax.ShapeDtypeStruct((16, LANES), F...]
    all_gather x2, blocking collectives: 42.2 us -> 12.3 us  [spread(): return lax.all_gather(part, 'c').reshape(1024, LANES)]
    all_to_all x0 -> x1, blocking collectives: none -> 21.6 us  [spread(): part = lax.all_to_all(part, ('x', 'z'), 0, 0)]
    ppermute x0 -> x6, waiting for transfers between devices: none -> 6.36 us  [exchange_y(): lax.ppermute(part, 'y', [(i, (i + k) % 4) for i in range(4)])]
  transfers between devices with their start and end apart: 1 -> 7, of which waited for: 1 -> 6; matrix products, arithmetic and copies ran while one was open for 0% -> 0% of each run, Pallas kernels for 0% -> 7%
where the time goes in v1:
time: 88.7 us; the launch traced here: 88.3 us
  blocking collectives  33.9 us (38%)
  Pallas kernels  30.9 us (35%)
  waiting for transfers between devices  10.4 us (12%)
  starting transfers between devices  9.92 us (11%)
  local copies, waits for them, and re-layouts  1.82 us (2%)
    all_to_all x1, blocking collectives, spread(): part = lax.all_to_all(part, ('x', 'z'), 0, 0)  21.6 us
    all_gather x2, blocking collectives, spread(): return lax.all_gather(part, 'c').reshape(1024, LANES)  12.3 us
    pallas_call x1, Pallas kernels, body(): pl.pallas_call(pair_kernel, out_shape=jax.ShapeDtypeStruct((16, LANES), F...  11.8 us
    pallas_call x1, Pallas kernels, body(): pl.pallas_call(finish_kernel, out_shape=[jax.ShapeDtypeStruct((12, SHARD)...  9.28 us
    ppermute x6, waiting for transfers between devices, exchange_y(): lax.ppermute(part, 'y', [(i, (i + k) % 4) for i in range(4)])  6.36 us
    ppermute x6, starting transfers between devices, exchange_y(): lax.ppermute(part, 'y', [(i, (i + k) % 4) for i in range(4)])  5.81 us
    pallas_call x1, Pallas kernels, body(): pl.pallas_call(inverse_kernel, out_shape=[jax.ShapeDtypeStruct((16, LANES...  5.75 us
    all_to_all x1, starting transfers between devices, spread(): part = lax.all_to_all(part, ('x', 'z'), 0, 0)  4.11 us
  transfers between devices with their start and end apart: 7, of which 6 were waited for; matrix products, arithmetic and copies ran while one was open for 0% of the time, Pallas kernels for 7%

profile of v1, /device:TPU:1, one launch (start us, length us, event | category | flops | bytes accessed | tf_op | source)
XLA Modules:
  0.0 88.3 jit_solution(17251262565660108455)
XLA Ops:
  0.6 1.7 %pack.1 = f32[32,16,128]{2,1,0:T(8,128)} custom-call(f32[12,2048]{1,0:T(8,128)} %state_ref.3, f32[1,2048]{1,0:T(1,128)} %bitcast.11, f32[1,2048]{1,0:T(1,128)} %bitcast.9, s32[1,2048]{1,0:T(1,128)} %bitcast.12), custom_call_target="tpu_custom_call" | custom-call | tf_op jit(solution)/shard_map/pack/pallas_call | solution.py:284
  2.3 21.6 %all_to_all.10 = f32[32,16,128]{2,1,0:T(8,128)S(1)} all-to-all(f32[32,16,128]{2,1,0:T(8,128)} %pack.1), channel_id=1, replica_groups=mesh['x'=4,'c'=2,'y'=4,'z'=8] {'x','z'}, dimensions={0} | all-to-all | bytes 524288 | tf_op jit(solution)/shard_map/all_to_all | solution.py:276
  23.8 5.7 %all-gather = f32[64,16,128]{2,1,0:T(8,128)} all-gather(f32[32,16,128]{2,1,0:T(8,128)S(1)} %all_to_all.10), channel_id=2, replica_groups=mesh['x'=4,'c'=2,'y'=4,'z'=8] {'c'}, dimensions={0}, use_global_device_ids=true | all-gather | bytes 786432 | tf_op jit(solution)/shard_map/all_gather | solution.py:277
  29.5 2.5 %extract.1.own_ref = f32[16,128]{1,0:T(8,128)} custom-call(s32[8]{0:T(128)} %counts_ref.7, f32[1024,128]{1,0:T(8,128)} %bitcast.5), custom_call_target="tpu_custom_call" | custom-call | tf_op jit(solution)/shard_map/extract/pallas_call | solution.py:292
  32.0 2.7 %collective-permute-start.2 = (f32[16,128]{1,0:T(8,128)}, f32[16,128]{1,0:T(8,128)S(1)}, u32[]{:S(2)}, u32[]{:S(2)}) collective-permute-start(f32[16,128]{1,0:T(8,128)} %extract.1.own_ref), channel_id=1, source_target_pairs={{0,24},{8,0},{16,8},{24,16},{1,25},{9,1},{17,9},{25,17},{2,26},{10... | collective-permute-start | bytes 24584 | tf_op jit(solution)/shard_map/ppermute | solution.py:272
  34.7 0.3 collective-permute-start.1
  35.1 0.7 collective-permute-start
  35.7 0.0 collective-permute-done.2.three_ref
  35.8 0.0 copy-start
  35.8 3.2 %collective-permute-done.1.two_ref = f32[16,128]{1,0:T(8,128)S(1)} collective-permute-done((f32[16,128]{1,0:T(8,128)}, f32[16,128]{1,0:T(8,128)S(1)}, u32[]{:S(2)}, u32[]{:S(2)}) %collective-permute-start.1) | collective-permute-done | bytes 8224 | tf_op jit(solution)/shard_map/ppermute | solution.py:272
  38.9 0.0 copy-start.1
  38.9 0.1 collective-permute-done.one_ref
  39.0 0.0 copy-done
  39.0 0.5 copy-done.1
  39.5 0.0 copy-start.2
  39.5 0.6 copy-done.2
  40.1 11.8 %pairs.1 = f32[16,128]{1,0:T(8,128)} custom-call(s32[8]{0:T(128)} %counts_ref.7, f32[16,128]{1,0:T(8,128)} %extract.1.own_ref, f32[16,128]{1,0:T(8,128)} %copy-done.2, f32[16,128]{1,0:T(8,128)} %copy-done.1, f32[16,128]{1,0:T(8,128)} %copy-done, f32[1024,128]{1,0:T(8,128)} %bitcast.6), custom_call_target="tpu_custom_call" | custom-call | tf_op jit(solution)/shard_map/pairs/pallas_call | solution.py:307
  51.9 0.5 collective-permute-start.5
  52.4 0.7 collective-permute-start.4
  53.1 0.9 collective-permute-start.3
  53.9 0.7 collective-permute-done.5
  54.6 2.0 %collective-permute-done.4 = f32[16,128]{1,0:T(8,128)S(1)} collective-permute-done((f32[16,128]{1,0:T(8,128)}, f32[16,128]{1,0:T(8,128)S(1)}, u32[]{:S(2)}, u32[]{:S(2)}) %collective-permute-start.4) | collective-permute-done | bytes 8224 | tf_op jit(solution)/shard_map/ppermute | solution.py:272
  56.6 0.5 collective-permute-done.3
  57.0 0.7 add_add_fusion
  57.7 0.7 broadcast_in_dim.2
  58.5 4.1 %all-to-all-start.1 = ((f32[32,16,128]{2,1,0:T(8,128)}), f32[32,16,128]{2,1,0:T(8,128)S(1)}, u32[]{:S(2)}, u32[]{:S(2)}) async-start(f32[32,16,128]{2,1,0:T(8,128)} %broadcast_in_dim.2), calls=%async_computation.1 | async-start | bytes 524288 | tf_op jit(solution)/shard_map/all_to_all | solution.py:276
  62.6 5.7 %inverse.1 = (s32[16,128]{1,0:T(8,128)}, s32[16,128]{1,0:T(8,128)}) custom-call(s32[8]{0:T(128)} %counts_ref.7, f32[1024,128]{1,0:T(8,128)} %bitcast.7), custom_call_target="tpu_custom_call" | custom-call | tf_op jit(solution)/shard_map/inverse/pallas_call | solution.py:300
  68.3 4.0 %all-to-all-done.1 = f32[32,16,128]{2,1,0:T(8,128)S(1)} async-done(((f32[32,16,128]{2,1,0:T(8,128)}), f32[32,16,128]{2,1,0:T(8,128)S(1)}, u32[]{:S(2)}, u32[]{:S(2)}) %all-to-all-start.1) | async-done | bytes 262176 | tf_op jit(solution)/shard_map/all_to_all | solution.py:276
  72.4 6.7 %all-gather.1 = f32[64,16,128]{2,1,0:T(8,128)} all-gather(f32[32,16,128]{2,1,0:T(8,128)S(1)} %all-to-all-done.1), channel_id=3, replica_groups=mesh['x'=4,'c'=2,'y'=4,'z'=8] {'c'}, dimensions={0}, use_global_device_ids=true | all-gather | bytes 786432 | tf_op jit(solution)/shard_map/all_gather | solution.py:277
  79.1 9.3 %finish.1 = (f32[12,2048]{1,0:T(8,128)}, f32[6,2048]{1,0:T(8,128)}) custom-call(s32[8]{0:T(128)} %counts_ref.7, s32[16,128]{1,0:T(8,128)} %get-tuple-element.4.block_ref, s32[16,128]{1,0:T(8,128)} %get-tuple-element.5.lane_ref, f32[1024,128]{1,0:T(8,128)} %bitcast.8, f32[12,2048]{1,0:T(8,128)} %state_ref.3, f32[1,2048]{1,0:T(1,128)} %bitcast.10), custom_call_target="tpu_custom_call" | custom-call | tf_op jit(solution)/shard_map/finish/pallas_call | solution.py:318
Async XLA Ops:
  32.0 3.8 %collective-permute-start.2 = (f32[16,128]{1,0:T(8,128)}, f32[16,128]{1,0:T(8,128)S(1)}, u32[]{:S(2)}, u32[]{:S(2)}) collective-permute-start(f32[16,128]{1,0:T(8,128)} %extract.1.own_ref), channel_id=1, source_target_pairs={{0,24},{8,0},{16,8},{24,16},{1,25},{9,1},{17,9},{25,17},{2,26},{10... | collective-permute-start | bytes 24584 | tf_op jit(solution)/shard_map/ppermute | solution.py:272
  34.7 4.2 %collective-permute-start.1 = (f32[16,128]{1,0:T(8,128)}, f32[16,128]{1,0:T(8,128)S(1)}, u32[]{:S(2)}, u32[]{:S(2)}) collective-permute-start(f32[16,128]{1,0:T(8,128)} %extract.1.own_ref), channel_id=1, source_target_pairs={{0,16},{8,24},{16,0},{24,8},{1,17},{9,25},{17,1},{25,9},{2,18},{10... | collective-permute-start | bytes 24584 | tf_op jit(solution)/shard_map/ppermute | solution.py:272
  35.1 4.0 %collective-permute-start = (f32[16,128]{1,0:T(8,128)}, f32[16,128]{1,0:T(8,128)S(1)}, u32[]{:S(2)}, u32[]{:S(2)}) collective-permute-start(f32[16,128]{1,0:T(8,128)} %extract.1.own_ref), channel_id=1, source_target_pairs={{0,8},{8,16},{16,24},{24,0},{1,9},{9,17},{17,25},{25,1},{2,10},{10... | collective-permute-start | bytes 24584 | tf_op jit(solution)/shard_map/ppermute | solution.py:272
  35.8 3.3 %copy-start = (f32[16,128]{1,0:T(8,128)}, f32[16,128]{1,0:T(8,128)S(1)}, u32[]{:S(2)}) copy-start(f32[16,128]{1,0:T(8,128)S(1)} %collective-permute-done.2.three_ref) | copy-start | bytes 24580
  38.9 0.6 copy-start.1
  39.5 0.6 copy-start.2
  51.9 2.7 %collective-permute-start.5 = (f32[16,128]{1,0:T(8,128)}, f32[16,128]{1,0:T(8,128)S(1)}, u32[]{:S(2)}, u32[]{:S(2)}) collective-permute-start(f32[16,128]{1,0:T(8,128)} %pairs.1), channel_id=1, source_target_pairs={{0,24},{8,0},{16,8},{24,16},{1,25},{9,1},{17,9},{25,17},{2,26},{10... | collective-permute-start | bytes 24584 | tf_op jit(solution)/shard_map/ppermute | solution.py:272
  52.4 4.2 %collective-permute-start.4 = (f32[16,128]{1,0:T(8,128)}, f32[16,128]{1,0:T(8,128)S(1)}, u32[]{:S(2)}, u32[]{:S(2)}) collective-permute-start(f32[16,128]{1,0:T(8,128)} %pairs.1), channel_id=1, source_target_pairs={{0,16},{8,24},{16,0},{24,8},{1,17},{9,25},{17,1},{25,9},{2,18},{10... | collective-permute-start | bytes 24584 | tf_op jit(solution)/shard_map/ppermute | solution.py:272
  53.1 4.0 %collective-permute-start.3 = (f32[16,128]{1,0:T(8,128)}, f32[16,128]{1,0:T(8,128)S(1)}, u32[]{:S(2)}, u32[]{:S(2)}) collective-permute-start(f32[16,128]{1,0:T(8,128)} %pairs.1), channel_id=1, source_target_pairs={{0,8},{8,16},{16,24},{24,0},{1,9},{9,17},{17,25},{25,1},{2,10},{10... | collective-permute-start | bytes 24584 | tf_op jit(solution)/shard_map/ppermute | solution.py:272
  58.5 13.9 %all-to-all-start.1 = ((f32[32,16,128]{2,1,0:T(8,128)}), f32[32,16,128]{2,1,0:T(8,128)S(1)}, u32[]{:S(2)}, u32[]{:S(2)}) async-start(f32[32,16,128]{2,1,0:T(8,128)} %broadcast_in_dim.2), calls=%async_computation.1 | async-start | bytes 524288 | tf_op jit(solution)/shard_map/all_to_all | solution.py:276

commit v2 on v1

--- a/solution.py
+++ b/solution.py
@@ -88,14 +88,9 @@
         place = jnp.where(mine, place, -1)
         inside = star & 127
 
-        def step(turn, acc):
-            for k in range(16):
-                b = turn * 16 + k
-                tile = slab_ref[pl.ds(pl.multiple_of(b * 8, 8), 8), :]
-                acc = jnp.where(place == b, take(tile, inside), acc)
-            return acc
-
-        picked = lax.fori_loop(0, BLOCKS // 16, step, jnp.zeros((8, LANES), F32))
+        picked = jnp.zeros((8, LANES), F32)
+        for b in range(BLOCKS):
+            picked = jnp.where(place == b, take(slab_ref[b * 8 : b * 8 + 8, :], inside), picked)
         out_ref[half * 8 : half * 8 + 8, :] = jnp.where(sub < 6, picked, 0.0)
 
     one_half(0)
@@ -106,7 +101,10 @@
         one_half(1)
 
 
-def inverse_kernel(counts_ref, slab_ref, block_ref, lane_ref):
+def plan_kernel(
+    counts_ref, slab_ref, state_ref, elapsed_ref,
+    number_ref, rank_ref, block_ref, lane_ref, known_ref, one_ref, two_ref,
+):
     offsets, live = list_offsets(counts_ref)
     size = group_size(live)
     shard = lax.axis_index("y") * 8 + lax.axis_index("z")
@@ -114,38 +112,92 @@
     row16 = lax.broadcasted_iota(I32, (16, wide), 0)
     row128 = lax.broadcasted_iota(I32, (LANES, wide), 0)
     column = lax.broadcasted_iota(I32, (1, wide), 1)
+    square_row = lax.broadcasted_iota(I32, (LANES, LANES), 0)
+    square_column = lax.broadcasted_iota(I32, (LANES, LANES), 1)
+    contract = (((1,), (1,)), ((), ()))
     total = jnp.zeros((32, LANES), F32)
     for i in range(LISTS):
-        first = ((i & 1) * 32 + (i >> 1) * 8) * 16
+        first = 7 + 64 * ((i & 1) * 8 + (i >> 1) * 2)
 
         def step(turn, acc):
-            row = first + turn * 16
-            ids = jnp.concatenate(
-                [slab_ref[pl.ds(row + 7, 1), :], slab_ref[pl.ds(row + 15, 1), :]], axis=1
-            ).astype(I32)
-            slot = turn * wide + column
-            mine = (slot < counts_ref[i]) & ((ids >> 11) == shard)
-            high = jnp.where(mine, (ids >> 7) & 15, -1)
-            low = ids & 127
-            mark = offsets[i] + slot + 1
-            here = row16 == high
-            left = jnp.concatenate(
-                [
-                    jnp.where(here, (mark >> 7).astype(F32), 0.0),
-                    jnp.where(here, (mark & 127).astype(F32), 0.0),
-                ],
-                axis=0,
-            ).astype(jnp.bfloat16)
-            right = jnp.where(row128 == low, 1.0, 0.0).astype(jnp.bfloat16)
-            return acc + lax.dot_general(
-                left, right, (((1,), (1,)), ((), ())), preferred_element_type=F32
+            ids8 = slab_ref[pl.ds(first + 64 * turn, 8, stride=8), :].astype(I32)
+            for k in range(0, 8, 2):
+                ids = jnp.concatenate([ids8[k : k + 1], ids8[k + 1 : k + 2]], axis=1)
+                slot = turn * 1024 + k * LANES + column
+                mine = (slot < counts_ref[i]) & ((ids >> 11) == shard)
+                high = jnp.where(mine, (ids >> 7) & 15, -1)
+                low = ids & 127
+                mark = offsets[i] + slot + 1
+                here = row16 == high
+                left = jnp.concatenate(
+                    [
+                        jnp.where(here, (mark >> 7).astype(F32), 0.0),
+                        jnp.where(here, (mark & 127).astype(F32), 0.0),
+                    ],
+                    axis=0,
+                ).astype(jnp.bfloat16)
+                right = jnp.where(row128 == low, 1.0, 0.0).astype(jnp.bfloat16)
+                acc = acc + lax.dot_general(left, right, contract, preferred_element_type=F32)
+            return acc
+
+        total = lax.fori_loop(0, (counts_ref[i] + 1023) >> 10, step, total)
+    mark = (total[0:16] * 128.0 + total[16:32]).astype(I32)
+    active = mark > 0
+    flags = jnp.where(active, 1.0, 0.0).astype(jnp.bfloat16)
+    upto = jnp.where(square_row <= square_column, 1.0, 0.0).astype(jnp.bfloat16)
+    within = jnp.dot(flags, upto, preferred_element_type=F32)
+    rows = jnp.broadcast_to(within[:, LANES - 1 :], (16, LANES)).astype(jnp.bfloat16)
+    below = jnp.where(square_column[0:16, 0:16] < square_row[0:16, 0:16], 1.0, 0.0).astype(jnp.bfloat16)
+    before = jnp.dot(below, rows, preferred_element_type=F32)
+    rank = jnp.where(active, (within + before).astype(I32) - 1, -1)
+    rank_ref[...] = rank
+    number = jnp.sum(jnp.where(active, 1, 0))
+    number_ref[0] = number
+    row8 = lax.broadcasted_iota(I32, (8, LANES), 0)
+    column8 = lax.broadcasted_iota(I32, (8, LANES), 1)
+
+    def compact(turn, carry):
+        sums = jnp.zeros((8, LANES), F32)
+        for r in range(16):
+            hit = jnp.where(rank[r : r + 1] - turn * LANES == square_row, 1.0, 0.0).astype(jnp.bfloat16)
+            mine = mark[r : r + 1]
+            facts = jnp.where(row8 == 0, mine >> 7, jnp.where(row8 == 1, mine & 127, jnp.where(row8 == 2, r, column8)))
+            sums = sums + lax.dot_general(
+                facts.astype(F32).astype(jnp.bfloat16), hit, contract, preferred_element_type=F32
             )
-
-        total = lax.fori_loop(0, (counts_ref[i] + (wide - 1)) >> 8, step, total)
-    position = (total[0:16] * 128.0 + total[16:32]).astype(I32) - 1
-    block, lane = split_position(position, size)
-    block_ref[...] = jnp.where(position >= 0, block, -1)
-    lane_ref[...] = jnp.where(position >= 0, lane, 0)
+        mark_of = (sums[0:1] * 128.0 + sums[1:2]).astype(I32)
+        block, lane = split_position(mark_of - 1, size)
+        block_ref[pl.ds(turn, 1), :] = jnp.where(mark_of > 0, block, -1)
+        lane_ref[pl.ds(turn, 1), :] = jnp.where(mark_of > 0, lane, 0)
+        star_row = jnp.broadcast_to(sums[2:3], (8, LANES)).astype(I32)
+        star_lane = jnp.broadcast_to(sums[3:4], (8, LANES)).astype(I32)
+        head = jnp.zeros((8, LANES), F32)
+        tail = jnp.zeros((8, LANES), F32)
+        for r in range(16):
+            part = slice(r * LANES, (r + 1) * LANES)
+            here = star_row == r
+            head = jnp.where(here, take(state_ref[0:8, part], star_lane), head)
+            rest = jnp.concatenate(
+                [state_ref[8:12, part], jnp.broadcast_to(elapsed_ref[:, part], (4, LANES))], axis=0
+            )
+            tail = jnp.where(here, take(rest, star_lane), tail)
+        pos, vel = head[0:3], head[3:6]
+        accel = jnp.concatenate([head[6:8], tail[0:1]], axis=0)
+        jerk = tail[1:4]
+        step_time = tail[4:5]
+        half = step_time * 0.5
+        twelfth = step_time * step_time / 12.0
+        known_vel = vel + accel * half + jerk * twelfth
+        known_pos = pos + (vel + known_vel) * half + accel * twelfth
+        none = jnp.zeros((2, LANES), F32)
+        wide3 = lambda value: jnp.broadcast_to(value, (3, LANES))
+        begin = pl.ds(pl.multiple_of(turn * 8, 8), 8)
+        known_ref[begin, :] = jnp.concatenate([known_pos, known_vel, none], axis=0)
+        one_ref[begin, :] = jnp.concatenate([wide3(half * half - twelfth), wide3(half), none], axis=0)
+        two_ref[begin, :] = jnp.concatenate([wide3(twelfth * half), wide3(twelfth), none], axis=0)
+        return carry
+
+    lax.fori_loop(0, (number + 127) >> 7, compact, 0)
 
 
 def pair_kernel(counts_ref, own_ref, one_ref, two_ref, three_ref, slab_ref, out_ref, target_ref, sum_ref):
@@ -207,65 +259,72 @@
         out_ref[half * 8 : half * 8 + 8, :] = sum_ref[half * LANES : (half + 1) * LANES, :].T[0:8]
 
 
-def finish_kernel(counts_ref, block_ref, lane_ref, force_ref, state_ref, elapsed_ref, new_ref, active_ref):
+def finish_kernel(
+    counts_ref, number_ref, rank_ref, block_ref, lane_ref, known_ref, one_ref, two_ref,
+    force_ref, state_ref, new_ref, active_ref,
+):
     offsets, live = list_offsets(counts_ref)
     size = group_size(live)
-    halves = jnp.where(size > LANES, 2, 1)
+    full = jnp.where(size > LANES, 1, 0)
     my_list = lax.axis_index("x") * 2 + lax.axis_index("c")
     count = counts_ref[my_list]
     start = jnp.int32(0)
     for i in range(LISTS):
         start = jnp.where(my_list == i, offsets[i], start)
+    zero = jnp.zeros((8, LANES), F32)
     row = lax.broadcasted_iota(I32, (8, LANES), 1)
 
-    def gather(blocks, lanes):
-        blocks = [jnp.broadcast_to(b, (8, LANES)) for b in blocks]
-        lanes = [jnp.broadcast_to(b, (8, LANES)) for b in lanes]
-
-        def step(turn, acc):
-            acc = list(acc)
-            for k in range(8):
-                b = (turn * 8 + k) * (3 - halves)
-                tile = force_ref[pl.ds(pl.multiple_of(b * 8, 8), 8), :]
-                for n in range(len(acc)):
-                    acc[n] = jnp.where(blocks[n] == b, take(tile, lanes[n]), acc[n])
-            return tuple(acc)
-
-        zero = jnp.zeros((8, LANES), F32)
-        return lax.fori_loop(0, 8 * halves, step, (zero,) * len(blocks))
-
-    for quarter in range(4):
-        blocks = [block_ref[quarter * 4 + k : quarter * 4 + k + 1, :] for k in range(4)]
-        lanes = [lane_ref[quarter * 4 + k : quarter * 4 + k + 1, :] for k in range(4)]
-        found = gather(blocks, lanes)
-        for k in range(4):
-            part = slice((quarter * 4 + k) * LANES, (quarter * 4 + k + 1) * LANES)
-            old = state_ref[:, part]
-            step_time = elapsed_ref[:, part]
-            force = found[k]
-            half = step_time * 0.5
-            twelfth = step_time * step_time / 12.0
-            vel = old[3:6] + (old[6:9] + force[0:3]) * half + (old[9:12] - force[3:6]) * twelfth
-            pos = old[0:3] + (old[3:6] + vel) * half + (old[6:9] - force[0:3]) * twelfth
-            fresh = jnp.concatenate([pos, vel, force[0:6]], axis=0)
-            new_ref[:, part] = jnp.where(blocks[k] >= 0, fresh, old)
-
-    for quarter in range(4):
-        span = slice(quarter * 512, quarter * 512 + 512)
-        active_ref[:, span] = jnp.zeros((6, 512), F32)
-
-        @pl.when(quarter * 512 < count)
-        def _():
-            blocks, lanes = [], []
-            for k in range(4):
-                slot = row + (quarter * 4 + k) * LANES
-                b, lane = split_position(start + slot, size)
-                blocks.append(jnp.where(slot < count, b, -1))
-                lanes.append(lane)
-            found = gather(blocks, lanes)
-            for k in range(4):
-                part = slice((quarter * 4 + k) * LANES, (quarter * 4 + k + 1) * LANES)
-                active_ref[:, part] = found[k][0:6]
+    blocks, lanes, firsts = [], [], []
+    for b in range(CAP // LANES):
+        slot = row + b * LANES
+        block, lane = split_position(start + slot, size)
+        blocks.append(jnp.where(slot < count, block, -1))
+        lanes.append(lane)
+        firsts.append(lax.div(start + b * LANES, size))
+
+    def span(turn, acc):
+        acc = list(acc)
+        for b in range(CAP // LANES):
+            tile = jnp.minimum(firsts[b] + (turn >> full), GROUPS - 1) * 2 + (turn & full)
+            got = take(force_ref[pl.ds(pl.multiple_of(tile * 8, 8), 8), :], lanes[b])
+            acc[b] = jnp.where(blocks[b] == tile, got, acc[b])
+        return tuple(acc)
+
+    spans = lax.div(jnp.int32(LANES - 1), size) + 2
+    found = lax.fori_loop(0, spans << full, span, (zero,) * (CAP // LANES))
+    for b in range(CAP // LANES):
+        active_ref[:, b * LANES : (b + 1) * LANES] = found[b][0:6]
+
+    new_ref[...] = state_ref[...]
+    none = jnp.zeros((2, LANES), F32)
+
+    def compact(turn, carry):
+        block = jnp.broadcast_to(block_ref[pl.ds(turn, 1), :], (8, LANES))
+        lane = jnp.broadcast_to(lane_ref[pl.ds(turn, 1), :], (8, LANES))
+
+        def half(h, force):
+            for g in range(GROUPS):
+                tile = force_ref[pl.ds(pl.multiple_of(g * 16 + h * 8, 8), 8), :]
+                force = jnp.where(block == g * 2 + h, take(tile, lane), force)
+            return force
+
+        force = lax.fori_loop(0, 1 + full, half, zero)
+        begin = pl.ds(pl.multiple_of(turn * 8, 8), 8)
+        accel = jnp.concatenate([force[0:3], force[0:3], none], axis=0)
+        jerk = jnp.concatenate([force[3:6], force[3:6], none], axis=0)
+        moved = known_ref[begin, :] + accel * one_ref[begin, :] - jerk * two_ref[begin, :]
+        head = jnp.concatenate([moved[0:6], force[0:2]], axis=0)
+        tail = jnp.concatenate([force[2:6], none, none], axis=0)
+        for r in range(16):
+            part = slice(r * LANES, (r + 1) * LANES)
+            rank = jnp.broadcast_to(rank_ref[r : r + 1, :], (8, LANES))
+            here = (rank >> 7) == turn
+            place = rank & 127
+            new_ref[0:8, part] = jnp.where(here, take(head, place), new_ref[0:8, part])
+            new_ref[8:12, part] = jnp.where(here[0:4], take(tail, place)[0:4], new_ref[8:12, part])
+        return carry
+
+    lax.fori_loop(0, (number_ref[0] + 127) >> 7, compact, 0)
 
 
 def exchange_y(part):
@@ -297,13 +356,16 @@
         name="extract",
     )(active_count, slab)
     others = exchange_y(own)
-    blocks, lanes = pl.pallas_call(
-        inverse_kernel,
-        out_shape=[jax.ShapeDtypeStruct((16, LANES), I32)] * 2,
-        in_specs=[SMEM, VMEM],
-        out_specs=[VMEM, VMEM],
-        name="inverse",
-    )(active_count, slab)
+    square = jax.ShapeDtypeStruct((LANES, LANES), F32)
+    plan = pl.pallas_call(
+        plan_kernel,
+        out_shape=[jax.ShapeDtypeStruct((1,), I32)]
+        + [jax.ShapeDtypeStruct((16, LANES), I32)] * 3
+        + [square] * 3,
+        in_specs=[SMEM] + [VMEM] * 3,
+        out_specs=[SMEM] + [VMEM] * 6,
+        name="plan",
+    )(active_count, slab, state, elapsed)
     partial = pl.pallas_call(
         pair_kernel,
         out_shape=jax.ShapeDtypeStruct((16, LANES), F32),
@@ -321,10 +383,10 @@
             jax.ShapeDtypeStruct((12, SHARD), F32),
             jax.ShapeDtypeStruct((6, CAP), F32),
         ],
-        in_specs=[SMEM] + [VMEM] * 5,
+        in_specs=[SMEM] * 2 + [VMEM] * 8,
         out_specs=[VMEM, VMEM],
         name="finish",
-    )(active_count, blocks, lanes, forces, state, elapsed)
+    )(active_count, *plan, forces, state)
 
 
 def solution(mesh):

time: 88.7 us -> 84.1 us (0.948)
  Pallas kernels: 30.9 us -> 25.6 us
    pallas_call x1, Pallas kernels: 9.28 us -> 3.52 us  [body(): pl.pallas_call(finish_kernel, out_shape=[jax.ShapeDtypeStruct((12, SHARD)...]
    pallas_call x1, Pallas kernels: 11.8 us -> 13.4 us  [body(): pl.pallas_call(pair_kernel, out_shape=jax.ShapeDtypeStruct((16, LANES), F...]
  transfers between devices with their start and end apart: 7 -> 7, of which waited for: 6 -> 6; matrix products, arithmetic and copies ran while one was open for 0% -> 0% of each run, Pallas kernels for 7% -> 6%
where the time goes in v2:
time: 84.1 us; the launch traced here: 83.7 us
  blocking collectives  33.9 us (40%)
  Pallas kernels  25.6 us (30%)
  waiting for transfers between devices  11.1 us (13%)
  starting transfers between devices  9.92 us (12%)
  local copies, waits for them, and re-layouts  1.82 us (2%)
    all_to_all x1, blocking collectives, spread(): part = lax.all_to_all(part, ('x', 'z'), 0, 0)  21.6 us
    pallas_call x1, Pallas kernels, body(): pl.pallas_call(pair_kernel, out_shape=jax.ShapeDtypeStruct((16, LANES), F...  13.4 us
    all_gather x2, blocking collectives, spread(): return lax.all_gather(part, 'c').reshape(1024, LANES)  12.3 us
    ppermute x6, waiting for transfers between devices, exchange_y(): lax.ppermute(part, 'y', [(i, (i + k) % 4) for i in range(4)])  6.36 us
    ppermute x6, starting transfers between devices, exchange_y(): lax.ppermute(part, 'y', [(i, (i + k) % 4) for i in range(4)])  5.81 us
    pallas_call x1, Pallas kernels, body(): pl.pallas_call(plan_kernel, out_shape=[jax.ShapeDtypeStruct((1,), I32)] +...  5.05 us
    all_to_all x1, waiting for transfers between devices, spread(): part = lax.all_to_all(part, ('x', 'z'), 0, 0)  4.73 us
    all_to_all x1, starting transfers between devices, spread(): part = lax.all_to_all(part, ('x', 'z'), 0, 0)  4.11 us
  transfers between devices with their start and end apart: 7, of which 6 were waited for; matrix products, arithmetic and copies ran while one was open for 0% of the time, Pallas kernels for 6%

profile of v2, /device:TPU:1, one launch (start us, length us, event | category | flops | bytes accessed | tf_op | source)
XLA Modules:
  0.0 83.7 jit_solution(4112647329862467196)
XLA Ops:
  0.6 1.7 %pack.1 = f32[32,16,128]{2,1,0:T(8,128)} custom-call(f32[12,2048]{1,0:T(8,128)} %state_ref.5, f32[1,2048]{1,0:T(1,128)} %bitcast.11, f32[1,2048]{1,0:T(1,128)} %bitcast.9, s32[1,2048]{1,0:T(1,128)} %bitcast.12), custom_call_target="tpu_custom_call" | custom-call | tf_op jit(solution)/shard_map/pack/pallas_call | solution.py:343
  2.3 21.6 %all_to_all.10 = f32[32,16,128]{2,1,0:T(8,128)S(1)} all-to-all(f32[32,16,128]{2,1,0:T(8,128)} %pack.1), channel_id=1, replica_groups=mesh['x'=4,'c'=2,'y'=4,'z'=8] {'x','z'}, dimensions={0} | all-to-all | bytes 524288 | tf_op jit(solution)/shard_map/all_to_all | solution.py:335
  23.8 5.7 %all-gather = f32[64,16,128]{2,1,0:T(8,128)} all-gather(f32[32,16,128]{2,1,0:T(8,128)S(1)} %all_to_all.10), channel_id=2, replica_groups=mesh['x'=4,'c'=2,'y'=4,'z'=8] {'c'}, dimensions={0}, use_global_device_ids=true | all-gather | bytes 786432 | tf_op jit(solution)/shard_map/all_gather | solution.py:336
  29.5 2.0 %extract.1.own_ref = f32[16,128]{1,0:T(8,128)} custom-call(s32[8]{0:T(128)} %counts_ref.7, f32[1024,128]{1,0:T(8,128)} %bitcast.5), custom_call_target="tpu_custom_call" | custom-call | tf_op jit(solution)/shard_map/extract/pallas_call | solution.py:351
  31.5 2.7 %collective-permute-start.2 = (f32[16,128]{1,0:T(8,128)}, f32[16,128]{1,0:T(8,128)S(1)}, u32[]{:S(2)}, u32[]{:S(2)}) collective-permute-start(f32[16,128]{1,0:T(8,128)} %extract.1.own_ref), channel_id=1, source_target_pairs={{0,24},{8,0},{16,8},{24,16},{1,25},{9,1},{17,9},{25,17},{2,26},{10... | collective-permute-start | bytes 24584 | tf_op jit(solution)/shard_map/ppermute | solution.py:331
  34.2 0.3 collective-permute-start.1
  34.6 0.7 collective-permute-start
  35.2 0.0 collective-permute-done.2.three_ref
  35.3 0.0 copy-start
  35.3 3.2 %collective-permute-done.1.two_ref = f32[16,128]{1,0:T(8,128)S(1)} collective-permute-done((f32[16,128]{1,0:T(8,128)}, f32[16,128]{1,0:T(8,128)S(1)}, u32[]{:S(2)}, u32[]{:S(2)}) %collective-permute-start.1) | collective-permute-done | bytes 8224 | tf_op jit(solution)/shard_map/ppermute | solution.py:331
  38.4 0.0 copy-start.1
  38.4 0.1 collective-permute-done.one_ref
  38.5 0.0 copy-done
  38.5 0.5 copy-done.1
  39.0 0.0 copy-start.2
  39.0 0.6 copy-done.2
  39.6 13.4 %pairs.1 = f32[16,128]{1,0:T(8,128)} custom-call(s32[8]{0:T(128)} %counts_ref.7, f32[16,128]{1,0:T(8,128)} %extract.1.own_ref, f32[16,128]{1,0:T(8,128)} %copy-done.2, f32[16,128]{1,0:T(8,128)} %copy-done.1, f32[16,128]{1,0:T(8,128)} %copy-done, f32[1024,128]{1,0:T(8,128)} %bitcast.6), custom_call_target="tpu_custom_call" | custom-call | tf_op jit(solution)/shard_map/pairs/pallas_call | solution.py:369
  53.0 0.5 collective-permute-start.5
  53.5 0.7 collective-permute-start.4
  54.2 0.9 %collective-permute-start.3 = (f32[16,128]{1,0:T(8,128)}, f32[16,128]{1,0:T(8,128)S(1)}, u32[]{:S(2)}, u32[]{:S(2)}) collective-permute-start(f32[16,128]{1,0:T(8,128)} %pairs.1), channel_id=1, source_target_pairs={{0,8},{8,16},{16,24},{24,0},{1,9},{9,17},{17,25},{25,1},{2,10},{10... | collective-permute-start | bytes 24584 | tf_op jit(solution)/shard_map/ppermute | solution.py:331
  55.1 0.7 collective-permute-done.5
  55.8 2.0 %collective-permute-done.4 = f32[16,128]{1,0:T(8,128)S(1)} collective-permute-done((f32[16,128]{1,0:T(8,128)}, f32[16,128]{1,0:T(8,128)S(1)}, u32[]{:S(2)}, u32[]{:S(2)}) %collective-permute-start.4) | collective-permute-done | bytes 8224 | tf_op jit(solution)/shard_map/ppermute | solution.py:331
  57.7 0.5 collective-permute-done.3
  58.2 0.7 add_add_fusion
  58.9 0.7 broadcast_in_dim.2
  59.6 4.1 %all-to-all-start.1 = ((f32[32,16,128]{2,1,0:T(8,128)}), f32[32,16,128]{2,1,0:T(8,128)S(1)}, u32[]{:S(2)}, u32[]{:S(2)}) async-start(f32[32,16,128]{2,1,0:T(8,128)} %broadcast_in_dim.2), calls=%async_computation.1 | async-start | bytes 524288 | tf_op jit(solution)/shard_map/all_to_all | solution.py:335
  63.7 5.1 %plan.1 = (s32[1]{0:T(128)}, s32[16,128]{1,0:T(8,128)}, s32[16,128]{1,0:T(8,128)}, s32[16,128]{1,0:T(8,128)}, f32[128,128]{1,0:T(8,128)}, /*index=5*/f32[128,128]{1,0:T(8,128)}, f32[128,128]{1,0:T(8,128)}) custom-call(s32[8]{0:T(128)} %counts_ref.7, f32[1024,128]{1,0:T(8,128)} %bitcast.7, f32[12,2048]{1,0:T(8,128)} %state_ref.5, f32[1,2048]{1,0:T(1,128)} %bitcast.10), custom_call_target="tpu_custom_call" | custom-call | tf_op jit(solution)/shard_map/plan/pallas_call | solution.py:360
  68.8 4.7 %all-to-all-done.1 = f32[32,16,128]{2,1,0:T(8,128)S(1)} async-done(((f32[32,16,128]{2,1,0:T(8,128)}), f32[32,16,128]{2,1,0:T(8,128)S(1)}, u32[]{:S(2)}, u32[]{:S(2)}) %all-to-all-start.1) | async-done | bytes 262176 | tf_op jit(solution)/shard_map/all_to_all | solution.py:335
  73.5 6.7 %all-gather.1 = f32[64,16,128]{2,1,0:T(8,128)} all-gather(f32[32,16,128]{2,1,0:T(8,128)S(1)} %all-to-all-done.1), channel_id=3, replica_groups=mesh['x'=4,'c'=2,'y'=4,'z'=8] {'c'}, dimensions={0}, use_global_device_ids=true | all-gather | bytes 786432 | tf_op jit(solution)/shard_map/all_gather | solution.py:336
  80.2 3.5 %finish.1 = (f32[12,2048]{1,0:T(8,128)}, f32[6,2048]{1,0:T(8,128)}) custom-call(s32[8]{0:T(128)} %counts_ref.7, s32[1]{0:T(128)} %get-tuple-element.9.number_ref, s32[16,128]{1,0:T(8,128)} %get-tuple-element.10.rank_ref, s32[16,128]{1,0:T(8,128)} %get-tuple-element.11.block_ref, s32[16,128]{1,0:T(8,128)} %get-tuple-element.12.lane_ref, ...), custom_call_target="tpu_custom_call" | custom-call | tf_op jit(solution)/shard_map/finish/pallas_call | solution.py:380
Async XLA Ops:
  31.5 3.8 %collective-permute-start.2 = (f32[16,128]{1,0:T(8,128)}, f32[16,128]{1,0:T(8,128)S(1)}, u32[]{:S(2)}, u32[]{:S(2)}) collective-permute-start(f32[16,128]{1,0:T(8,128)} %extract.1.own_ref), channel_id=1, source_target_pairs={{0,24},{8,0},{16,8},{24,16},{1,25},{9,1},{17,9},{25,17},{2,26},{10... | collective-permute-start | bytes 24584 | tf_op jit(solution)/shard_map/ppermute | solution.py:331
  34.2 4.2 %collective-permute-start.1 = (f32[16,128]{1,0:T(8,128)}, f32[16,128]{1,0:T(8,128)S(1)}, u32[]{:S(2)}, u32[]{:S(2)}) collective-permute-start(f32[16,128]{1,0:T(8,128)} %extract.1.own_ref), channel_id=1, source_target_pairs={{0,16},{8,24},{16,0},{24,8},{1,17},{9,25},{17,1},{25,9},{2,18},{10... | collective-permute-start | bytes 24584 | tf_op jit(solution)/shard_map/ppermute | solution.py:331
  34.6 4.0 %collective-permute-start = (f32[16,128]{1,0:T(8,128)}, f32[16,128]{1,0:T(8,128)S(1)}, u32[]{:S(2)}, u32[]{:S(2)}) collective-permute-start(f32[16,128]{1,0:T(8,128)} %extract.1.own_ref), channel_id=1, source_target_pairs={{0,8},{8,16},{16,24},{24,0},{1,9},{9,17},{17,25},{25,1},{2,10},{10... | collective-permute-start | bytes 24584 | tf_op jit(solution)/shard_map/ppermute | solution.py:331
  35.3 3.3 %copy-start = (f32[16,128]{1,0:T(8,128)}, f32[16,128]{1,0:T(8,128)S(1)}, u32[]{:S(2)}) copy-start(f32[16,128]{1,0:T(8,128)S(1)} %collective-permute-done.2.three_ref) | copy-start | bytes 24580
  38.4 0.6 copy-start.1
  39.0 0.6 copy-start.2
  53.0 2.7 %collective-permute-start.5 = (f32[16,128]{1,0:T(8,128)}, f32[16,128]{1,0:T(8,128)S(1)}, u32[]{:S(2)}, u32[]{:S(2)}) collective-permute-start(f32[16,128]{1,0:T(8,128)} %pairs.1), channel_id=1, source_target_pairs={{0,24},{8,0},{16,8},{24,16},{1,25},{9,1},{17,9},{25,17},{2,26},{10... | collective-permute-start | bytes 24584 | tf_op jit(solution)/shard_map/ppermute | solution.py:331
  53.5 4.2 %collective-permute-start.4 = (f32[16,128]{1,0:T(8,128)}, f32[16,128]{1,0:T(8,128)S(1)}, u32[]{:S(2)}, u32[]{:S(2)}) collective-permute-start(f32[16,128]{1,0:T(8,128)} %pairs.1), channel_id=1, source_target_pairs={{0,16},{8,24},{16,0},{24,8},{1,17},{9,25},{17,1},{25,9},{2,18},{10... | collective-permute-start | bytes 24584 | tf_op jit(solution)/shard_map/ppermute | solution.py:331
  54.2 4.0 %collective-permute-start.3 = (f32[16,128]{1,0:T(8,128)}, f32[16,128]{1,0:T(8,128)S(1)}, u32[]{:S(2)}, u32[]{:S(2)}) collective-permute-start(f32[16,128]{1,0:T(8,128)} %pairs.1), channel_id=1, source_target_pairs={{0,8},{8,16},{16,24},{24,0},{1,9},{9,17},{17,25},{25,1},{2,10},{10... | collective-permute-start | bytes 24584 | tf_op jit(solution)/shard_map/ppermute | solution.py:331
  59.6 13.9 %all-to-all-start.1 = ((f32[32,16,128]{2,1,0:T(8,128)}), f32[32,16,128]{2,1,0:T(8,128)S(1)}, u32[]{:S(2)}, u32[]{:S(2)}) async-start(f32[32,16,128]{2,1,0:T(8,128)} %broadcast_in_dim.2), calls=%async_computation.1 | async-start | bytes 524288 | tf_op jit(solution)/shard_map/all_to_all | solution.py:335

commit v3 on v2

--- a/solution.py
+++ b/solution.py
@@ -13,6 +13,7 @@
 SHARD = 2048
 GROUPS = 64
 LANES = 128
+SETS = 16
 BLOCKS = 128
 SMEM = pl.BlockSpec(memory_space=pltpu.SMEM)
 VMEM = pl.BlockSpec(memory_space=pltpu.VMEM)
@@ -200,63 +201,93 @@
     lax.fori_loop(0, (number + 127) >> 7, compact, 0)
 
 
-def pair_kernel(counts_ref, own_ref, one_ref, two_ref, three_ref, slab_ref, out_ref, target_ref, sum_ref):
+def pair_kernel(
+    counts_ref, own_ref, one_ref, two_ref, three_ref, slab_ref, out_ref,
+    splat_ref, source_ref, part_ref,
+):
     _, live = list_offsets(counts_ref)
     size = group_size(live)
+    column = lax.broadcasted_iota(I32, (8, LANES), 1)
+    zero = jnp.zeros((8, LANES), F32)
     targets = own_ref[...] + one_ref[...] + two_ref[...] + three_ref[...]
-    pad = jnp.zeros((LANES - 8, LANES), F32)
-    for half in range(2):
-        rows = jnp.concatenate([targets[half * 8 : half * 8 + 8], pad], axis=0)
-        target_ref[half * LANES : (half + 1) * LANES, :] = rows.T
-    sum_ref[...] = jnp.zeros_like(sum_ref)
-    column = lax.broadcasted_iota(I32, (16, LANES), 1)
-    zero = jnp.zeros((16, LANES), F32)
-
-    def tile_of_targets(turn, carry):
-        begin = pl.multiple_of(turn * 16, 16)
-        mine = target_ref[pl.ds(begin, 16), :]
-        tx, ty, tz, ux, uy, uz = [jnp.broadcast_to(mine[:, k : k + 1], (16, LANES)) for k in range(6)]
-
-        def block(b, acc):
-            ax, ay, az, jx, jy, jz = acc
-            source = slab_ref[pl.ds(pl.multiple_of(b * 8, 8), 8), :]
-            sx, sy, sz, vx, vy, vz, mass = [source[k : k + 1] for k in range(7)]
-            rx = sx - tx
-            ry = sy - ty
-            rz = sz - tz
-            wx = vx - ux
-            wy = vy - uy
-            wz = vz - uz
-            square = (rx * rx + softening_square) + ry * ry + rz * rz
-            dot = rx * wx + ry * wy + rz * wz
-            inverse = lax.rsqrt(square)
-            inverse2 = inverse * inverse
-            weight = (mass * inverse) * inverse2
-            radial = (3.0 * dot) * inverse2
-            return (
-                ax + weight * rx,
-                ay + weight * ry,
-                az + weight * rz,
-                jx + weight * (wx - radial * rx),
-                jy + weight * (wy - radial * ry),
-                jz + weight * (wz - radial * rz),
-            )
-
-        def blocks(turn8, acc):
-            for k in range(8):
-                acc = block(turn8 * 8 + k, acc)
-            return acc
-
-        acc = lax.fori_loop(0, BLOCKS // 8, blocks, (zero,) * 6)
-        result = zero
-        for k in range(6):
-            result = jnp.where(column == k, jnp.sum(acc[k], axis=1, keepdims=True), result)
-        sum_ref[pl.ds(begin, 16), :] = result
-        return carry
-
-    lax.fori_loop(0, (size + 15) >> 4, tile_of_targets, 0)
-    for half in range(2):
-        out_ref[half * 8 : half * 8 + 8, :] = sum_ref[half * LANES : (half + 1) * LANES, :].T[0:8]
+
+    for v in range(SETS):
+        for c in range(7):
+            at = (c * SETS + v) * 8
+            source_ref[at : at + 8, :] = slab_ref[pl.ds(v * 64 + c, 8, stride=8), :]
+
+    def one_half(half):
+        mine = targets[half * 8 : half * 8 + 8]
+        for t in range(LANES):
+            values = take(mine, jnp.full((8, LANES), t, I32))
+            for c in range(6):
+                at = (t * 6 + c) * 8
+                splat_ref[at : at + 8, :] = jnp.broadcast_to(values[c : c + 1], (8, LANES))
+
+        def four_targets(turn, carry):
+            first = turn * 4
+            sums = [zero] * 24
+            for v in range(SETS):
+                sx, sy, sz, vx, vy, vz, mass = [
+                    source_ref[(c * SETS + v) * 8 : (c * SETS + v) * 8 + 8, :] for c in range(7)
+                ]
+                for t in range(4):
+                    tx, ty, tz, ux, uy, uz = [
+                        splat_ref[pl.ds(pl.multiple_of(((first + t) * 6 + c) * 8, 8), 8), :]
+                        for c in range(6)
+                    ]
+                    rx = sx - tx
+                    ry = sy - ty
+                    rz = sz - tz
+                    wx = vx - ux
+                    wy = vy - uy
+                    wz = vz - uz
+                    square = (rx * rx + softening_square) + ry * ry + rz * rz
+                    dot = rx * wx + ry * wy + rz * wz
+                    inverse = lax.rsqrt(square)
+                    inverse2 = inverse * inverse
+                    weight = (mass * inverse) * inverse2
+                    radial = (3.0 * dot) * inverse2
+                    terms = (
+                        rx, ry, rz,
+                        wx - radial * rx, wy - radial * ry, wz - radial * rz,
+                    )
+                    for c in range(6):
+                        sums[t * 6 + c] = sums[t * 6 + c] + weight * terms[c]
+            for t in range(4):
+                for c in range(6):
+                    part_ref[pl.ds(pl.multiple_of((c * LANES + first + t) * 8, 8), 8), :] = sums[t * 6 + c]
+            return carry
+
+        count = jnp.minimum(size - half * LANES, LANES)
+        lax.fori_loop(0, (count + 3) >> 2, four_targets, 0)
+        rows = []
+        for o in range(16):
+            row = zero
+            for c in range(6):
+                first = (c * LANES + o * 8) * 8
+                total = part_ref[pl.ds(first, 8, stride=8), :]
+                for k in range(1, 8):
+                    total = total + part_ref[pl.ds(first + k, 8, stride=8), :]
+                row = jnp.where(column == c, jnp.sum(total, axis=1, keepdims=True), row)
+            rows.append(row)
+        out_ref[half * 8 : half * 8 + 8, :] = jnp.concatenate(rows, axis=0).T[0:8]
+
+    one_half(0)
+
+    @pl.when(size <= LANES)
+    def _():
+        out_ref[8:16, :] = zero
+
+    @pl.when(size > LANES)
+    def _():
+        one_half(1)
+
+
+def combine_kernel(own_ref, one_ref, two_ref, three_ref, out_ref):
+    force = own_ref[...] + one_ref[...] + two_ref[...] + three_ref[...]
+    for peer in range(32):
+        out_ref[peer] = force
 
 
 def finish_kernel(
@@ -336,13 +367,17 @@
     return lax.all_gather(part, "c").reshape(1024, LANES)
 
 
+def in_vmem(*arrays):
+    return [pltpu.with_memory_space_constraint(array, pltpu.VMEM) for array in arrays]
+
+
 def body(state, mass, elapsed, active_ids, active_count):
     mass = mass.reshape(1, SHARD)
     elapsed = elapsed.reshape(1, SHARD)
     ids = active_ids.reshape(1, CAP)
     packed = pl.pallas_call(
         pack_kernel,
-        out_shape=jax.ShapeDtypeStruct((32, 16, LANES), F32),
+        out_shape=pltpu.VMEM((32, 16, LANES), F32),
         in_specs=[VMEM] * 4,
         out_specs=VMEM,
         name="pack",
@@ -350,33 +385,43 @@
     slab = spread(packed)
     own = pl.pallas_call(
         extract_kernel,
-        out_shape=jax.ShapeDtypeStruct((16, LANES), F32),
+        out_shape=pltpu.VMEM((16, LANES), F32),
         in_specs=[SMEM, VMEM],
         out_specs=VMEM,
         name="extract",
-    )(active_count, slab)
+    )(active_count, *in_vmem(slab))
     others = exchange_y(own)
-    square = jax.ShapeDtypeStruct((LANES, LANES), F32)
+    square = pltpu.VMEM((LANES, LANES), F32)
     plan = pl.pallas_call(
         plan_kernel,
         out_shape=[jax.ShapeDtypeStruct((1,), I32)]
-        + [jax.ShapeDtypeStruct((16, LANES), I32)] * 3
+        + [pltpu.VMEM((16, LANES), I32)] * 3
         + [square] * 3,
         in_specs=[SMEM] + [VMEM] * 3,
         out_specs=[SMEM] + [VMEM] * 6,
         name="plan",
-    )(active_count, slab, state, elapsed)
+    )(active_count, *in_vmem(slab, state, elapsed))
     partial = pl.pallas_call(
         pair_kernel,
-        out_shape=jax.ShapeDtypeStruct((16, LANES), F32),
+        out_shape=pltpu.VMEM((16, LANES), F32),
         in_specs=[SMEM] + [VMEM] * 5,
         out_specs=VMEM,
-        scratch_shapes=[pltpu.VMEM((256, LANES), F32), pltpu.VMEM((256, LANES), F32)],
+        scratch_shapes=[
+            pltpu.VMEM((LANES * 6 * 8, LANES), F32),
+            pltpu.VMEM((7 * SETS * 8, LANES), F32),
+            pltpu.VMEM((6 * LANES * 8, LANES), F32),
+        ],
+        compiler_params=pltpu.CompilerParams(vmem_limit_bytes=24 * 2**20),
         name="pairs",
-    )(active_count, own, *others, slab)
-    more = exchange_y(partial)
-    force = partial + more[0] + more[1] + more[2]
-    forces = spread(jnp.broadcast_to(force[None], (32, 16, LANES)))
+    )(active_count, *in_vmem(own, *others, slab))
+    combined = pl.pallas_call(
+        combine_kernel,
+        out_shape=pltpu.VMEM((32, 16, LANES), F32),
+        in_specs=[VMEM] * 4,
+        out_specs=VMEM,
+        name="combine",
+    )(*in_vmem(partial, *exchange_y(partial)))
+    forces = spread(combined)
     return pl.pallas_call(
         finish_kernel,
         out_shape=[
@@ -386,7 +431,7 @@
         in_specs=[SMEM] * 2 + [VMEM] * 8,
         out_specs=[VMEM, VMEM],
         name="finish",
-    )(active_count, *plan, forces, state)
+    )(active_count, plan[0], *in_vmem(*plan[1:], forces, state))
 
 
 def solution(mesh):

time: 84.1 us -> 77.4 us (0.920)
  Pallas kernels: 25.6 us -> 21 us
  local copies, waits for them, and re-layouts: 1.82 us -> 0.01 us
    pallas_call x3 -> x4, Pallas kernels: 17.1 us -> 13.6 us  [the longest x1 10.8 us: body(): pl.pallas_call(pair_kernel, out_shape=pltpu.VMEM((16, LANES), F32), in_sp...]
    unnamed x6, local copies, waits for them, and re-layouts: 1.1 us -> 0.01 us
  transfers between devices with their start and end apart: 7 -> 7, of which waited for: 6 -> 5; matrix products, arithmetic and copies ran while one was open for 0% -> 0% of each run, Pallas kernels for 6% -> 6%
where the time goes in v3:
time: 77.4 us; the launch traced here: 77.2 us
  blocking collectives  33.4 us (43%)
  Pallas kernels  21 us (27%)
  waiting for transfers between devices  11.3 us (15%)
  starting transfers between devices  10.7 us (14%)
    all_to_all x1, blocking collectives, spread(): part = lax.all_to_all(part, ('x', 'z'), 0, 0)  21.4 us
    all_gather x2, blocking collectives, spread(): return lax.all_gather(part, 'c').reshape(1024, LANES)  12.1 us
    pallas_call x1, Pallas kernels, body(): pl.pallas_call(pair_kernel, out_shape=pltpu.VMEM((16, LANES), F32), in_sp...  10.8 us
    ppermute x6, starting transfers between devices, exchange_y(): lax.ppermute(part, 'y', [(i, (i + k) % 4) for i in range(4)])  6.43 us
    ppermute x6, waiting for transfers between devices, exchange_y(): lax.ppermute(part, 'y', [(i, (i + k) % 4) for i in range(4)])  6 us
    all_to_all x1, waiting for transfers between devices, spread(): part = lax.all_to_all(part, ('x', 'z'), 0, 0)  5.3 us
    pallas_call x1, Pallas kernels, body(): pl.pallas_call(plan_kernel, out_shape=[jax.ShapeDtypeStruct((1,), I32)] +...  4.41 us
    all_to_all x1, starting transfers between devices, spread(): part = lax.all_to_all(part, ('x', 'z'), 0, 0)  4.25 us
  transfers between devices with their start and end apart: 7, of which 5 were waited for; matrix products, arithmetic and copies ran while one was open for 0% of the time, Pallas kernels for 6%

profile of v3, /device:TPU:1, one launch (start us, length us, event | category | flops | bytes accessed | tf_op | source)
XLA Modules:
  0.0 77.2 jit_solution(2731802271783630194)
XLA Ops:
  0.6 1.0 %pack.1 = f32[32,16,128]{2,1,0:T(8,128)S(1)} custom-call(f32[12,2048]{1,0:T(8,128)} %state_ref.5, f32[1,2048]{1,0:T(1,128)} %bitcast.11, f32[1,2048]{1,0:T(1,128)} %bitcast.9, s32[1,2048]{1,0:T(1,128)} %bitcast.12), custom_call_target="tpu_custom_call" | custom-call | tf_op jit(solution)/shard_map/pack/pallas_call | solution.py:378
  1.6 21.4 %all_to_all.10 = f32[32,16,128]{2,1,0:T(8,128)S(1)} all-to-all(f32[32,16,128]{2,1,0:T(8,128)S(1)} %pack.1), channel_id=1, replica_groups=mesh['x'=4,'c'=2,'y'=4,'z'=8] {'x','z'}, dimensions={0} | all-to-all | bytes 524288 | tf_op jit(solution)/shard_map/all_to_all | solution.py:366
  22.9 5.5 %all-gather = f32[64,16,128]{2,1,0:T(8,128)S(1)} all-gather(f32[32,16,128]{2,1,0:T(8,128)S(1)} %all_to_all.10), channel_id=2, replica_groups=mesh['x'=4,'c'=2,'y'=4,'z'=8] {'c'}, dimensions={0}, use_global_device_ids=true | all-gather | bytes 786432 | tf_op jit(solution)/shard_map/all_gather | solution.py:367
  28.5 0.0 copy-start.2
  28.5 1.1 %extract.1.own_ref = f32[16,128]{1,0:T(8,128)S(1)} custom-call(s32[8]{0:T(128)} %counts_ref.7, f32[1024,128]{1,0:T(8,128)S(1)} %bitcast.5), custom_call_target="tpu_custom_call" | custom-call | tf_op jit(solution)/shard_map/extract/pallas_call | solution.py:386
  29.6 2.8 %collective-permute-start.2 = (f32[16,128]{1,0:T(8,128)S(1)}, f32[16,128]{1,0:T(8,128)S(1)}, u32[]{:S(2)}, u32[]{:S(2)}) collective-permute-start(f32[16,128]{1,0:T(8,128)S(1)} %extract.1.own_ref), channel_id=1, source_target_pairs={{0,24},{8,0},{16,8},{24,16},{1,25},{9,1},{17,9},{25,17},{2,26},{10... | collective-permute-start | bytes 24584 | tf_op jit(solution)/shard_map/ppermute | solution.py:362
  32.4 0.3 collective-permute-start.1
  32.7 0.7 collective-permute-start
  33.4 0.0 collective-permute-done.2.three_ref
  33.4 3.0 %collective-permute-done.1.two_ref = f32[16,128]{1,0:T(8,128)S(1)} collective-permute-done((f32[16,128]{1,0:T(8,128)S(1)}, f32[16,128]{1,0:T(8,128)S(1)}, u32[]{:S(2)}, u32[]{:S(2)}) %collective-permute-start.1) | collective-permute-done | bytes 8224 | tf_op jit(solution)/shard_map/ppermute | solution.py:362
  36.4 0.1 collective-permute-done.one_ref
  36.5 0.0 copy-done.2
  36.5 10.8 %pairs.1.own_ref = f32[16,128]{1,0:T(8,128)S(1)} custom-call(s32[8]{0:T(128)S(1)} %copy-done.2, f32[16,128]{1,0:T(8,128)S(1)} %extract.1.own_ref, f32[16,128]{1,0:T(8,128)S(1)} %collective-permute-done.one_ref, f32[16,128]{1,0:T(8,128)S(1)} %collective-permute-done.1.two_ref, f32[16,128]{1,0:T(8,128)S(1)} %collective-permute-done.2.three_ref, ...), custom_call_target="tpu_custom_call" | custom-call | tf_op jit(solution)/shard_map/pairs/pallas_call | solution.py:404
  47.3 0.6 collective-permute-start.5
  48.0 1.2 %collective-permute-start.4 = (f32[16,128]{1,0:T(8,128)S(1)}, f32[16,128]{1,0:T(8,128)S(1)}, u32[]{:S(2)}, u32[]{:S(2)}) collective-permute-start(f32[16,128]{1,0:T(8,128)S(1)} %pairs.1.own_ref), channel_id=1, source_target_pairs={{0,16},{8,24},{16,0},{24,8},{1,17},{9,25},{17,1},{25,9},{2,18},{10... | collective-permute-start | bytes 24584 | tf_op jit(solution)/shard_map/ppermute | solution.py:362
  49.2 0.8 collective-permute-start.3
  49.9 0.0 collective-permute-done.5.three_ref
  49.9 2.0 %collective-permute-done.4.two_ref = f32[16,128]{1,0:T(8,128)S(1)} collective-permute-done((f32[16,128]{1,0:T(8,128)S(1)}, f32[16,128]{1,0:T(8,128)S(1)}, u32[]{:S(2)}, u32[]{:S(2)}) %collective-permute-start.4) | collective-permute-done | bytes 8224 | tf_op jit(solution)/shard_map/ppermute | solution.py:362
  52.0 0.9 %collective-permute-done.3.one_ref = f32[16,128]{1,0:T(8,128)S(1)} collective-permute-done((f32[16,128]{1,0:T(8,128)S(1)}, f32[16,128]{1,0:T(8,128)S(1)}, u32[]{:S(2)}, u32[]{:S(2)}) %collective-permute-start.3) | collective-permute-done | bytes 8224 | tf_op jit(solution)/shard_map/ppermute | solution.py:362
  52.9 0.7 combine.1
  53.6 0.0 copy-start
  53.6 0.0 copy-start.1
  53.6 4.2 %all-to-all-start.1 = ((f32[32,16,128]{2,1,0:T(8,128)}), f32[32,16,128]{2,1,0:T(8,128)S(1)}, u32[]{:S(2)}, u32[]{:S(2)}) async-start(f32[32,16,128]{2,1,0:T(8,128)} %combine.1), calls=%async_computation.1 | async-start | bytes 524288 | tf_op jit(solution)/shard_map/all_to_all | solution.py:366
  57.9 0.0 copy-done
  57.9 0.0 copy-done.1
  57.9 4.4 %plan.1 = (s32[1]{0:T(128)}, s32[16,128]{1,0:T(8,128)S(1)}, s32[16,128]{1,0:T(8,128)S(1)}, s32[16,128]{1,0:T(8,128)S(1)}, f32[128,128]{1,0:T(8,128)S(1)}, /*inde...) custom-call(s32[8]{0:T(128)} %counts_ref.7, f32[1024,128]{1,0:T(8,128)S(1)} %bitcast.7, f32[12,2048]{1,0:T(8,128)S(1)} %copy-done, ...), custom_call_target="tpu_custom_call" | custom-call | tf_op jit(solution)/shard_map/plan/pallas_call | solution.py:395
  62.3 5.3 %all-to-all-done.1 = f32[32,16,128]{2,1,0:T(8,128)S(1)} async-done(((f32[32,16,128]{2,1,0:T(8,128)}), f32[32,16,128]{2,1,0:T(8,128)S(1)}, u32[]{:S(2)}, u32[]{:S(2)}) %all-to-all-start.1) | async-done | bytes 262176 | tf_op jit(solution)/shard_map/all_to_all | solution.py:366
  67.6 6.6 %all-gather.1 = f32[64,16,128]{2,1,0:T(8,128)S(1)} all-gather(f32[32,16,128]{2,1,0:T(8,128)S(1)} %all-to-all-done.1), channel_id=3, replica_groups=mesh['x'=4,'c'=2,'y'=4,'z'=8] {'c'}, dimensions={0}, use_global_device_ids=true | all-gather | bytes 786432 | tf_op jit(solution)/shard_map/all_gather | solution.py:367
  74.2 3.0 %finish.1 = (f32[12,2048]{1,0:T(8,128)}, f32[6,2048]{1,0:T(8,128)}) custom-call(s32[8]{0:T(128)} %counts_ref.7, s32[1]{0:T(128)} %get-tuple-element.9.number_ref, s32[16,128]{1,0:T(8,128)S(1)} %get-tuple-element.10.rank_ref, s32[16,128]{1,0:T(8,128)S(1)} %get-tuple-element.11.block_ref, s32[16,128]{1,0:T(8,128)S(1)} %get-tuple-element.12.lane_ref, ...), custom_call_target="tpu_custom_call" | custom-call | tf_op jit(solution)/shard_map/finish/pallas_call | solution.py:425
Async XLA Ops:
  28.5 8.0 %copy-start.2 = (s32[8]{0:T(128)S(1)}, s32[8]{0:T(128)}, u32[]{:S(2)}) copy-start(s32[8]{0:T(128)} %counts_ref.7) | copy-start | bytes 100
  29.6 3.9 %collective-permute-start.2 = (f32[16,128]{1,0:T(8,128)S(1)}, f32[16,128]{1,0:T(8,128)S(1)}, u32[]{:S(2)}, u32[]{:S(2)}) collective-permute-start(f32[16,128]{1,0:T(8,128)S(1)} %extract.1.own_ref), channel_id=1, source_target_pairs={{0,24},{8,0},{16,8},{24,16},{1,25},{9,1},{17,9},{25,17},{2,26},{10... | collective-permute-start | bytes 24584 | tf_op jit(solution)/shard_map/ppermute | solution.py:362
  32.4 4.0 %collective-permute-start.1 = (f32[16,128]{1,0:T(8,128)S(1)}, f32[16,128]{1,0:T(8,128)S(1)}, u32[]{:S(2)}, u32[]{:S(2)}) collective-permute-start(f32[16,128]{1,0:T(8,128)S(1)} %extract.1.own_ref), channel_id=1, source_target_pairs={{0,16},{8,24},{16,0},{24,8},{1,17},{9,25},{17,1},{25,9},{2,18},{10... | collective-permute-start | bytes 24584 | tf_op jit(solution)/shard_map/ppermute | solution.py:362
  32.7 3.7 %collective-permute-start = (f32[16,128]{1,0:T(8,128)S(1)}, f32[16,128]{1,0:T(8,128)S(1)}, u32[]{:S(2)}, u32[]{:S(2)}) collective-permute-start(f32[16,128]{1,0:T(8,128)S(1)} %extract.1.own_ref), channel_id=1, source_target_pairs={{0,8},{8,16},{16,24},{24,0},{1,9},{9,17},{17,25},{25,1},{2,10},{10... | collective-permute-start | bytes 24584 | tf_op jit(solution)/shard_map/ppermute | solution.py:362
  47.3 2.6 %collective-permute-start.5 = (f32[16,128]{1,0:T(8,128)S(1)}, f32[16,128]{1,0:T(8,128)S(1)}, u32[]{:S(2)}, u32[]{:S(2)}) collective-permute-start(f32[16,128]{1,0:T(8,128)S(1)} %pairs.1.own_ref), channel_id=1, source_target_pairs={{0,24},{8,0},{16,8},{24,16},{1,25},{9,1},{17,9},{25,17},{2,26},{10... | collective-permute-start | bytes 24584 | tf_op jit(solution)/shard_map/ppermute | solution.py:362
  48.0 4.0 %collective-permute-start.4 = (f32[16,128]{1,0:T(8,128)S(1)}, f32[16,128]{1,0:T(8,128)S(1)}, u32[]{:S(2)}, u32[]{:S(2)}) collective-permute-start(f32[16,128]{1,0:T(8,128)S(1)} %pairs.1.own_ref), channel_id=1, source_target_pairs={{0,16},{8,24},{16,0},{24,8},{1,17},{9,25},{17,1},{25,9},{2,18},{10... | collective-permute-start | bytes 24584 | tf_op jit(solution)/shard_map/ppermute | solution.py:362
  49.2 3.7 %collective-permute-start.3 = (f32[16,128]{1,0:T(8,128)S(1)}, f32[16,128]{1,0:T(8,128)S(1)}, u32[]{:S(2)}, u32[]{:S(2)}) collective-permute-start(f32[16,128]{1,0:T(8,128)S(1)} %pairs.1.own_ref), channel_id=1, source_target_pairs={{0,8},{8,16},{16,24},{24,0},{1,9},{9,17},{17,25},{25,1},{2,10},{10... | collective-permute-start | bytes 24584 | tf_op jit(solution)/shard_map/ppermute | solution.py:362
  53.6 4.3 %copy-start = (f32[12,2048]{1,0:T(8,128)S(1)}, f32[12,2048]{1,0:T(8,128)}, u32[]{:S(2)}) copy-start(f32[12,2048]{1,0:T(8,128)} %state_ref.5) | copy-start | bytes 294916
  53.6 4.3 %copy-start.1 = (f32[2048]{0:T(1024)S(1)}, f32[2048]{0:T(1024)}, u32[]{:S(2)}) copy-start(f32[2048]{0:T(1024)} %param.7) | copy-start | bytes 24580
  53.6 14.0 %all-to-all-start.1 = ((f32[32,16,128]{2,1,0:T(8,128)}), f32[32,16,128]{2,1,0:T(8,128)S(1)}, u32[]{:S(2)}, u32[]{:S(2)}) async-start(f32[32,16,128]{2,1,0:T(8,128)} %combine.1), calls=%async_computation.1 | async-start | bytes 524288 | tf_op jit(solution)/shard_map/all_to_all | solution.py:366

commit v4 on v3

--- a/solution.py
+++ b/solution.py
@@ -28,6 +28,13 @@
     for i in range(LISTS):
         offsets.append(offsets[-1] + counts_ref[i])
     return offsets[:LISTS], offsets[LISTS]
+
+
+def at_list(offsets, wanted):
+    start = jnp.int32(0)
+    for i in range(LISTS):
+        start = jnp.where(wanted == i, offsets[i], start)
+    return start
 
 
 def group_size(live):
@@ -58,11 +65,13 @@
         out_ref[peer] = both
 
 
-def extract_kernel(counts_ref, slab_ref, out_ref):
+def extract_kernel(counts_ref, mine_ref, other_ref, out_ref):
     offsets, live = list_offsets(counts_ref)
     size = group_size(live)
-    group = lax.axis_index("c") * 32 + lax.axis_index("x") * 8 + lax.axis_index("z")
+    core = lax.axis_index("c")
+    group = core * 32 + lax.axis_index("x") * 8 + lax.axis_index("z")
     my_y = lax.axis_index("y")
+    halves = (mine_ref, other_ref)
     sub = lax.broadcasted_iota(I32, (8, LANES), 0)
     column = lax.broadcasted_iota(I32, (8, LANES), 1)
 
@@ -77,21 +86,21 @@
             which = jnp.where(after, i, which)
             base = jnp.where(after, offsets[i], base)
         slot = jnp.where(valid, position - base, 0)
-        block = (which & 1) * 64 + (which >> 1) * 16 + (slot >> 8) * 2 + ((slot >> 7) & 1)
+        block = ((which & 1) ^ core) * 64 + (which >> 1) * 16 + (slot >> 7)
         within = slot & 127
         found = jnp.zeros((8, LANES), F32)
         for v in range(16):
-            tile = slab_ref[pl.ds(7 + 64 * v, 8, stride=8), :]
+            tile = halves[v >> 3][pl.ds(7 + 64 * (v & 7), 8, stride=8), :]
             found = jnp.where(block == v * 8 + sub, take(tile, within), found)
         star = jnp.broadcast_to(jnp.sum(found, axis=0, keepdims=True), (8, LANES)).astype(I32)
         mine = valid & ((star >> 14) == my_y)
-        place = ((star >> 8) & 1) * 64 + ((star >> 9) & 3) * 16 + ((star >> 11) & 7) * 2 + ((star >> 7) & 1)
+        place = (((star >> 8) & 1) ^ core) * 64 + ((star >> 9) & 3) * 16 + ((star >> 11) & 7) * 2 + ((star >> 7) & 1)
         place = jnp.where(mine, place, -1)
         inside = star & 127
-
         picked = jnp.zeros((8, LANES), F32)
         for b in range(BLOCKS):
-            picked = jnp.where(place == b, take(slab_ref[b * 8 : b * 8 + 8, :], inside), picked)
+            tile = halves[b >> 6][(b & 63) * 8 : (b & 63) * 8 + 8, :]
+            picked = jnp.where(place == b, take(tile, inside), picked)
         out_ref[half * 8 : half * 8 + 8, :] = jnp.where(sub < 6, picked, 0.0)
 
     one_half(0)
@@ -103,7 +112,7 @@
 
 
 def plan_kernel(
-    counts_ref, slab_ref, state_ref, elapsed_ref,
+    counts_ref, mine_ref, other_ref, state_ref, elapsed_ref,
     number_ref, rank_ref, block_ref, lane_ref, known_ref, one_ref, two_ref,
 ):
     offsets, live = list_offsets(counts_ref)
@@ -117,18 +126,22 @@
     square_column = lax.broadcasted_iota(I32, (LANES, LANES), 1)
     contract = (((1,), (1,)), ((), ()))
     total = jnp.zeros((32, LANES), F32)
-    for i in range(LISTS):
-        first = 7 + 64 * ((i & 1) * 8 + (i >> 1) * 2)
+    for n in range(LISTS):
+        i = (n & 6) + ((n & 1) ^ lax.axis_index("c"))
+        count = counts_ref[i]
+        start = at_list(offsets, i)
+        half_ref = other_ref if n & 1 else mine_ref
+        first = 7 + 64 * (n & 6)
 
         def step(turn, acc):
-            ids8 = slab_ref[pl.ds(first + 64 * turn, 8, stride=8), :].astype(I32)
+            ids8 = half_ref[pl.ds(first + 64 * turn, 8, stride=8), :].astype(I32)
             for k in range(0, 8, 2):
                 ids = jnp.concatenate([ids8[k : k + 1], ids8[k + 1 : k + 2]], axis=1)
                 slot = turn * 1024 + k * LANES + column
-                mine = (slot < counts_ref[i]) & ((ids >> 11) == shard)
+                mine = (slot < count) & ((ids >> 11) == shard)
                 high = jnp.where(mine, (ids >> 7) & 15, -1)
                 low = ids & 127
-                mark = offsets[i] + slot + 1
+                mark = start + slot + 1
                 here = row16 == high
                 left = jnp.concatenate(
                     [
@@ -141,7 +154,7 @@
                 acc = acc + lax.dot_general(left, right, contract, preferred_element_type=F32)
             return acc
 
-        total = lax.fori_loop(0, (counts_ref[i] + 1023) >> 10, step, total)
+        total = lax.fori_loop(0, (count + 1023) >> 10, step, total)
     mark = (total[0:16] * 128.0 + total[16:32]).astype(I32)
     active = mark > 0
     flags = jnp.where(active, 1.0, 0.0).astype(jnp.bfloat16)
@@ -202,19 +215,20 @@
 
 
 def pair_kernel(
-    counts_ref, own_ref, one_ref, two_ref, three_ref, slab_ref, out_ref,
+    counts_ref, own_ref, one_ref, two_ref, three_ref, mine_ref, other_ref, out_ref,
     splat_ref, source_ref, part_ref,
 ):
     _, live = list_offsets(counts_ref)
     size = group_size(live)
     column = lax.broadcasted_iota(I32, (8, LANES), 1)
     zero = jnp.zeros((8, LANES), F32)
+    halves = (mine_ref, other_ref)
     targets = own_ref[...] + one_ref[...] + two_ref[...] + three_ref[...]
 
     for v in range(SETS):
         for c in range(7):
             at = (c * SETS + v) * 8
-            source_ref[at : at + 8, :] = slab_ref[pl.ds(v * 64 + c, 8, stride=8), :]
+            source_ref[at : at + 8, :] = halves[v >> 3][pl.ds((v & 7) * 64 + c, 8, stride=8), :]
 
     def one_half(half):
         mine = targets[half * 8 : half * 8 + 8]
@@ -292,16 +306,15 @@
 
 def finish_kernel(
     counts_ref, number_ref, rank_ref, block_ref, lane_ref, known_ref, one_ref, two_ref,
-    force_ref, state_ref, new_ref, active_ref,
+    mine_ref, other_ref, state_ref, new_ref, active_ref,
 ):
     offsets, live = list_offsets(counts_ref)
     size = group_size(live)
     full = jnp.where(size > LANES, 1, 0)
-    my_list = lax.axis_index("x") * 2 + lax.axis_index("c")
+    core = lax.axis_index("c")
+    my_list = lax.axis_index("x") * 2 + core
     count = counts_ref[my_list]
-    start = jnp.int32(0)
-    for i in range(LISTS):
-        start = jnp.where(my_list == i, offsets[i], start)
+    start = at_list(offsets, my_list)
     zero = jnp.zeros((8, LANES), F32)
     row = lax.broadcasted_iota(I32, (8, LANES), 1)
 
@@ -317,8 +330,9 @@
         acc = list(acc)
         for b in range(CAP // LANES):
             tile = jnp.minimum(firsts[b] + (turn >> full), GROUPS - 1) * 2 + (turn & full)
-            got = take(force_ref[pl.ds(pl.multiple_of(tile * 8, 8), 8), :], lanes[b])
-            acc[b] = jnp.where(blocks[b] == tile, got, acc[b])
+            rows = pl.ds(pl.multiple_of((tile & 63) * 8, 8), 8)
+            forces = jnp.where((tile >> 6) == core, mine_ref[rows, :], other_ref[rows, :])
+            acc[b] = jnp.where(blocks[b] == tile, take(forces, lanes[b]), acc[b])
         return tuple(acc)
 
     spans = lax.div(jnp.int32(LANES - 1), size) + 2
@@ -330,12 +344,13 @@
     none = jnp.zeros((2, LANES), F32)
 
     def compact(turn, carry):
-        block = jnp.broadcast_to(block_ref[pl.ds(turn, 1), :], (8, LANES))
+        block = jnp.broadcast_to(block_ref[pl.ds(turn, 1), :], (8, LANES)) ^ (core * 64)
         lane = jnp.broadcast_to(lane_ref[pl.ds(turn, 1), :], (8, LANES))
 
         def half(h, force):
             for g in range(GROUPS):
-                tile = force_ref[pl.ds(pl.multiple_of(g * 16 + h * 8, 8), 8), :]
+                half_ref = mine_ref if g < 32 else other_ref
+                tile = half_ref[pl.ds(pl.multiple_of((g & 31) * 16 + h * 8, 8), 8), :]
                 force = jnp.where(block == g * 2 + h, take(tile, lane), force)
             return force
 
@@ -362,13 +377,14 @@
     return [lax.ppermute(part, "y", [(i, (i + k) % 4) for i in range(4)]) for k in range(1, 4)]
 
 
-def spread(part):
-    part = lax.all_to_all(part, ("x", "z"), 0, 0)
-    return lax.all_gather(part, "c").reshape(1024, LANES)
-
-
 def in_vmem(*arrays):
     return [pltpu.with_memory_space_constraint(array, pltpu.VMEM) for array in arrays]
+
+
+def spread(part, *done):
+    part = lax.all_to_all(part, ("x", "z"), 0, 0).reshape(512, LANES)
+    part, *done = lax.optimization_barrier((part, *done))
+    return in_vmem(part, lax.ppermute(part, "c", [(0, 1), (1, 0)])), done
 
 
 def body(state, mass, elapsed, active_ids, active_count):
@@ -382,14 +398,14 @@
         out_specs=VMEM,
         name="pack",
     )(state, mass, elapsed, ids)
-    slab = spread(packed)
+    slab, _ = spread(packed)
     own = pl.pallas_call(
         extract_kernel,
         out_shape=pltpu.VMEM((16, LANES), F32),
-        in_specs=[SMEM, VMEM],
+        in_specs=[SMEM, VMEM, VMEM],
         out_specs=VMEM,
         name="extract",
-    )(active_count, *in_vmem(slab))
+    )(active_count, *slab)
     others = exchange_y(own)
     square = pltpu.VMEM((LANES, LANES), F32)
     plan = pl.pallas_call(
@@ -397,14 +413,14 @@
         out_shape=[jax.ShapeDtypeStruct((1,), I32)]
         + [pltpu.VMEM((16, LANES), I32)] * 3
         + [square] * 3,
-        in_specs=[SMEM] + [VMEM] * 3,
+        in_specs=[SMEM] + [VMEM] * 4,
         out_specs=[SMEM] + [VMEM] * 6,
         name="plan",
-    )(active_count, *in_vmem(slab, state, elapsed))
+    )(active_count, *slab, *in_vmem(state, elapsed))
     partial = pl.pallas_call(
         pair_kernel,
         out_shape=pltpu.VMEM((16, LANES), F32),
-        in_specs=[SMEM] + [VMEM] * 5,
+        in_specs=[SMEM] + [VMEM] * 6,
         out_specs=VMEM,
         scratch_shapes=[
             pltpu.VMEM((LANES * 6 * 8, LANES), F32),
@@ -413,7 +429,7 @@
         ],
         compiler_params=pltpu.CompilerParams(vmem_limit_bytes=24 * 2**20),
         name="pairs",
-    )(active_count, *in_vmem(own, *others, slab))
+    )(active_count, *in_vmem(own, *others), *slab)
     combined = pl.pallas_call(
         combine_kernel,
         out_shape=pltpu.VMEM((32, 16, LANES), F32),
@@ -421,17 +437,17 @@
         out_specs=VMEM,
         name="combine",
     )(*in_vmem(partial, *exchange_y(partial)))
-    forces = spread(combined)
+    forces, plan = spread(combined, *plan)
     return pl.pallas_call(
         finish_kernel,
         out_shape=[
             jax.ShapeDtypeStruct((12, SHARD), F32),
             jax.ShapeDtypeStruct((6, CAP), F32),
         ],
-        in_specs=[SMEM] * 2 + [VMEM] * 8,
+        in_specs=[SMEM] * 2 + [VMEM] * 9,
         out_specs=[VMEM, VMEM],
         name="finish",
-    )(active_count, plan[0], *in_vmem(*plan[1:], forces, state))
+    )(active_count, plan[0], *in_vmem(*plan[1:]), *forces, *in_vmem(state))
 
 
 def solution(mesh):

time: 77.4 us -> 74.8 us (0.966)
  blocking collectives: 33.4 us -> 21.4 us
  starting transfers between devices: 10.7 us -> 19.2 us
  waiting for transfers between devices: 11.3 us -> 13.6 us
  Pallas kernels: 21 us -> 20.2 us
    all_gather x2 -> x0, blocking collectives: 12.1 us -> none  [spread(): return lax.all_gather(part, 'c').reshape(1024, LANES)]
    ppermute x0 -> x2, starting transfers between devices: none -> 8.5 us  [spread(): return (in_vmem(part, lax.ppermute(part, 'c', [(0, 1), (1, 0)])), done)]
    ppermute x0 -> x2, waiting for transfers between devices: none -> 2.32 us  [spread(): return (in_vmem(part, lax.ppermute(part, 'c', [(0, 1), (1, 0)])), done)]
  transfers between devices with their start and end apart: 7 -> 9, of which waited for: 5 -> 7; matrix products, arithmetic and copies ran while one was open for 0% -> 0% of each run, Pallas kernels for 6% -> 6%
where the time goes in v4:
time: 74.8 us; the launch traced here: 75 us
  blocking collectives  21.4 us (29%)
  Pallas kernels  20.2 us (27%)
  starting transfers between devices  19.2 us (26%)
  waiting for transfers between devices  13.6 us (18%)
    all_to_all x1, blocking collectives, spread(): part = lax.all_to_all(part, ('x', 'z'), 0, 0).reshape(512, LANES)  21.4 us
    pallas_call x1, Pallas kernels, body(): pl.pallas_call(pair_kernel, out_shape=pltpu.VMEM((16, LANES), F32), in_sp...  10.1 us
    ppermute x2, starting transfers between devices, spread(): return (in_vmem(part, lax.ppermute(part, 'c', [(0, 1), (1, 0)])), done)  8.5 us
    ppermute x6, starting transfers between devices, exchange_y(): lax.ppermute(part, 'y', [(i, (i + k) % 4) for i in range(4)])  6.43 us
    ppermute x6, waiting for transfers between devices, exchange_y(): lax.ppermute(part, 'y', [(i, (i + k) % 4) for i in range(4)])  6 us
    all_to_all x1, waiting for transfers between devices, spread(): part = lax.all_to_all(part, ('x', 'z'), 0, 0).reshape(512, LANES)  5.29 us
    pallas_call x1, Pallas kernels, body(): pl.pallas_call(plan_kernel, out_shape=[jax.ShapeDtypeStruct((1,), I32)] +...  4.42 us
    all_to_all x1, starting transfers between devices, spread(): part = lax.all_to_all(part, ('x', 'z'), 0, 0).reshape(512, LANES)  4.25 us
  transfers between devices with their start and end apart: 9, of which 7 were waited for; matrix products, arithmetic and copies ran while one was open for 0% of the time, Pallas kernels for 6%

profile of v4, /device:TPU:1, one launch (start us, length us, event | category | flops | bytes accessed | tf_op | source)
XLA Modules:
  0.0 75.0 jit_solution(14821350075551717562)
XLA Ops:
  0.6 1.0 %pack.1 = f32[32,16,128]{2,1,0:T(8,128)S(1)} custom-call(f32[12,2048]{1,0:T(8,128)} %state_ref.5, f32[1,2048]{1,0:T(1,128)} %bitcast.13, f32[1,2048]{1,0:T(1,128)} %bitcast.11, s32[1,2048]{1,0:T(1,128)} %bitcast.14), custom_call_target="tpu_custom_call" | custom-call | tf_op jit(solution)/shard_map/pack/pallas_call | solution.py:394
  1.6 21.4 %all_to_all.10 = f32[32,16,128]{2,1,0:T(8,128)S(1)} all-to-all(f32[32,16,128]{2,1,0:T(8,128)S(1)} %pack.1), channel_id=1, replica_groups=mesh['x'=4,'c'=2,'y'=4,'z'=8] {'x','z'}, dimensions={0} | all-to-all | bytes 524288 | tf_op jit(solution)/shard_map/all_to_all | solution.py:385
  22.9 0.0 copy-start.2
  22.9 3.7 %collective-permute-start = (f32[512,128]{1,0:T(8,128)S(1)}, f32[512,128]{1,0:T(8,128)S(1)}, u32[]{:S(2)}, u32[]{:S(2)}) collective-permute-start(f32[512,128]{1,0:T(8,128)S(1)} %bitcast.5), channel_id=1, source_target_pairs={{0,32},{32,0},{1,33},{33,1},{2,34},{34,2},{3,35},{35,3},{4,36},{36... | collective-permute-start | bytes 786440 | tf_op jit(solution)/shard_map/ppermute | solution.py:387
  26.7 1.2 %collective-permute-done.other_ref = f32[512,128]{1,0:T(8,128)S(1)} collective-permute-done((f32[512,128]{1,0:T(8,128)S(1)}, f32[512,128]{1,0:T(8,128)S(1)}, u32[]{:S(2)}, u32[]{:S(2)}) %collective-permute-start) | collective-permute-done | bytes 262176 | tf_op jit(solution)/shard_map/ppermute | solution.py:387
  27.8 1.0 %extract.1.own_ref = f32[16,128]{1,0:T(8,128)S(1)} custom-call(s32[8]{0:T(128)} %counts_ref.7, f32[512,128]{1,0:T(8,128)S(1)} %bitcast.6, f32[512,128]{1,0:T(8,128)S(1)} %collective-permute-done.other_ref), custom_call_target="tpu_custom_call" | custom-call | tf_op jit(solution)/shard_map/extract/pallas_call | solution.py:402
  28.8 2.8 %collective-permute-start.3 = (f32[16,128]{1,0:T(8,128)S(1)}, f32[16,128]{1,0:T(8,128)S(1)}, u32[]{:S(2)}, u32[]{:S(2)}) collective-permute-start(f32[16,128]{1,0:T(8,128)S(1)} %extract.1.own_ref), channel_id=1, source_target_pairs={{0,24},{8,0},{16,8},{24,16},{1,25},{9,1},{17,9},{25,17},{2,26},{10... | collective-permute-start | bytes 24584 | tf_op jit(solution)/shard_map/ppermute | solution.py:377
  31.6 0.3 collective-permute-start.2
  32.0 0.7 collective-permute-start.1
  32.7 0.0 collective-permute-done.3.three_ref
  32.7 3.0 %collective-permute-done.2.two_ref = f32[16,128]{1,0:T(8,128)S(1)} collective-permute-done((f32[16,128]{1,0:T(8,128)S(1)}, f32[16,128]{1,0:T(8,128)S(1)}, u32[]{:S(2)}, u32[]{:S(2)}) %collective-permute-start.2) | collective-permute-done | bytes 8224 | tf_op jit(solution)/shard_map/ppermute | solution.py:377
  35.6 0.1 collective-permute-done.1.one_ref
  35.7 0.0 copy-done.2
  35.7 10.1 %pairs.1.own_ref = f32[16,128]{1,0:T(8,128)S(1)} custom-call(s32[8]{0:T(128)S(1)} %copy-done.2, f32[16,128]{1,0:T(8,128)S(1)} %extract.1.own_ref, f32[16,128]{1,0:T(8,128)S(1)} %collective-permute-done.1.one_ref, f32[16,128]{1,0:T(8,128)S(1)} %collective-permute-done.2.two_ref, f32[16,128]{1,0:T(8,128)S(1)} %collective-permute-done.3.three_ref, ...), custom_call_target="tpu_custom_call" | custom-call | tf_op jit(solution)/shard_map/pairs/pallas_call | solution.py:420
  45.8 0.6 collective-permute-start.6
  46.5 1.2 %collective-permute-start.5 = (f32[16,128]{1,0:T(8,128)S(1)}, f32[16,128]{1,0:T(8,128)S(1)}, u32[]{:S(2)}, u32[]{:S(2)}) collective-permute-start(f32[16,128]{1,0:T(8,128)S(1)} %pairs.1.own_ref), channel_id=1, source_target_pairs={{0,16},{8,24},{16,0},{24,8},{1,17},{9,25},{17,1},{25,9},{2,18},{10... | collective-permute-start | bytes 24584 | tf_op jit(solution)/shard_map/ppermute | solution.py:377
  47.7 0.8 %collective-permute-start.4 = (f32[16,128]{1,0:T(8,128)S(1)}, f32[16,128]{1,0:T(8,128)S(1)}, u32[]{:S(2)}, u32[]{:S(2)}) collective-permute-start(f32[16,128]{1,0:T(8,128)S(1)} %pairs.1.own_ref), channel_id=1, source_target_pairs={{0,8},{8,16},{16,24},{24,0},{1,9},{9,17},{17,25},{25,1},{2,10},{10... | collective-permute-start | bytes 24584 | tf_op jit(solution)/shard_map/ppermute | solution.py:377
  48.4 0.0 collective-permute-done.6.three_ref
  48.4 2.0 %collective-permute-done.5.two_ref = f32[16,128]{1,0:T(8,128)S(1)} collective-permute-done((f32[16,128]{1,0:T(8,128)S(1)}, f32[16,128]{1,0:T(8,128)S(1)}, u32[]{:S(2)}, u32[]{:S(2)}) %collective-permute-start.5) | collective-permute-done | bytes 8224 | tf_op jit(solution)/shard_map/ppermute | solution.py:377
  50.5 0.9 %collective-permute-done.4.one_ref = f32[16,128]{1,0:T(8,128)S(1)} collective-permute-done((f32[16,128]{1,0:T(8,128)S(1)}, f32[16,128]{1,0:T(8,128)S(1)}, u32[]{:S(2)}, u32[]{:S(2)}) %collective-permute-start.4) | collective-permute-done | bytes 8224 | tf_op jit(solution)/shard_map/ppermute | solution.py:377
  51.4 0.7 combine.1
  52.1 0.0 copy-start
  52.1 0.0 copy-start.1
  52.1 4.2 %all-to-all-start.1 = ((f32[32,16,128]{2,1,0:T(8,128)}), f32[32,16,128]{2,1,0:T(8,128)S(1)}, u32[]{:S(2)}, u32[]{:S(2)}) async-start(f32[32,16,128]{2,1,0:T(8,128)} %combine.1), calls=%async_computation.1 | async-start | bytes 524288 | tf_op jit(solution)/shard_map/all_to_all | solution.py:385
  56.4 0.0 copy-done
  56.4 0.0 copy-done.1
  56.4 4.4 %plan.1 = (s32[1]{0:T(128)}, s32[16,128]{1,0:T(8,128)S(1)}, s32[16,128]{1,0:T(8,128)S(1)}, s32[16,128]{1,0:T(8,128)S(1)}, f32[128,128]{1,0:T(8,128)S(1)}, /*inde...) custom-call(s32[8]{0:T(128)} %counts_ref.7, f32[512,128]{1,0:T(8,128)S(1)} %bitcast.8, ...), custom_call_target="tpu_custom_call" | custom-call | tf_op jit(solution)/shard_map/plan/pallas_call | solution.py:411
  60.8 5.3 %all-to-all-done.1 = f32[32,16,128]{2,1,0:T(8,128)S(1)} async-done(((f32[32,16,128]{2,1,0:T(8,128)}), f32[32,16,128]{2,1,0:T(8,128)S(1)}, u32[]{:S(2)}, u32[]{:S(2)}) %all-to-all-start.1) | async-done | bytes 262176 | tf_op jit(solution)/shard_map/all_to_all | solution.py:385
  66.1 4.8 %collective-permute-start.7 = (f32[512,128]{1,0:T(8,128)S(1)}, f32[512,128]{1,0:T(8,128)S(1)}, u32[]{:S(2)}, u32[]{:S(2)}) collective-permute-start(f32[512,128]{1,0:T(8,128)S(1)} %bitcast.9), channel_id=1, source_target_pairs={{0,32},{32,0},{1,33},{33,1},{2,34},{34,2},{3,35},{35,3},{4,36},{36... | collective-permute-start | bytes 786440 | tf_op jit(solution)/shard_map/ppermute | solution.py:387
  70.9 1.2 %collective-permute-done.7.other_ref = f32[512,128]{1,0:T(8,128)S(1)} collective-permute-done((f32[512,128]{1,0:T(8,128)S(1)}, f32[512,128]{1,0:T(8,128)S(1)}, u32[]{:S(2)}, u32[]{:S(2)}) %collective-permute-start.7) | collective-permute-done | bytes 262176 | tf_op jit(solution)/shard_map/ppermute | solution.py:387
  72.0 3.0 %finish.1 = (f32[12,2048]{1,0:T(8,128)}, f32[6,2048]{1,0:T(8,128)}) custom-call(s32[8]{0:T(128)} %counts_ref.7, s32[1]{0:T(128)} %get-tuple-element.24.number_ref, s32[16,128]{1,0:T(8,128)S(1)} %get-tuple-element.25.rank_ref, s32[16,128]{1,0:T(8,128)S(1)} %get-tuple-element.26.block_ref, s32[16,128]{1,0:T(8,128)S(1)} %get-tuple-element.27.lane_ref, ...), custom_call_target="tpu_custom_call" | custom-call | tf_op jit(solution)/shard_map/finish/pallas_call | solution.py:441
Async XLA Ops:
  22.9 12.8 %copy-start.2 = (s32[8]{0:T(128)S(1)}, s32[8]{0:T(128)}, u32[]{:S(2)}) copy-start(s32[8]{0:T(128)} %counts_ref.7) | copy-start | bytes 100
  22.9 4.9 %collective-permute-start = (f32[512,128]{1,0:T(8,128)S(1)}, f32[512,128]{1,0:T(8,128)S(1)}, u32[]{:S(2)}, u32[]{:S(2)}) collective-permute-start(f32[512,128]{1,0:T(8,128)S(1)} %bitcast.5), channel_id=1, source_target_pairs={{0,32},{32,0},{1,33},{33,1},{2,34},{34,2},{3,35},{35,3},{4,36},{36... | collective-permute-start | bytes 786440 | tf_op jit(solution)/shard_map/ppermute | solution.py:387
  28.8 3.9 %collective-permute-start.3 = (f32[16,128]{1,0:T(8,128)S(1)}, f32[16,128]{1,0:T(8,128)S(1)}, u32[]{:S(2)}, u32[]{:S(2)}) collective-permute-start(f32[16,128]{1,0:T(8,128)S(1)} %extract.1.own_ref), channel_id=1, source_target_pairs={{0,24},{8,0},{16,8},{24,16},{1,25},{9,1},{17,9},{25,17},{2,26},{10... | collective-permute-start | bytes 24584 | tf_op jit(solution)/shard_map/ppermute | solution.py:377
  31.6 4.0 %collective-permute-start.2 = (f32[16,128]{1,0:T(8,128)S(1)}, f32[16,128]{1,0:T(8,128)S(1)}, u32[]{:S(2)}, u32[]{:S(2)}) collective-permute-start(f32[16,128]{1,0:T(8,128)S(1)} %extract.1.own_ref), channel_id=1, source_target_pairs={{0,16},{8,24},{16,0},{24,8},{1,17},{9,25},{17,1},{25,9},{2,18},{10... | collective-permute-start | bytes 24584 | tf_op jit(solution)/shard_map/ppermute | solution.py:377
  32.0 3.7 %collective-permute-start.1 = (f32[16,128]{1,0:T(8,128)S(1)}, f32[16,128]{1,0:T(8,128)S(1)}, u32[]{:S(2)}, u32[]{:S(2)}) collective-permute-start(f32[16,128]{1,0:T(8,128)S(1)} %extract.1.own_ref), channel_id=1, source_target_pairs={{0,8},{8,16},{16,24},{24,0},{1,9},{9,17},{17,25},{25,1},{2,10},{10... | collective-permute-start | bytes 24584 | tf_op jit(solution)/shard_map/ppermute | solution.py:377
  45.8 2.6 %collective-permute-start.6 = (f32[16,128]{1,0:T(8,128)S(1)}, f32[16,128]{1,0:T(8,128)S(1)}, u32[]{:S(2)}, u32[]{:S(2)}) collective-permute-start(f32[16,128]{1,0:T(8,128)S(1)} %pairs.1.own_ref), channel_id=1, source_target_pairs={{0,24},{8,0},{16,8},{24,16},{1,25},{9,1},{17,9},{25,17},{2,26},{10... | collective-permute-start | bytes 24584 | tf_op jit(solution)/shard_map/ppermute | solution.py:377
  46.5 4.0 %collective-permute-start.5 = (f32[16,128]{1,0:T(8,128)S(1)}, f32[16,128]{1,0:T(8,128)S(1)}, u32[]{:S(2)}, u32[]{:S(2)}) collective-permute-start(f32[16,128]{1,0:T(8,128)S(1)} %pairs.1.own_ref), channel_id=1, source_target_pairs={{0,16},{8,24},{16,0},{24,8},{1,17},{9,25},{17,1},{25,9},{2,18},{10... | collective-permute-start | bytes 24584 | tf_op jit(solution)/shard_map/ppermute | solution.py:377
  47.7 3.7 %collective-permute-start.4 = (f32[16,128]{1,0:T(8,128)S(1)}, f32[16,128]{1,0:T(8,128)S(1)}, u32[]{:S(2)}, u32[]{:S(2)}) collective-permute-start(f32[16,128]{1,0:T(8,128)S(1)} %pairs.1.own_ref), channel_id=1, source_target_pairs={{0,8},{8,16},{16,24},{24,0},{1,9},{9,17},{17,25},{25,1},{2,10},{10... | collective-permute-start | bytes 24584 | tf_op jit(solution)/shard_map/ppermute | solution.py:377
  52.1 4.3 %copy-start = (f32[12,2048]{1,0:T(8,128)S(1)}, f32[12,2048]{1,0:T(8,128)}, u32[]{:S(2)}) copy-start(f32[12,2048]{1,0:T(8,128)} %state_ref.5) | copy-start | bytes 294916
  52.1 4.3 %copy-start.1 = (f32[2048]{0:T(1024)S(1)}, f32[2048]{0:T(1024)}, u32[]{:S(2)}) copy-start(f32[2048]{0:T(1024)} %param.7) | copy-start | bytes 24580
  52.1 14.0 %all-to-all-start.1 = ((f32[32,16,128]{2,1,0:T(8,128)}), f32[32,16,128]{2,1,0:T(8,128)S(1)}, u32[]{:S(2)}, u32[]{:S(2)}) async-start(f32[32,16,128]{2,1,0:T(8,128)} %combine.1), calls=%async_computation.1 | async-start | bytes 524288 | tf_op jit(solution)/shard_map/all_to_all | solution.py:385
  66.1 5.9 %collective-permute-start.7 = (f32[512,128]{1,0:T(8,128)S(1)}, f32[512,128]{1,0:T(8,128)S(1)}, u32[]{:S(2)}, u32[]{:S(2)}) collective-permute-start(f32[512,128]{1,0:T(8,128)S(1)} %bitcast.9), channel_id=1, source_target_pairs={{0,32},{32,0},{1,33},{33,1},{2,34},{34,2},{3,35},{35,3},{4,36},{36... | collective-permute-start | bytes 786440 | tf_op jit(solution)/shard_map/ppermute | solution.py:387

commit v5 on v4

--- a/solution.py
+++ b/solution.py
@@ -1,3 +1,5 @@
+import functools
+
 import jax
 import jax.numpy as jnp
 from jax import lax
@@ -69,7 +71,7 @@
     offsets, live = list_offsets(counts_ref)
     size = group_size(live)
     core = lax.axis_index("c")
-    group = core * 32 + lax.axis_index("x") * 8 + lax.axis_index("z")
+    group = core * 32 + lax.axis_index("z") * 4 + lax.axis_index("x")
     my_y = lax.axis_index("y")
     halves = (mine_ref, other_ref)
     sub = lax.broadcasted_iota(I32, (8, LANES), 0)
@@ -86,7 +88,7 @@
             which = jnp.where(after, i, which)
             base = jnp.where(after, offsets[i], base)
         slot = jnp.where(valid, position - base, 0)
-        block = ((which & 1) ^ core) * 64 + (which >> 1) * 16 + (slot >> 7)
+        block = ((which & 1) ^ core) * 64 + (slot >> 8) * 8 + (which >> 1) * 2 + ((slot >> 7) & 1)
         within = slot & 127
         found = jnp.zeros((8, LANES), F32)
         for v in range(16):
@@ -94,7 +96,7 @@
             found = jnp.where(block == v * 8 + sub, take(tile, within), found)
         star = jnp.broadcast_to(jnp.sum(found, axis=0, keepdims=True), (8, LANES)).astype(I32)
         mine = valid & ((star >> 14) == my_y)
-        place = (((star >> 8) & 1) ^ core) * 64 + ((star >> 9) & 3) * 16 + ((star >> 11) & 7) * 2 + ((star >> 7) & 1)
+        place = (((star >> 8) & 1) ^ core) * 64 + ((star >> 11) & 7) * 8 + ((star >> 9) & 3) * 2 + ((star >> 7) & 1)
         place = jnp.where(mine, place, -1)
         inside = star & 127
         picked = jnp.zeros((8, LANES), F32)
@@ -113,7 +115,7 @@
 
 def plan_kernel(
     counts_ref, mine_ref, other_ref, state_ref, elapsed_ref,
-    number_ref, rank_ref, block_ref, lane_ref, known_ref, one_ref, two_ref,
+    number_ref, first_ref, rank_ref, block_ref, lane_ref, slot_block_ref, slot_lane_ref, known_ref, one_ref, two_ref,
 ):
     offsets, live = list_offsets(counts_ref)
     size = group_size(live)
@@ -125,18 +127,31 @@
     square_row = lax.broadcasted_iota(I32, (LANES, LANES), 0)
     square_column = lax.broadcasted_iota(I32, (LANES, LANES), 1)
     contract = (((1,), (1,)), ((), ()))
+
+    my_list = lax.axis_index("x") * 2 + lax.axis_index("c")
+    start = at_list(offsets, my_list)
+    slots = lax.broadcasted_iota(I32, (16, LANES), 0) * LANES + lax.broadcasted_iota(I32, (16, LANES), 1)
+    block, lane = split_position(start + slots, size)
+    slot_block_ref[...] = jnp.where(slots < counts_ref[my_list], block, -1)
+    slot_lane_ref[...] = lane
+    for b in range(CAP // LANES):
+        first_ref[b] = lax.div(start + b * LANES, size)
+    first_ref[CAP // LANES] = lax.div(jnp.int32(LANES - 1), size) + 2
+
     total = jnp.zeros((32, LANES), F32)
     for n in range(LISTS):
         i = (n & 6) + ((n & 1) ^ lax.axis_index("c"))
         count = counts_ref[i]
         start = at_list(offsets, i)
         half_ref = other_ref if n & 1 else mine_ref
-        first = 7 + 64 * (n & 6)
+        first = 7 + 8 * (n & 6)
 
         def step(turn, acc):
-            ids8 = half_ref[pl.ds(first + 64 * turn, 8, stride=8), :].astype(I32)
+            even, odd = [
+                half_ref[pl.ds(first + 8 * k + 256 * turn, 4, stride=64), :].astype(I32) for k in range(2)
+            ]
             for k in range(0, 8, 2):
-                ids = jnp.concatenate([ids8[k : k + 1], ids8[k + 1 : k + 2]], axis=1)
+                ids = jnp.concatenate([even[k // 2 : k // 2 + 1], odd[k // 2 : k // 2 + 1]], axis=1)
                 slot = turn * 1024 + k * LANES + column
                 mine = (slot < count) & ((ids >> 11) == shard)
                 high = jnp.where(mine, (ids >> 7) & 15, -1)
@@ -211,7 +226,7 @@
         two_ref[begin, :] = jnp.concatenate([wide3(twelfth * half), wide3(twelfth), none], axis=0)
         return carry
 
-    lax.fori_loop(0, (number + 127) >> 7, compact, 0)
+    lax.fori_loop(0, ((number + 255) >> 8) * 2, compact, 0)
 
 
 def pair_kernel(
@@ -298,79 +313,86 @@
         one_half(1)
 
 
-def combine_kernel(own_ref, one_ref, two_ref, three_ref, out_ref):
+def combine_kernel(own_ref, one_ref, two_ref, three_ref, out_ref, rest_ref):
     force = own_ref[...] + one_ref[...] + two_ref[...] + three_ref[...]
     for peer in range(32):
-        out_ref[peer] = force
+        out_ref[peer] = force[0:8]
+    rest_ref[...] = force[8:16]
 
 
 def finish_kernel(
-    counts_ref, number_ref, rank_ref, block_ref, lane_ref, known_ref, one_ref, two_ref,
-    mine_ref, other_ref, state_ref, new_ref, active_ref,
+    half, number_ref, first_ref, rank_ref, block_ref, lane_ref, slot_block_ref, slot_lane_ref, known_ref, one_ref, two_ref,
+    mine_ref, other_ref, state_ref, *refs,
 ):
-    offsets, live = list_offsets(counts_ref)
-    size = group_size(live)
-    full = jnp.where(size > LANES, 1, 0)
+    new_ref, active_ref = refs[-2:]
     core = lax.axis_index("c")
-    my_list = lax.axis_index("x") * 2 + core
-    count = counts_ref[my_list]
-    start = at_list(offsets, my_list)
     zero = jnp.zeros((8, LANES), F32)
-    row = lax.broadcasted_iota(I32, (8, LANES), 1)
-
-    blocks, lanes, firsts = [], [], []
-    for b in range(CAP // LANES):
-        slot = row + b * LANES
-        block, lane = split_position(start + slot, size)
-        blocks.append(jnp.where(slot < count, block, -1))
-        lanes.append(lane)
-        firsts.append(lax.div(start + b * LANES, size))
+
+    def wide(row):
+        return jnp.broadcast_to(row, (8, LANES))
+
+    def group_of(block):
+        return jnp.where((block & 1) == half, block >> 1, -1)
+
+    wanted = [group_of(wide(slot_block_ref[b : b + 1, :])) for b in range(CAP // LANES)]
+    lanes = [wide(slot_lane_ref[b : b + 1, :]) for b in range(CAP // LANES)]
+    firsts = [first_ref[b] for b in range(CAP // LANES)]
 
     def span(turn, acc):
         acc = list(acc)
         for b in range(CAP // LANES):
-            tile = jnp.minimum(firsts[b] + (turn >> full), GROUPS - 1) * 2 + (turn & full)
-            rows = pl.ds(pl.multiple_of((tile & 63) * 8, 8), 8)
-            forces = jnp.where((tile >> 6) == core, mine_ref[rows, :], other_ref[rows, :])
-            acc[b] = jnp.where(blocks[b] == tile, take(forces, lanes[b]), acc[b])
+            group = jnp.minimum(firsts[b] + turn, GROUPS - 1)
+            rows = pl.ds(pl.multiple_of((group & 31) * 8, 8), 8)
+            forces = jnp.where((group >> 5) == core, mine_ref[rows, :], other_ref[rows, :])
+            acc[b] = jnp.where(wanted[b] == group, take(forces, lanes[b]), acc[b])
         return tuple(acc)
 
-    spans = lax.div(jnp.int32(LANES - 1), size) + 2
-    found = lax.fori_loop(0, spans << full, span, (zero,) * (CAP // LANES))
+    found = lax.fori_loop(0, first_ref[CAP // LANES], span, (zero,) * (CAP // LANES))
     for b in range(CAP // LANES):
-        active_ref[:, b * LANES : (b + 1) * LANES] = found[b][0:6]
+        part = slice(b * LANES, (b + 1) * LANES)
+        if half == 0:
+            active_ref[:, part] = found[b][0:6]
+        else:
+            active_ref[:, part] = jnp.where(wanted[b][0:6] >= 0, found[b][0:6], refs[0][:, part])
 
     new_ref[...] = state_ref[...]
     none = jnp.zeros((2, LANES), F32)
 
-    def compact(turn, carry):
-        block = jnp.broadcast_to(block_ref[pl.ds(turn, 1), :], (8, LANES)) ^ (core * 64)
-        lane = jnp.broadcast_to(lane_ref[pl.ds(turn, 1), :], (8, LANES))
-
-        def half(h, force):
-            for g in range(GROUPS):
-                half_ref = mine_ref if g < 32 else other_ref
-                tile = half_ref[pl.ds(pl.multiple_of((g & 31) * 16 + h * 8, 8), 8), :]
-                force = jnp.where(block == g * 2 + h, take(tile, lane), force)
-            return force
-
-        force = lax.fori_loop(0, 1 + full, half, zero)
+    def moved(turn):
+        group = group_of(wide(block_ref[pl.ds(turn, 1), :]))
+        lane = wide(lane_ref[pl.ds(turn, 1), :])
+        seen = group ^ (core * 32)
+        force = zero
+        for g in range(GROUPS):
+            half_ref = mine_ref if g < 32 else other_ref
+            force = jnp.where(seen == g, take(half_ref[(g & 31) * 8 : (g & 31) * 8 + 8, :], lane), force)
         begin = pl.ds(pl.multiple_of(turn * 8, 8), 8)
         accel = jnp.concatenate([force[0:3], force[0:3], none], axis=0)
         jerk = jnp.concatenate([force[3:6], force[3:6], none], axis=0)
-        moved = known_ref[begin, :] + accel * one_ref[begin, :] - jerk * two_ref[begin, :]
-        head = jnp.concatenate([moved[0:6], force[0:2]], axis=0)
-        tail = jnp.concatenate([force[2:6], none, none], axis=0)
+        place = known_ref[begin, :] + accel * one_ref[begin, :] - jerk * two_ref[begin, :]
+        head = jnp.concatenate([place[0:6], force[0:2]], axis=0)
+        flag = jnp.where(group[0:4] >= 0, 1.0, 0.0)
+        return head, jnp.concatenate([force[2:6], flag], axis=0)
+
+    def compact(turn, carry):
+        tiles = [moved(turn * 2), moved(turn * 2 + 1)]
         for r in range(16):
             part = slice(r * LANES, (r + 1) * LANES)
-            rank = jnp.broadcast_to(rank_ref[r : r + 1, :], (8, LANES))
-            here = (rank >> 7) == turn
+            rank = wide(rank_ref[r : r + 1, :])
             place = rank & 127
-            new_ref[0:8, part] = jnp.where(here, take(head, place), new_ref[0:8, part])
-            new_ref[8:12, part] = jnp.where(here[0:4], take(tail, place)[0:4], new_ref[8:12, part])
+            top, bottom = new_ref[0:8, part], new_ref[8:12, part]
+            for k, (head, tail) in enumerate(tiles):
+                got = take(tail, place)
+                here = (rank >> 7) == turn * 2 + k
+                if half == 1:
+                    here = here & (wide(got[7:8]) > 0.5)
+                top = jnp.where(here, take(head, place), top)
+                bottom = jnp.where(here[0:4], got[0:4], bottom)
+            new_ref[0:8, part] = top
+            new_ref[8:12, part] = bottom
         return carry
 
-    lax.fori_loop(0, (number_ref[0] + 127) >> 7, compact, 0)
+    lax.fori_loop(0, (number_ref[0] + 255) >> 8, compact, 0)
 
 
 def exchange_y(part):
@@ -382,9 +404,22 @@
 
 
 def spread(part, *done):
-    part = lax.all_to_all(part, ("x", "z"), 0, 0).reshape(512, LANES)
+    part = lax.all_to_all(part, ("z", "x"), 0, 0).reshape(-1, LANES)
     part, *done = lax.optimization_barrier((part, *done))
     return in_vmem(part, lax.ppermute(part, "c", [(0, 1), (1, 0)])), done
+
+
+def finish(half, plan, forces, state, *rest):
+    return pl.pallas_call(
+        functools.partial(finish_kernel, half),
+        out_shape=[
+            jax.ShapeDtypeStruct((12, SHARD), F32),
+            jax.ShapeDtypeStruct((6, CAP), F32),
+        ],
+        in_specs=[SMEM] * 2 + [VMEM] * (11 + len(rest)),
+        out_specs=[VMEM, VMEM],
+        name="finish",
+    )(*plan[:2], *in_vmem(*plan[2:]), *forces, *in_vmem(state, *rest))
 
 
 def body(state, mass, elapsed, active_ids, active_count):
@@ -410,11 +445,11 @@
     square = pltpu.VMEM((LANES, LANES), F32)
     plan = pl.pallas_call(
         plan_kernel,
-        out_shape=[jax.ShapeDtypeStruct((1,), I32)]
-        + [pltpu.VMEM((16, LANES), I32)] * 3
+        out_shape=[jax.ShapeDtypeStruct((1,), I32), jax.ShapeDtypeStruct((CAP // LANES + 1,), I32)]
+        + [pltpu.VMEM((16, LANES), I32)] * 5
         + [square] * 3,
         in_specs=[SMEM] + [VMEM] * 4,
-        out_specs=[SMEM] + [VMEM] * 6,
+        out_specs=[SMEM] * 2 + [VMEM] * 8,
         name="plan",
     )(active_count, *slab, *in_vmem(state, elapsed))
     partial = pl.pallas_call(
@@ -430,24 +465,23 @@
         compiler_params=pltpu.CompilerParams(vmem_limit_bytes=24 * 2**20),
         name="pairs",
     )(active_count, *in_vmem(own, *others), *slab)
-    combined = pl.pallas_call(
+    combined, rest = pl.pallas_call(
         combine_kernel,
-        out_shape=pltpu.VMEM((32, 16, LANES), F32),
+        out_shape=[pltpu.VMEM((32, 8, LANES), F32), jax.ShapeDtypeStruct((8, LANES), F32)],
         in_specs=[VMEM] * 4,
-        out_specs=VMEM,
+        out_specs=[VMEM] * 2,
         name="combine",
     )(*in_vmem(partial, *exchange_y(partial)))
-    forces, plan = spread(combined, *plan)
-    return pl.pallas_call(
-        finish_kernel,
-        out_shape=[
-            jax.ShapeDtypeStruct((12, SHARD), F32),
-            jax.ShapeDtypeStruct((6, CAP), F32),
-        ],
-        in_specs=[SMEM] * 2 + [VMEM] * 9,
-        out_specs=[VMEM, VMEM],
-        name="finish",
-    )(active_count, plan[0], *in_vmem(*plan[1:]), *forces, *in_vmem(state))
+    turns = (group_size(jnp.sum(active_count)) > LANES).astype(I32)
+    forces, (turns, *plan) = spread(combined, turns, *plan)
+    outputs = finish(0, plan, forces, state)
+
+    def more(carry):
+        turn, new_state, active_force = carry
+        forces, _ = spread(jnp.broadcast_to(rest[None], (32, 8, LANES)))
+        return (turn + 1, *finish(1, plan, forces, new_state, active_force))
+
+    return lax.while_loop(lambda carry: carry[0] < turns, more, (jnp.int32(0), *outputs))[1:]
 
 
 def solution(mesh):

time: 74.8 us -> 73.5 us (0.983); the launches traced: 75 us -> 72.9 us
  waiting for transfers between devices: 13.6 us -> 11.4 us
  Pallas kernels: 20.2 us -> 18.2 us
  starting transfers between devices: 19.2 us -> 17.6 us
  blocking collectives: 21.4 us -> 22.9 us
    all_to_all x1, waiting for transfers between devices: 5.29 us -> 3.27 us  [spread(): part = lax.all_to_all(part, ('z', 'x'), 0, 0).reshape(-1, LANES)]
    all_to_all x1, blocking collectives: 21.4 us -> 22.9 us  [spread(): part = lax.all_to_all(part, ('z', 'x'), 0, 0).reshape(-1, LANES)]
    ppermute x2, starting transfers between devices: 8.5 us -> 7.14 us  [spread(): return (in_vmem(part, lax.ppermute(part, 'c', [(0, 1), (1, 0)])), done)]
    pallas_call x1, Pallas kernels: 10.1 us -> 9.03 us  [body(): pl.pallas_call(pair_kernel, out_shape=pltpu.VMEM((16, LANES), F32), in_sp...]
    pallas_call x3, Pallas kernels: 8.14 us -> 7.28 us  [the longest x1 4.58 us: body(): pl.pallas_call(plan_kernel, out_shape=[jax.ShapeDtypeStruct((1,), I32), j...]
  transfers between devices with their start and end apart: 9 -> 9, of which waited for: 7 -> 7; matrix products, arithmetic and copies ran while one was open for 0% -> 1% of each run, Pallas kernels for 6% -> 6%
where the time goes in v5:
time: 73.5 us; the launch traced here: 72.9 us
  blocking collectives  22.9 us (31%)
  Pallas kernels  18.2 us (25%)
  starting transfers between devices  17.6 us (24%)
  waiting for transfers between devices  11.4 us (16%)
  between operations  1.41 us (2%)
    all_to_all x1, blocking collectives, spread(): part = lax.all_to_all(part, ('z', 'x'), 0, 0).reshape(-1, LANES)  22.9 us
    pallas_call x1, Pallas kernels, body(): pl.pallas_call(pair_kernel, out_shape=pltpu.VMEM((16, LANES), F32), in_sp...  9.03 us
    ppermute x2, starting transfers between devices, spread(): return (in_vmem(part, lax.ppermute(part, 'c', [(0, 1), (1, 0)])), done)  7.14 us
    ppermute x6, starting transfers between devices, exchange_y(): lax.ppermute(part, 'y', [(i, (i + k) % 4) for i in range(4)])  6.43 us
    ppermute x6, waiting for transfers between devices, exchange_y(): lax.ppermute(part, 'y', [(i, (i + k) % 4) for i in range(4)])  6 us
    pallas_call x1, Pallas kernels, body(): pl.pallas_call(plan_kernel, out_shape=[jax.ShapeDtypeStruct((1,), I32), j...  4.58 us
    all_to_all x1, starting transfers between devices, spread(): part = lax.all_to_all(part, ('z', 'x'), 0, 0).reshape(-1, LANES)  3.99 us
    all_to_all x1, waiting for transfers between devices, spread(): part = lax.all_to_all(part, ('z', 'x'), 0, 0).reshape(-1, LANES)  3.27 us
  transfers between devices with their start and end apart: 9, of which 7 were waited for; matrix products, arithmetic and copies ran while one was open for 1% of the time, Pallas kernels for 6%

profile of v5, /device:TPU:1, one launch (start us, length us, event | category | flops | bytes accessed | tf_op | source)
XLA Modules:
  0.0 72.9 jit_solution(8135691195484027595)
XLA Ops:
  0.6 1.0 %pack.1 = f32[32,16,128]{2,1,0:T(8,128)S(1)} custom-call(f32[12,2048]{1,0:T(8,128)} %state_ref.5, f32[1,2048]{1,0:T(1,128)} %bitcast.18, f32[1,2048]{1,0:T(1,128)} %bitcast.16, s32[1,2048]{1,0:T(1,128)} %bitcast.19), custom_call_target="tpu_custom_call" | custom-call | tf_op jit(solution)/shard_map/pack/pallas_call | solution.py:429
  1.6 22.9 %all_to_all.16 = f32[32,16,128]{2,1,0:T(8,128)S(1)} all-to-all(f32[32,16,128]{2,1,0:T(8,128)S(1)} %pack.1), channel_id=1, replica_groups=mesh['x'=4,'c'=2,'y'=4,'z'=8] {'z','x'}, dimensions={0} | all-to-all | bytes 524288 | tf_op jit(solution)/shard_map/all_to_all | solution.py:407
  24.4 0.0 copy-start.2
  24.4 2.5 %collective-permute-start.1 = (f32[512,128]{1,0:T(8,128)S(1)}, f32[512,128]{1,0:T(8,128)S(1)}, u32[]{:S(2)}, u32[]{:S(2)}) collective-permute-start(f32[512,128]{1,0:T(8,128)S(1)} %bitcast.10), channel_id=1, source_target_pairs={{0,32},{32,0},{1,33},{33,1},{2,34},{34,2},{3,35},{35,3},{4,36},{36... | collective-permute-start | bytes 786440 | tf_op jit(solution)/shard_map/ppermute | solution.py:409
  26.9 1.2 %collective-permute-done.1.other_ref = f32[512,128]{1,0:T(8,128)S(1)} collective-permute-done((f32[512,128]{1,0:T(8,128)S(1)}, f32[512,128]{1,0:T(8,128)S(1)}, u32[]{:S(2)}, u32[]{:S(2)}) %collective-permute-start.1) | collective-permute-done | bytes 262176 | tf_op jit(solution)/shard_map/ppermute | solution.py:409
  28.1 1.0 %extract.1.own_ref = f32[16,128]{1,0:T(8,128)S(1)} custom-call(s32[8]{0:T(128)} %counts_ref.5, f32[512,128]{1,0:T(8,128)S(1)} %bitcast.11, f32[512,128]{1,0:T(8,128)S(1)} %collective-permute-done.1.other_ref), custom_call_target="tpu_custom_call" | custom-call | tf_op jit(solution)/shard_map/extract/pallas_call | solution.py:437
  29.1 2.8 %collective-permute-start.4 = (f32[16,128]{1,0:T(8,128)S(1)}, f32[16,128]{1,0:T(8,128)S(1)}, u32[]{:S(2)}, u32[]{:S(2)}) collective-permute-start(f32[16,128]{1,0:T(8,128)S(1)} %extract.1.own_ref), channel_id=1, source_target_pairs={{0,24},{8,0},{16,8},{24,16},{1,25},{9,1},{17,9},{25,17},{2,26},{10... | collective-permute-start | bytes 24584 | tf_op jit(solution)/shard_map/ppermute | solution.py:399
  31.9 0.3 collective-permute-start.3
  32.2 0.7 collective-permute-start.2
  32.9 0.0 collective-permute-done.4.three_ref
  32.9 3.0 %collective-permute-done.3.two_ref = f32[16,128]{1,0:T(8,128)S(1)} collective-permute-done((f32[16,128]{1,0:T(8,128)S(1)}, f32[16,128]{1,0:T(8,128)S(1)}, u32[]{:S(2)}, u32[]{:S(2)}) %collective-permute-start.3) | collective-permute-done | bytes 8224 | tf_op jit(solution)/shard_map/ppermute | solution.py:399
  35.9 0.1 collective-permute-done.2.one_ref
  36.0 0.0 copy-done.2
  36.0 9.0 %pairs.1.own_ref = f32[16,128]{1,0:T(8,128)S(1)} custom-call(s32[8]{0:T(128)S(1)} %copy-done.2, f32[16,128]{1,0:T(8,128)S(1)} %extract.1.own_ref, f32[16,128]{1,0:T(8,128)S(1)} %collective-permute-done.2.one_ref, f32[16,128]{1,0:T(8,128)S(1)} %collective-permute-done.3.two_ref, f32[16,128]{1,0:T(8,128)S(1)} %collective-permute-done.4.three_ref, ...), custom_call_target="tpu_custom_call" | custom-call | tf_op jit(solution)/shard_map/pairs/pallas_call | solution.py:455
  45.0 0.6 collective-permute-start.7
  45.6 1.2 %collective-permute-start.6 = (f32[16,128]{1,0:T(8,128)S(1)}, f32[16,128]{1,0:T(8,128)S(1)}, u32[]{:S(2)}, u32[]{:S(2)}) collective-permute-start(f32[16,128]{1,0:T(8,128)S(1)} %pairs.1.own_ref), channel_id=1, source_target_pairs={{0,16},{8,24},{16,0},{24,8},{1,17},{9,25},{17,1},{25,9},{2,18},{10... | collective-permute-start | bytes 24584 | tf_op jit(solution)/shard_map/ppermute | solution.py:399
  46.8 0.8 %collective-permute-start.5 = (f32[16,128]{1,0:T(8,128)S(1)}, f32[16,128]{1,0:T(8,128)S(1)}, u32[]{:S(2)}, u32[]{:S(2)}) collective-permute-start(f32[16,128]{1,0:T(8,128)S(1)} %pairs.1.own_ref), channel_id=1, source_target_pairs={{0,8},{8,16},{16,24},{24,0},{1,9},{9,17},{17,25},{25,1},{2,10},{10... | collective-permute-start | bytes 24584 | tf_op jit(solution)/shard_map/ppermute | solution.py:399
  47.6 0.0 collective-permute-done.7.three_ref
  47.6 2.0 %collective-permute-done.6.two_ref = f32[16,128]{1,0:T(8,128)S(1)} collective-permute-done((f32[16,128]{1,0:T(8,128)S(1)}, f32[16,128]{1,0:T(8,128)S(1)}, u32[]{:S(2)}, u32[]{:S(2)}) %collective-permute-start.6) | collective-permute-done | bytes 8224 | tf_op jit(solution)/shard_map/ppermute | solution.py:399
  49.6 0.9 %collective-permute-done.5.one_ref = f32[16,128]{1,0:T(8,128)S(1)} collective-permute-done((f32[16,128]{1,0:T(8,128)S(1)}, f32[16,128]{1,0:T(8,128)S(1)}, u32[]{:S(2)}, u32[]{:S(2)}) %collective-permute-start.5) | collective-permute-done | bytes 8224 | tf_op jit(solution)/shard_map/ppermute | solution.py:399
  50.5 0.7 combine.1
  51.2 0.0 copy-start
  51.2 4.0 %all-to-all-start.2 = ((f32[32,8,128]{2,1,0:T(8,128)}), f32[32,8,128]{2,1,0:T(8,128)S(1)}, u32[]{:S(2)}, u32[]{:S(2)}) async-start(f32[32,8,128]{2,1,0:T(8,128)} %get-tuple-element.109), calls=%async_computation.2 | async-start | bytes 262144 | tf_op jit(solution)/shard_map/all_to_all | solution.py:407
  55.2 0.0 copy-start.1
  55.2 0.7 reduce_sum.9
  56.6 0.0 copy-done
  56.6 0.0 copy-done.1
  56.6 4.6 %plan.1 = (s32[1]{0:T(128)}, s32[17]{0:T(128)S(1)}, s32[16,128]{1,0:T(8,128)S(1)}, s32[16,128]{1,0:T(8,128)S(1)}, s32[16,128]{1,0:T(8,128)S(1)}, /*index=5*/s32[...) custom-call(s32[8]{0:T(128)} %counts_ref.5, ...), custom_call_target="tpu_custom_call" | custom-call | tf_op jit(solution)/shard_map/plan/pallas_call | solution.py:446
  61.2 3.3 %all-to-all-done.2 = f32[32,8,128]{2,1,0:T(8,128)S(1)} async-done(((f32[32,8,128]{2,1,0:T(8,128)}), f32[32,8,128]{2,1,0:T(8,128)S(1)}, u32[]{:S(2)}, u32[]{:S(2)}) %all-to-all-start.2) | async-done | bytes 131104 | tf_op jit(solution)/shard_map/all_to_all | solution.py:407
  64.5 4.7 %collective-permute-start.8 = (f32[256,128]{1,0:T(8,128)S(1)}, f32[256,128]{1,0:T(8,128)S(1)}, u32[]{:S(2)}, u32[]{:S(2)}) collective-permute-start(f32[256,128]{1,0:T(8,128)S(1)} %bitcast.14), channel_id=1, source_target_pairs={{0,32},{32,0},{1,33},{33,1},{2,34},{34,2},{3,35},{35,3},{4,36},{36... | collective-permute-start | bytes 393224 | tf_op jit(solution)/shard_map/ppermute | solution.py:409
  69.2 1.0 %collective-permute-done.8.other_ref = f32[256,128]{1,0:T(8,128)S(1)} collective-permute-done((f32[256,128]{1,0:T(8,128)S(1)}, f32[256,128]{1,0:T(8,128)S(1)}, u32[]{:S(2)}, u32[]{:S(2)}) %collective-permute-start.8) | collective-permute-done | bytes 131104 | tf_op jit(solution)/shard_map/ppermute | solution.py:409
  70.2 2.0 %finish.2 = (f32[12,2048]{1,0:T(8,128)S(1)}, f32[6,2048]{1,0:T(8,128)S(1)}) custom-call(s32[1]{0:T(128)} %get-tuple-element.268.number_ref, s32[17]{0:T(128)S(1)} %get-tuple-element.269.first_ref, s32[16,128]{1,0:T(8,128)S(1)} %get-tuple-element.270.rank_ref, s32[16,128]{1,0:T(8,128)S(1)} %get-tuple-element.271.block_ref, ...), custom_call_target="tpu_custom_call" | custom-call | tf_op jit(solution)/shard_map/finish/pallas_call | solution.py:413
  72.2 0.0 copy-start.3
  72.2 0.0 copy-start.4
  72.2 0.6 copy-done.3
  72.9 0.0 copy-done.4
  (1 shorter events, 0.0 us)
Async XLA Ops:
  24.4 11.5 %copy-start.2 = (s32[8]{0:T(128)S(1)}, s32[8]{0:T(128)}, u32[]{:S(2)}) copy-start(s32[8]{0:T(128)} %counts_ref.5) | copy-start | bytes 100
  24.4 3.6 %collective-permute-start.1 = (f32[512,128]{1,0:T(8,128)S(1)}, f32[512,128]{1,0:T(8,128)S(1)}, u32[]{:S(2)}, u32[]{:S(2)}) collective-permute-start(f32[512,128]{1,0:T(8,128)S(1)} %bitcast.10), channel_id=1, source_target_pairs={{0,32},{32,0},{1,33},{33,1},{2,34},{34,2},{3,35},{35,3},{4,36},{36... | collective-permute-start | bytes 786440 | tf_op jit(solution)/shard_map/ppermute | solution.py:409
  29.1 3.9 %collective-permute-start.4 = (f32[16,128]{1,0:T(8,128)S(1)}, f32[16,128]{1,0:T(8,128)S(1)}, u32[]{:S(2)}, u32[]{:S(2)}) collective-permute-start(f32[16,128]{1,0:T(8,128)S(1)} %extract.1.own_ref), channel_id=1, source_target_pairs={{0,24},{8,0},{16,8},{24,16},{1,25},{9,1},{17,9},{25,17},{2,26},{10... | collective-permute-start | bytes 24584 | tf_op jit(solution)/shard_map/ppermute | solution.py:399
  31.9 4.0 %collective-permute-start.3 = (f32[16,128]{1,0:T(8,128)S(1)}, f32[16,128]{1,0:T(8,128)S(1)}, u32[]{:S(2)}, u32[]{:S(2)}) collective-permute-start(f32[16,128]{1,0:T(8,128)S(1)} %extract.1.own_ref), channel_id=1, source_target_pairs={{0,16},{8,24},{16,0},{24,8},{1,17},{9,25},{17,1},{25,9},{2,18},{10... | collective-permute-start | bytes 24584 | tf_op jit(solution)/shard_map/ppermute | solution.py:399
  32.2 3.7 %collective-permute-start.2 = (f32[16,128]{1,0:T(8,128)S(1)}, f32[16,128]{1,0:T(8,128)S(1)}, u32[]{:S(2)}, u32[]{:S(2)}) collective-permute-start(f32[16,128]{1,0:T(8,128)S(1)} %extract.1.own_ref), channel_id=1, source_target_pairs={{0,8},{8,16},{16,24},{24,0},{1,9},{9,17},{17,25},{25,1},{2,10},{10... | collective-permute-start | bytes 24584 | tf_op jit(solution)/shard_map/ppermute | solution.py:399
  45.0 2.6 %collective-permute-start.7 = (f32[16,128]{1,0:T(8,128)S(1)}, f32[16,128]{1,0:T(8,128)S(1)}, u32[]{:S(2)}, u32[]{:S(2)}) collective-permute-start(f32[16,128]{1,0:T(8,128)S(1)} %pairs.1.own_ref), channel_id=1, source_target_pairs={{0,24},{8,0},{16,8},{24,16},{1,25},{9,1},{17,9},{25,17},{2,26},{10... | collective-permute-start | bytes 24584 | tf_op jit(solution)/shard_map/ppermute | solution.py:399
  45.6 4.0 %collective-permute-start.6 = (f32[16,128]{1,0:T(8,128)S(1)}, f32[16,128]{1,0:T(8,128)S(1)}, u32[]{:S(2)}, u32[]{:S(2)}) collective-permute-start(f32[16,128]{1,0:T(8,128)S(1)} %pairs.1.own_ref), channel_id=1, source_target_pairs={{0,16},{8,24},{16,0},{24,8},{1,17},{9,25},{17,1},{25,9},{2,18},{10... | collective-permute-start | bytes 24584 | tf_op jit(solution)/shard_map/ppermute | solution.py:399
  46.8 3.7 %collective-permute-start.5 = (f32[16,128]{1,0:T(8,128)S(1)}, f32[16,128]{1,0:T(8,128)S(1)}, u32[]{:S(2)}, u32[]{:S(2)}) collective-permute-start(f32[16,128]{1,0:T(8,128)S(1)} %pairs.1.own_ref), channel_id=1, source_target_pairs={{0,8},{8,16},{16,24},{24,0},{1,9},{9,17},{17,25},{25,1},{2,10},{10... | collective-permute-start | bytes 24584 | tf_op jit(solution)/shard_map/ppermute | solution.py:399
  51.2 5.4 %copy-start = (f32[12,2048]{1,0:T(8,128)S(1)}, f32[12,2048]{1,0:T(8,128)}, u32[]{:S(2)}) copy-start(f32[12,2048]{1,0:T(8,128)} %state_ref.5) | copy-start | bytes 294916
  51.2 13.3 %all-to-all-start.2 = ((f32[32,8,128]{2,1,0:T(8,128)}), f32[32,8,128]{2,1,0:T(8,128)S(1)}, u32[]{:S(2)}, u32[]{:S(2)}) async-start(f32[32,8,128]{2,1,0:T(8,128)} %get-tuple-element.109), calls=%async_computation.2 | async-start | bytes 262144 | tf_op jit(solution)/shard_map/all_to_all | solution.py:407
  55.2 1.4 %copy-start.1 = (f32[2048]{0:T(1024)S(1)}, f32[2048]{0:T(1024)}, u32[]{:S(2)}) copy-start(f32[2048]{0:T(1024)} %param.9) | copy-start | bytes 24580
  64.5 5.7 %collective-permute-start.8 = (f32[256,128]{1,0:T(8,128)S(1)}, f32[256,128]{1,0:T(8,128)S(1)}, u32[]{:S(2)}, u32[]{:S(2)}) collective-permute-start(f32[256,128]{1,0:T(8,128)S(1)} %bitcast.14), channel_id=1, source_target_pairs={{0,32},{32,0},{1,33},{33,1},{2,34},{34,2},{3,35},{35,3},{4,36},{36... | collective-permute-start | bytes 393224 | tf_op jit(solution)/shard_map/ppermute | solution.py:409
  72.2 0.7 copy-start.3
  72.2 0.7 copy-start.4

commit v6 on v5

--- a/solution.py
+++ b/solution.py
@@ -12,6 +12,7 @@
 softening_square = 0.01
 LISTS = 8
 CAP = 2048
+SHIFT = 5
 SHARD = 2048
 GROUPS = 64
 LANES = 128
@@ -43,10 +44,26 @@
     return lax.shift_right_logical(live + (GROUPS - 1), 6)
 
 
-def split_position(position, size):
-    group = jnp.floor((position.astype(F32) + 0.5) / size.astype(F32)).astype(I32)
-    lane = position - group * size
+def two_sizes(live):
+    size = group_size(live)
+    shift = jnp.minimum(lax.shift_right_logical(size * SHIFT, 5), jnp.maximum(LANES - size, 0))
+    return size - shift, size + shift
+
+
+def split_position(position, sizes):
+    second = position >= 32 * sizes[0]
+    rest = jnp.where(second, position - 32 * sizes[0], position)
+    size = jnp.where(second, sizes[1], sizes[0])
+    group = jnp.floor((rest.astype(F32) + 0.5) / size.astype(F32)).astype(I32)
+    lane = rest - group * size
+    group = jnp.where(second, group + 32, group)
     return group * 2 + (lane >> 7), lane & 127
+
+
+def group_at(position, sizes):
+    second = position >= 32 * sizes[0]
+    rest = jnp.where(second, position - 32 * sizes[0], position)
+    return lax.div(rest, jnp.where(second, sizes[1], sizes[0])) + jnp.where(second, 32, 0)
 
 
 def pack_kernel(state_ref, mass_ref, elapsed_ref, ids_ref, out_ref):
@@ -69,9 +86,10 @@
 
 def extract_kernel(counts_ref, mine_ref, other_ref, out_ref):
     offsets, live = list_offsets(counts_ref)
-    size = group_size(live)
+    sizes = two_sizes(live)
     core = lax.axis_index("c")
-    group = core * 32 + lax.axis_index("z") * 4 + lax.axis_index("x")
+    size = jnp.where(core == 0, sizes[0], sizes[1])
+    begin = jnp.where(core == 0, 0, 32 * sizes[0]) + (lax.axis_index("z") * 4 + lax.axis_index("x")) * size
     my_y = lax.axis_index("y")
     halves = (mine_ref, other_ref)
     sub = lax.broadcasted_iota(I32, (8, LANES), 0)
@@ -79,7 +97,7 @@
 
     def one_half(half):
         lane = column + half * LANES
-        position = group * size + lane
+        position = begin + lane
         valid = (lane < size) & (position < live)
         which = jnp.zeros((8, LANES), I32)
         base = jnp.zeros((8, LANES), I32)
@@ -118,7 +136,7 @@
     number_ref, first_ref, rank_ref, block_ref, lane_ref, slot_block_ref, slot_lane_ref, known_ref, one_ref, two_ref,
 ):
     offsets, live = list_offsets(counts_ref)
-    size = group_size(live)
+    sizes = two_sizes(live)
     shard = lax.axis_index("y") * 8 + lax.axis_index("z")
     wide = 2 * LANES
     row16 = lax.broadcasted_iota(I32, (16, wide), 0)
@@ -131,12 +149,12 @@
     my_list = lax.axis_index("x") * 2 + lax.axis_index("c")
     start = at_list(offsets, my_list)
     slots = lax.broadcasted_iota(I32, (16, LANES), 0) * LANES + lax.broadcasted_iota(I32, (16, LANES), 1)
-    block, lane = split_position(start + slots, size)
+    block, lane = split_position(start + slots, sizes)
     slot_block_ref[...] = jnp.where(slots < counts_ref[my_list], block, -1)
     slot_lane_ref[...] = lane
     for b in range(CAP // LANES):
-        first_ref[b] = lax.div(start + b * LANES, size)
-    first_ref[CAP // LANES] = lax.div(jnp.int32(LANES - 1), size) + 2
+        first_ref[b] = group_at(start + b * LANES, sizes)
+    first_ref[CAP // LANES] = lax.div(jnp.int32(LANES - 1), sizes[0]) + 2
 
     total = jnp.zeros((32, LANES), F32)
     for n in range(LISTS):
@@ -195,7 +213,7 @@
                 facts.astype(F32).astype(jnp.bfloat16), hit, contract, preferred_element_type=F32
             )
         mark_of = (sums[0:1] * 128.0 + sums[1:2]).astype(I32)
-        block, lane = split_position(mark_of - 1, size)
+        block, lane = split_position(mark_of - 1, sizes)
         block_ref[pl.ds(turn, 1), :] = jnp.where(mark_of > 0, block, -1)
         lane_ref[pl.ds(turn, 1), :] = jnp.where(mark_of > 0, lane, 0)
         star_row = jnp.broadcast_to(sums[2:3], (8, LANES)).astype(I32)
@@ -226,7 +244,7 @@
         two_ref[begin, :] = jnp.concatenate([wide3(twelfth * half), wide3(twelfth), none], axis=0)
         return carry
 
-    lax.fori_loop(0, ((number + 255) >> 8) * 2, compact, 0)
+    lax.fori_loop(0, jnp.maximum(((number + 255) >> 8) * 2, 2), compact, 0)
 
 
 def pair_kernel(
@@ -234,7 +252,7 @@
     splat_ref, source_ref, part_ref,
 ):
     _, live = list_offsets(counts_ref)
-    size = group_size(live)
+    size = jnp.where(lax.axis_index("c") == 0, *two_sizes(live))
     column = lax.broadcasted_iota(I32, (8, LANES), 1)
     zero = jnp.zeros((8, LANES), F32)
     halves = (mine_ref, other_ref)
@@ -347,7 +365,10 @@
             acc[b] = jnp.where(wanted[b] == group, take(forces, lanes[b]), acc[b])
         return tuple(acc)
 
-    found = lax.fori_loop(0, first_ref[CAP // LANES], span, (zero,) * (CAP // LANES))
+    found = (zero,) * (CAP // LANES)
+    for turn in range(3):
+        found = span(jnp.int32(turn), found)
+    found = lax.fori_loop(3, first_ref[CAP // LANES], span, found)
     for b in range(CAP // LANES):
         part = slice(b * LANES, (b + 1) * LANES)
         if half == 0:
@@ -392,7 +413,8 @@
             new_ref[8:12, part] = bottom
         return carry
 
-    lax.fori_loop(0, (number_ref[0] + 255) >> 8, compact, 0)
+    compact(jnp.int32(0), 0)
+    lax.fori_loop(1, (number_ref[0] + 255) >> 8, compact, 0)
 
 
 def exchange_y(part):

time: 73.5 us -> 73.1 us (level)
  starting transfers between devices: 17.6 us -> 15 us
  Pallas kernels: 18.2 us -> 19.5 us
  waiting for transfers between devices: 11.4 us -> 12.2 us
    ppermute x2, starting transfers between devices: 7.14 us -> 4.55 us  [spread(): return (in_vmem(part, lax.ppermute(part, 'c', [(0, 1), (1, 0)])), done)]
    pallas_call x1, Pallas kernels: 9.03 us -> 10.8 us  [body(): pl.pallas_call(pair_kernel, out_shape=pltpu.VMEM((16, LANES), F32), in_sp...]
  transfers between devices with their start and end apart: 9 -> 9, of which waited for: 7 -> 8; matrix products, arithmetic and copies ran while one was open for 1% -> 1% of each run, Pallas kernels for 6% -> 6%
where the time goes in v6:
time: 73.1 us; the launch traced here: 72.3 us
  blocking collectives  22.9 us (31%)
  Pallas kernels  19.5 us (27%)
  starting transfers between devices  15 us (21%)
  waiting for transfers between devices  12.2 us (17%)
  between operations  1.41 us (2%)
    all_to_all x1, blocking collectives, spread(): part = lax.all_to_all(part, ('z', 'x'), 0, 0).reshape(-1, LANES)  22.9 us
    pallas_call x1, Pallas kernels, body(): pl.pallas_call(pair_kernel, out_shape=pltpu.VMEM((16, LANES), F32), in_sp...  10.8 us
    ppermute x6, starting transfers between devices, exchange_y(): lax.ppermute(part, 'y', [(i, (i + k) % 4) for i in range(4)])  6.43 us
    ppermute x6, waiting for transfers between devices, exchange_y(): lax.ppermute(part, 'y', [(i, (i + k) % 4) for i in range(4)])  6.35 us
    ppermute x2, starting transfers between devices, spread(): return (in_vmem(part, lax.ppermute(part, 'c', [(0, 1), (1, 0)])), done)  4.55 us
    pallas_call x1, Pallas kernels, body(): pl.pallas_call(plan_kernel, out_shape=[jax.ShapeDtypeStruct((1,), I32), j...  4.14 us
    all_to_all x1, starting transfers between devices, spread(): part = lax.all_to_all(part, ('z', 'x'), 0, 0).reshape(-1, LANES)  3.99 us
    all_to_all x1, waiting for transfers between devices, spread(): part = lax.all_to_all(part, ('z', 'x'), 0, 0).reshape(-1, LANES)  3.71 us
  transfers between devices with their start and end apart: 9, of which 8 were waited for; matrix products, arithmetic and copies ran while one was open for 1% of the time, Pallas kernels for 6%

profile of v6, /device:TPU:1, one launch (start us, length us, event | category | flops | bytes accessed | tf_op | source)
XLA Modules:
  0.0 72.3 jit_solution(13991501019646587207)
XLA Ops:
  0.6 1.0 %pack.1 = f32[32,16,128]{2,1,0:T(8,128)S(1)} custom-call(f32[12,2048]{1,0:T(8,128)} %state_ref.5, f32[1,2048]{1,0:T(1,128)} %bitcast.18, f32[1,2048]{1,0:T(1,128)} %bitcast.16, s32[1,2048]{1,0:T(1,128)} %bitcast.19), custom_call_target="tpu_custom_call" | custom-call | tf_op jit(solution)/shard_map/pack/pallas_call | solution.py:451
  1.6 22.9 %all_to_all.16 = f32[32,16,128]{2,1,0:T(8,128)S(1)} all-to-all(f32[32,16,128]{2,1,0:T(8,128)S(1)} %pack.1), channel_id=1, replica_groups=mesh['x'=4,'c'=2,'y'=4,'z'=8] {'z','x'}, dimensions={0} | all-to-all | bytes 524288 | tf_op jit(solution)/shard_map/all_to_all | solution.py:429
  24.4 0.0 copy-start.2
  24.4 2.5 %collective-permute-start.1 = (f32[512,128]{1,0:T(8,128)S(1)}, f32[512,128]{1,0:T(8,128)S(1)}, u32[]{:S(2)}, u32[]{:S(2)}) collective-permute-start(f32[512,128]{1,0:T(8,128)S(1)} %bitcast.10), channel_id=1, source_target_pairs={{0,32},{32,0},{1,33},{33,1},{2,34},{34,2},{3,35},{35,3},{4,36},{36... | collective-permute-start | bytes 786440 | tf_op jit(solution)/shard_map/ppermute | solution.py:431
  26.9 1.2 %collective-permute-done.1.other_ref = f32[512,128]{1,0:T(8,128)S(1)} collective-permute-done((f32[512,128]{1,0:T(8,128)S(1)}, f32[512,128]{1,0:T(8,128)S(1)}, u32[]{:S(2)}, u32[]{:S(2)}) %collective-permute-start.1) | collective-permute-done | bytes 262176 | tf_op jit(solution)/shard_map/ppermute | solution.py:431
  28.1 1.0 %extract.1.own_ref = f32[16,128]{1,0:T(8,128)S(1)} custom-call(s32[8]{0:T(128)} %counts_ref.5, f32[512,128]{1,0:T(8,128)S(1)} %bitcast.11, f32[512,128]{1,0:T(8,128)S(1)} %collective-permute-done.1.other_ref), custom_call_target="tpu_custom_call" | custom-call | tf_op jit(solution)/shard_map/extract/pallas_call | solution.py:459
  29.1 2.8 %collective-permute-start.4 = (f32[16,128]{1,0:T(8,128)S(1)}, f32[16,128]{1,0:T(8,128)S(1)}, u32[]{:S(2)}, u32[]{:S(2)}) collective-permute-start(f32[16,128]{1,0:T(8,128)S(1)} %extract.1.own_ref), channel_id=1, source_target_pairs={{0,24},{8,0},{16,8},{24,16},{1,25},{9,1},{17,9},{25,17},{2,26},{10... | collective-permute-start | bytes 24584 | tf_op jit(solution)/shard_map/ppermute | solution.py:421
  31.9 0.3 collective-permute-start.3
  32.2 0.7 collective-permute-start.2
  32.9 0.0 collective-permute-done.4.three_ref
  32.9 3.0 %collective-permute-done.3.two_ref = f32[16,128]{1,0:T(8,128)S(1)} collective-permute-done((f32[16,128]{1,0:T(8,128)S(1)}, f32[16,128]{1,0:T(8,128)S(1)}, u32[]{:S(2)}, u32[]{:S(2)}) %collective-permute-start.3) | collective-permute-done | bytes 8224 | tf_op jit(solution)/shard_map/ppermute | solution.py:421
  35.9 0.1 collective-permute-done.2.one_ref
  36.0 0.0 copy-done.2
  36.0 10.8 %pairs.1.own_ref = f32[16,128]{1,0:T(8,128)S(1)} custom-call(s32[8]{0:T(128)S(1)} %copy-done.2, f32[16,128]{1,0:T(8,128)S(1)} %extract.1.own_ref, f32[16,128]{1,0:T(8,128)S(1)} %collective-permute-done.2.one_ref, f32[16,128]{1,0:T(8,128)S(1)} %collective-permute-done.3.two_ref, f32[16,128]{1,0:T(8,128)S(1)} %collective-permute-done.4.three_ref, ...), custom_call_target="tpu_custom_call" | custom-call | tf_op jit(solution)/shard_map/pairs/pallas_call | solution.py:477
  46.8 0.6 collective-permute-start.7
  47.4 1.2 %collective-permute-start.6 = (f32[16,128]{1,0:T(8,128)S(1)}, f32[16,128]{1,0:T(8,128)S(1)}, u32[]{:S(2)}, u32[]{:S(2)}) collective-permute-start(f32[16,128]{1,0:T(8,128)S(1)} %pairs.1.own_ref), channel_id=1, source_target_pairs={{0,16},{8,24},{16,0},{24,8},{1,17},{9,25},{17,1},{25,9},{2,18},{10... | collective-permute-start | bytes 24584 | tf_op jit(solution)/shard_map/ppermute | solution.py:421
  48.6 0.8 %collective-permute-start.5 = (f32[16,128]{1,0:T(8,128)S(1)}, f32[16,128]{1,0:T(8,128)S(1)}, u32[]{:S(2)}, u32[]{:S(2)}) collective-permute-start(f32[16,128]{1,0:T(8,128)S(1)} %pairs.1.own_ref), channel_id=1, source_target_pairs={{0,8},{8,16},{16,24},{24,0},{1,9},{9,17},{17,25},{25,1},{2,10},{10... | collective-permute-start | bytes 24584 | tf_op jit(solution)/shard_map/ppermute | solution.py:421
  49.4 0.3 collective-permute-done.7.three_ref
  49.7 1.9 %collective-permute-done.6.two_ref = f32[16,128]{1,0:T(8,128)S(1)} collective-permute-done((f32[16,128]{1,0:T(8,128)S(1)}, f32[16,128]{1,0:T(8,128)S(1)}, u32[]{:S(2)}, u32[]{:S(2)}) %collective-permute-start.6) | collective-permute-done | bytes 8224 | tf_op jit(solution)/shard_map/ppermute | solution.py:421
  51.5 1.1 %collective-permute-done.5.one_ref = f32[16,128]{1,0:T(8,128)S(1)} collective-permute-done((f32[16,128]{1,0:T(8,128)S(1)}, f32[16,128]{1,0:T(8,128)S(1)}, u32[]{:S(2)}, u32[]{:S(2)}) %collective-permute-start.5) | collective-permute-done | bytes 8224 | tf_op jit(solution)/shard_map/ppermute | solution.py:421
  52.7 0.7 combine.1
  53.3 0.0 copy-start
  53.4 4.0 %all-to-all-start.2 = ((f32[32,8,128]{2,1,0:T(8,128)}), f32[32,8,128]{2,1,0:T(8,128)S(1)}, u32[]{:S(2)}, u32[]{:S(2)}) async-start(f32[32,8,128]{2,1,0:T(8,128)} %get-tuple-element.109), calls=%async_computation.2 | async-start | bytes 262144 | tf_op jit(solution)/shard_map/all_to_all | solution.py:429
  57.4 0.0 copy-start.1
  57.4 0.7 reduce_sum.9
  58.8 0.0 copy-done
  58.8 0.0 copy-done.1
  58.8 4.1 %plan.1 = (s32[1]{0:T(128)}, s32[17]{0:T(128)S(1)}, s32[16,128]{1,0:T(8,128)S(1)}, s32[16,128]{1,0:T(8,128)S(1)}, s32[16,128]{1,0:T(8,128)S(1)}, /*index=5*/s32[...) custom-call(s32[8]{0:T(128)} %counts_ref.5, ...), custom_call_target="tpu_custom_call" | custom-call | tf_op jit(solution)/shard_map/plan/pallas_call | solution.py:468
  62.9 3.7 %all-to-all-done.2 = f32[32,8,128]{2,1,0:T(8,128)S(1)} async-done(((f32[32,8,128]{2,1,0:T(8,128)}), f32[32,8,128]{2,1,0:T(8,128)S(1)}, u32[]{:S(2)}, u32[]{:S(2)}) %all-to-all-start.2) | async-done | bytes 131104 | tf_op jit(solution)/shard_map/all_to_all | solution.py:429
  66.7 2.1 %collective-permute-start.8 = (f32[256,128]{1,0:T(8,128)S(1)}, f32[256,128]{1,0:T(8,128)S(1)}, u32[]{:S(2)}, u32[]{:S(2)}) collective-permute-start(f32[256,128]{1,0:T(8,128)S(1)} %bitcast.14), channel_id=1, source_target_pairs={{0,32},{32,0},{1,33},{33,1},{2,34},{34,2},{3,35},{35,3},{4,36},{36... | collective-permute-start | bytes 393224 | tf_op jit(solution)/shard_map/ppermute | solution.py:431
  68.7 1.0 %collective-permute-done.8.other_ref = f32[256,128]{1,0:T(8,128)S(1)} collective-permute-done((f32[256,128]{1,0:T(8,128)S(1)}, f32[256,128]{1,0:T(8,128)S(1)}, u32[]{:S(2)}, u32[]{:S(2)}) %collective-permute-start.8) | collective-permute-done | bytes 131104 | tf_op jit(solution)/shard_map/ppermute | solution.py:431
  69.7 1.9 %finish.2 = (f32[12,2048]{1,0:T(8,128)S(1)}, f32[6,2048]{1,0:T(8,128)S(1)}) custom-call(s32[1]{0:T(128)} %get-tuple-element.268.number_ref, s32[17]{0:T(128)S(1)} %get-tuple-element.269.first_ref, s32[16,128]{1,0:T(8,128)S(1)} %get-tuple-element.270.rank_ref, s32[16,128]{1,0:T(8,128)S(1)} %get-tuple-element.271.block_ref, ...), custom_call_target="tpu_custom_call" | custom-call | tf_op jit(solution)/shard_map/finish/pallas_call | solution.py:435
  71.6 0.0 copy-start.3
  71.7 0.0 copy-start.4
  71.7 0.6 copy-done.3
  72.3 0.0 copy-done.4
  (1 shorter events, 0.0 us)
Async XLA Ops:
  24.4 11.5 %copy-start.2 = (s32[8]{0:T(128)S(1)}, s32[8]{0:T(128)}, u32[]{:S(2)}) copy-start(s32[8]{0:T(128)} %counts_ref.5) | copy-start | bytes 100
  24.4 3.6 %collective-permute-start.1 = (f32[512,128]{1,0:T(8,128)S(1)}, f32[512,128]{1,0:T(8,128)S(1)}, u32[]{:S(2)}, u32[]{:S(2)}) collective-permute-start(f32[512,128]{1,0:T(8,128)S(1)} %bitcast.10), channel_id=1, source_target_pairs={{0,32},{32,0},{1,33},{33,1},{2,34},{34,2},{3,35},{35,3},{4,36},{36... | collective-permute-start | bytes 786440 | tf_op jit(solution)/shard_map/ppermute | solution.py:431
  29.1 3.9 %collective-permute-start.4 = (f32[16,128]{1,0:T(8,128)S(1)}, f32[16,128]{1,0:T(8,128)S(1)}, u32[]{:S(2)}, u32[]{:S(2)}) collective-permute-start(f32[16,128]{1,0:T(8,128)S(1)} %extract.1.own_ref), channel_id=1, source_target_pairs={{0,24},{8,0},{16,8},{24,16},{1,25},{9,1},{17,9},{25,17},{2,26},{10... | collective-permute-start | bytes 24584 | tf_op jit(solution)/shard_map/ppermute | solution.py:421
  31.9 4.0 %collective-permute-start.3 = (f32[16,128]{1,0:T(8,128)S(1)}, f32[16,128]{1,0:T(8,128)S(1)}, u32[]{:S(2)}, u32[]{:S(2)}) collective-permute-start(f32[16,128]{1,0:T(8,128)S(1)} %extract.1.own_ref), channel_id=1, source_target_pairs={{0,16},{8,24},{16,0},{24,8},{1,17},{9,25},{17,1},{25,9},{2,18},{10... | collective-permute-start | bytes 24584 | tf_op jit(solution)/shard_map/ppermute | solution.py:421
  32.2 3.7 %collective-permute-start.2 = (f32[16,128]{1,0:T(8,128)S(1)}, f32[16,128]{1,0:T(8,128)S(1)}, u32[]{:S(2)}, u32[]{:S(2)}) collective-permute-start(f32[16,128]{1,0:T(8,128)S(1)} %extract.1.own_ref), channel_id=1, source_target_pairs={{0,8},{8,16},{16,24},{24,0},{1,9},{9,17},{17,25},{25,1},{2,10},{10... | collective-permute-start | bytes 24584 | tf_op jit(solution)/shard_map/ppermute | solution.py:421
  46.8 2.9 %collective-permute-start.7 = (f32[16,128]{1,0:T(8,128)S(1)}, f32[16,128]{1,0:T(8,128)S(1)}, u32[]{:S(2)}, u32[]{:S(2)}) collective-permute-start(f32[16,128]{1,0:T(8,128)S(1)} %pairs.1.own_ref), channel_id=1, source_target_pairs={{0,24},{8,0},{16,8},{24,16},{1,25},{9,1},{17,9},{25,17},{2,26},{10... | collective-permute-start | bytes 24584 | tf_op jit(solution)/shard_map/ppermute | solution.py:421
  47.4 4.1 %collective-permute-start.6 = (f32[16,128]{1,0:T(8,128)S(1)}, f32[16,128]{1,0:T(8,128)S(1)}, u32[]{:S(2)}, u32[]{:S(2)}) collective-permute-start(f32[16,128]{1,0:T(8,128)S(1)} %pairs.1.own_ref), channel_id=1, source_target_pairs={{0,16},{8,24},{16,0},{24,8},{1,17},{9,25},{17,1},{25,9},{2,18},{10... | collective-permute-start | bytes 24584 | tf_op jit(solution)/shard_map/ppermute | solution.py:421
  48.6 4.1 %collective-permute-start.5 = (f32[16,128]{1,0:T(8,128)S(1)}, f32[16,128]{1,0:T(8,128)S(1)}, u32[]{:S(2)}, u32[]{:S(2)}) collective-permute-start(f32[16,128]{1,0:T(8,128)S(1)} %pairs.1.own_ref), channel_id=1, source_target_pairs={{0,8},{8,16},{16,24},{24,0},{1,9},{9,17},{17,25},{25,1},{2,10},{10... | collective-permute-start | bytes 24584 | tf_op jit(solution)/shard_map/ppermute | solution.py:421
  53.3 5.4 %copy-start = (f32[12,2048]{1,0:T(8,128)S(1)}, f32[12,2048]{1,0:T(8,128)}, u32[]{:S(2)}) copy-start(f32[12,2048]{1,0:T(8,128)} %state_ref.5) | copy-start | bytes 294916
  53.4 13.3 %all-to-all-start.2 = ((f32[32,8,128]{2,1,0:T(8,128)}), f32[32,8,128]{2,1,0:T(8,128)S(1)}, u32[]{:S(2)}, u32[]{:S(2)}) async-start(f32[32,8,128]{2,1,0:T(8,128)} %get-tuple-element.109), calls=%async_computation.2 | async-start | bytes 262144 | tf_op jit(solution)/shard_map/all_to_all | solution.py:429
  57.4 1.4 %copy-start.1 = (f32[2048]{0:T(1024)S(1)}, f32[2048]{0:T(1024)}, u32[]{:S(2)}) copy-start(f32[2048]{0:T(1024)} %param.9) | copy-start | bytes 24580
  66.7 3.1 %collective-permute-start.8 = (f32[256,128]{1,0:T(8,128)S(1)}, f32[256,128]{1,0:T(8,128)S(1)}, u32[]{:S(2)}, u32[]{:S(2)}) collective-permute-start(f32[256,128]{1,0:T(8,128)S(1)} %bitcast.14), channel_id=1, source_target_pairs={{0,32},{32,0},{1,33},{33,1},{2,34},{34,2},{3,35},{35,3},{4,36},{36... | collective-permute-start | bytes 393224 | tf_op jit(solution)/shard_map/ppermute | solution.py:431
  71.6 0.7 copy-start.3
  71.7 0.7 copy-start.4

commit v7 on v6

--- a/solution.py
+++ b/solution.py
@@ -249,7 +249,7 @@
 
 def pair_kernel(
     counts_ref, own_ref, one_ref, two_ref, three_ref, mine_ref, other_ref, out_ref,
-    splat_ref, source_ref, part_ref,
+    splat_ref, source_ref, part_ref, sum_ref,
 ):
     _, live = list_offsets(counts_ref)
     size = jnp.where(lax.axis_index("c") == 0, *two_sizes(live))
@@ -265,15 +265,22 @@
 
     def one_half(half):
         mine = targets[half * 8 : half * 8 + 8]
-        for t in range(LANES):
-            values = take(mine, jnp.full((8, LANES), t, I32))
-            for c in range(6):
-                at = (t * 6 + c) * 8
-                splat_ref[at : at + 8, :] = jnp.broadcast_to(values[c : c + 1], (8, LANES))
+        count = jnp.minimum(size - half * LANES, LANES)
+
+        def splat(chunk):
+            for t in range(chunk * 32, chunk * 32 + 32):
+                values = take(mine, jnp.full((8, LANES), t, I32))
+                for c in range(6):
+                    at = (t * 6 + c) * 8
+                    splat_ref[at : at + 8, :] = jnp.broadcast_to(values[c : c + 1], (8, LANES))
+
+        splat(0)
+        for chunk in range(1, 4):
+            pl.when(count > chunk * 32)(functools.partial(splat, chunk))
 
         def four_targets(turn, carry):
             first = turn * 4
-            sums = [zero] * 24
+            sums = [zero] * 36
             for v in range(SETS):
                 sx, sy, sz, vx, vy, vz, mass = [
                     source_ref[(c * SETS + v) * 8 : (c * SETS + v) * 8 + 8, :] for c in range(7)
@@ -294,22 +301,28 @@
                     inverse = lax.rsqrt(square)
                     inverse2 = inverse * inverse
                     weight = (mass * inverse) * inverse2
-                    radial = (3.0 * dot) * inverse2
-                    terms = (
-                        rx, ry, rz,
-                        wx - radial * rx, wy - radial * ry, wz - radial * rz,
-                    )
-                    for c in range(6):
-                        sums[t * 6 + c] = sums[t * 6 + c] + weight * terms[c]
+                    radial = dot * inverse2
+                    pulls = (weight * rx, weight * ry, weight * rz)
+                    drifts = (weight * wx, weight * wy, weight * wz)
+                    for c in range(3):
+                        sums[t * 9 + c] = sums[t * 9 + c] + pulls[c]
+                        sums[t * 9 + 3 + c] = sums[t * 9 + 3 + c] + drifts[c]
+                        sums[t * 9 + 6 + c] = sums[t * 9 + 6 + c] + radial * pulls[c]
             for t in range(4):
                 for c in range(6):
-                    part_ref[pl.ds(pl.multiple_of((c * LANES + first + t) * 8, 8), 8), :] = sums[t * 6 + c]
+                    total = sums[t * 9 + c]
+                    if c >= 3:
+                        total = total - 3.0 * sums[t * 9 + 3 + c]
+                    part_ref[pl.ds(pl.multiple_of((c * LANES + first + t) * 8, 8), 8), :] = total
             return carry
 
-        count = jnp.minimum(size - half * LANES, LANES)
         lax.fori_loop(0, (count + 3) >> 2, four_targets, 0)
-        rows = []
-        for o in range(16):
+
+        def gather_sums(octets):
+            for o in octets:
+                one_octet(o)
+
+        def one_octet(o):
             row = zero
             for c in range(6):
                 first = (c * LANES + o * 8) * 8
@@ -317,8 +330,12 @@
                 for k in range(1, 8):
                     total = total + part_ref[pl.ds(first + k, 8, stride=8), :]
                 row = jnp.where(column == c, jnp.sum(total, axis=1, keepdims=True), row)
-            rows.append(row)
-        out_ref[half * 8 : half * 8 + 8, :] = jnp.concatenate(rows, axis=0).T[0:8]
+            sum_ref[o * 8 : o * 8 + 8, :] = row
+
+        gather_sums(range(4))
+        for chunk in range(1, 4):
+            pl.when(count > chunk * 32)(functools.partial(gather_sums, range(chunk * 4, chunk * 4 + 4)))
+        out_ref[half * 8 : half * 8 + 8, :] = sum_ref[...].T[0:8]
 
     one_half(0)
 
@@ -483,13 +500,14 @@
             pltpu.VMEM((LANES * 6 * 8, LANES), F32),
             pltpu.VMEM((7 * SETS * 8, LANES), F32),
             pltpu.VMEM((6 * LANES * 8, LANES), F32),
+            pltpu.VMEM((LANES, LANES), F32),
         ],
         compiler_params=pltpu.CompilerParams(vmem_limit_bytes=24 * 2**20),
         name="pairs",
     )(active_count, *in_vmem(own, *others), *slab)
     combined, rest = pl.pallas_call(
         combine_kernel,
-        out_shape=[pltpu.VMEM((32, 8, LANES), F32), jax.ShapeDtypeStruct((8, LANES), F32)],
+        out_shape=[pltpu.VMEM((32, 8, LANES), F32), pltpu.VMEM((8, LANES), F32)],
         in_specs=[VMEM] * 4,
         out_specs=[VMEM] * 2,
         name="combine",

time: 73.1 us -> 73.6 us (level)
  transfers between devices with their start and end apart: 9 -> 9, of which waited for: 8 -> 7; matrix products, arithmetic and copies ran while one was open for 1% -> 1% of each run, Pallas kernels for 6% -> 6%
where the time goes in v7:
time: 73.6 us; the launch traced here: 72.7 us
  blocking collectives  22.9 us (31%)
  Pallas kernels  20.1 us (27%)
  starting transfers between devices  15 us (20%)
  waiting for transfers between devices  11.9 us (16%)
  between operations  1.41 us (2%)
    all_to_all x1, blocking collectives, spread(): part = lax.all_to_all(part, ('z', 'x'), 0, 0).reshape(-1, LANES)  22.9 us
    pallas_call x1, Pallas kernels, body(): pl.pallas_call(pair_kernel, out_shape=pltpu.VMEM((16, LANES), F32), in_sp...  11.5 us
    ppermute x6, starting transfers between devices, exchange_y(): lax.ppermute(part, 'y', [(i, (i + k) % 4) for i in range(4)])  6.43 us
    ppermute x6, waiting for transfers between devices, exchange_y(): lax.ppermute(part, 'y', [(i, (i + k) % 4) for i in range(4)])  6.07 us
    ppermute x2, starting transfers between devices, spread(): return (in_vmem(part, lax.ppermute(part, 'c', [(0, 1), (1, 0)])), done)  4.54 us
    pallas_call x1, Pallas kernels, body(): pl.pallas_call(plan_kernel, out_shape=[jax.ShapeDtypeStruct((1,), I32), j...  4.14 us
    all_to_all x1, starting transfers between devices, spread(): part = lax.all_to_all(part, ('z', 'x'), 0, 0).reshape(-1, LANES)  3.99 us
    all_to_all x1, waiting for transfers between devices, spread(): part = lax.all_to_all(part, ('z', 'x'), 0, 0).reshape(-1, LANES)  3.72 us
  transfers between devices with their start and end apart: 9, of which 7 were waited for; matrix products, arithmetic and copies ran while one was open for 1% of the time, Pallas kernels for 6%

profile of v7, /device:TPU:1, one launch (start us, length us, event | category | flops | bytes accessed | tf_op | source)
XLA Modules:
  0.0 72.7 jit_solution(7562283601837833407)
XLA Ops:
  0.6 1.0 %pack.1 = f32[32,16,128]{2,1,0:T(8,128)S(1)} custom-call(f32[12,2048]{1,0:T(8,128)} %state_ref.5, f32[1,2048]{1,0:T(1,128)} %bitcast.18, f32[1,2048]{1,0:T(1,128)} %bitcast.16, s32[1,2048]{1,0:T(1,128)} %bitcast.19), custom_call_target="tpu_custom_call" | custom-call | tf_op jit(solution)/shard_map/pack/pallas_call | solution.py:468
  1.6 22.9 %all_to_all.16 = f32[32,16,128]{2,1,0:T(8,128)S(1)} all-to-all(f32[32,16,128]{2,1,0:T(8,128)S(1)} %pack.1), channel_id=1, replica_groups=mesh['x'=4,'c'=2,'y'=4,'z'=8] {'z','x'}, dimensions={0} | all-to-all | bytes 524288 | tf_op jit(solution)/shard_map/all_to_all | solution.py:446
  24.4 0.0 copy-start.2
  24.4 2.5 %collective-permute-start.1 = (f32[512,128]{1,0:T(8,128)S(1)}, f32[512,128]{1,0:T(8,128)S(1)}, u32[]{:S(2)}, u32[]{:S(2)}) collective-permute-start(f32[512,128]{1,0:T(8,128)S(1)} %bitcast.10), channel_id=1, source_target_pairs={{0,32},{32,0},{1,33},{33,1},{2,34},{34,2},{3,35},{35,3},{4,36},{36... | collective-permute-start | bytes 786440 | tf_op jit(solution)/shard_map/ppermute | solution.py:448
  26.9 1.2 %collective-permute-done.1.other_ref = f32[512,128]{1,0:T(8,128)S(1)} collective-permute-done((f32[512,128]{1,0:T(8,128)S(1)}, f32[512,128]{1,0:T(8,128)S(1)}, u32[]{:S(2)}, u32[]{:S(2)}) %collective-permute-start.1) | collective-permute-done | bytes 262176 | tf_op jit(solution)/shard_map/ppermute | solution.py:448
  28.1 1.0 %extract.1.own_ref = f32[16,128]{1,0:T(8,128)S(1)} custom-call(s32[8]{0:T(128)} %counts_ref.5, f32[512,128]{1,0:T(8,128)S(1)} %bitcast.11, f32[512,128]{1,0:T(8,128)S(1)} %collective-permute-done.1.other_ref), custom_call_target="tpu_custom_call" | custom-call | tf_op jit(solution)/shard_map/extract/pallas_call | solution.py:476
  29.1 2.8 %collective-permute-start.4 = (f32[16,128]{1,0:T(8,128)S(1)}, f32[16,128]{1,0:T(8,128)S(1)}, u32[]{:S(2)}, u32[]{:S(2)}) collective-permute-start(f32[16,128]{1,0:T(8,128)S(1)} %extract.1.own_ref), channel_id=1, source_target_pairs={{0,24},{8,0},{16,8},{24,16},{1,25},{9,1},{17,9},{25,17},{2,26},{10... | collective-permute-start | bytes 24584 | tf_op jit(solution)/shard_map/ppermute | solution.py:438
  31.9 0.3 collective-permute-start.3
  32.2 0.7 collective-permute-start.2
  32.9 0.0 collective-permute-done.4.three_ref
  32.9 3.0 %collective-permute-done.3.two_ref = f32[16,128]{1,0:T(8,128)S(1)} collective-permute-done((f32[16,128]{1,0:T(8,128)S(1)}, f32[16,128]{1,0:T(8,128)S(1)}, u32[]{:S(2)}, u32[]{:S(2)}) %collective-permute-start.3) | collective-permute-done | bytes 8224 | tf_op jit(solution)/shard_map/ppermute | solution.py:438
  35.9 0.1 collective-permute-done.2.one_ref
  36.0 0.0 copy-done.2
  36.0 11.5 %pairs.1.own_ref = f32[16,128]{1,0:T(8,128)S(1)} custom-call(s32[8]{0:T(128)S(1)} %copy-done.2, f32[16,128]{1,0:T(8,128)S(1)} %extract.1.own_ref, f32[16,128]{1,0:T(8,128)S(1)} %collective-permute-done.2.one_ref, f32[16,128]{1,0:T(8,128)S(1)} %collective-permute-done.3.two_ref, f32[16,128]{1,0:T(8,128)S(1)} %collective-permute-done.4.three_ref, ...), custom_call_target="tpu_custom_call" | custom-call | tf_op jit(solution)/shard_map/pairs/pallas_call | solution.py:494
  47.4 0.6 collective-permute-start.7
  48.1 1.2 %collective-permute-start.6 = (f32[16,128]{1,0:T(8,128)S(1)}, f32[16,128]{1,0:T(8,128)S(1)}, u32[]{:S(2)}, u32[]{:S(2)}) collective-permute-start(f32[16,128]{1,0:T(8,128)S(1)} %pairs.1.own_ref), channel_id=1, source_target_pairs={{0,16},{8,24},{16,0},{24,8},{1,17},{9,25},{17,1},{25,9},{2,18},{10... | collective-permute-start | bytes 24584 | tf_op jit(solution)/shard_map/ppermute | solution.py:438
  49.2 0.8 %collective-permute-start.5 = (f32[16,128]{1,0:T(8,128)S(1)}, f32[16,128]{1,0:T(8,128)S(1)}, u32[]{:S(2)}, u32[]{:S(2)}) collective-permute-start(f32[16,128]{1,0:T(8,128)S(1)} %pairs.1.own_ref), channel_id=1, source_target_pairs={{0,8},{8,16},{16,24},{24,0},{1,9},{9,17},{17,25},{25,1},{2,10},{10... | collective-permute-start | bytes 24584 | tf_op jit(solution)/shard_map/ppermute | solution.py:438
  50.0 0.0 collective-permute-done.7.three_ref
  50.0 2.0 %collective-permute-done.6.two_ref = f32[16,128]{1,0:T(8,128)S(1)} collective-permute-done((f32[16,128]{1,0:T(8,128)S(1)}, f32[16,128]{1,0:T(8,128)S(1)}, u32[]{:S(2)}, u32[]{:S(2)}) %collective-permute-start.6) | collective-permute-done | bytes 8224 | tf_op jit(solution)/shard_map/ppermute | solution.py:438
  52.1 1.0 %collective-permute-done.5.one_ref = f32[16,128]{1,0:T(8,128)S(1)} collective-permute-done((f32[16,128]{1,0:T(8,128)S(1)}, f32[16,128]{1,0:T(8,128)S(1)}, u32[]{:S(2)}, u32[]{:S(2)}) %collective-permute-start.5) | collective-permute-done | bytes 8224 | tf_op jit(solution)/shard_map/ppermute | solution.py:438
  53.0 0.7 combine.1
  53.7 0.0 copy-start
  53.7 4.0 %all-to-all-start.2 = ((f32[32,8,128]{2,1,0:T(8,128)}), f32[32,8,128]{2,1,0:T(8,128)S(1)}, u32[]{:S(2)}, u32[]{:S(2)}) async-start(f32[32,8,128]{2,1,0:T(8,128)} %get-tuple-element.109), calls=%async_computation.2 | async-start | bytes 262144 | tf_op jit(solution)/shard_map/all_to_all | solution.py:446
  57.7 0.0 copy-start.1
  57.7 0.7 reduce_sum.9
  59.1 0.0 copy-done
  59.1 0.0 copy-done.1
  59.1 4.1 %plan.1 = (s32[1]{0:T(128)}, s32[17]{0:T(128)S(1)}, s32[16,128]{1,0:T(8,128)S(1)}, s32[16,128]{1,0:T(8,128)S(1)}, s32[16,128]{1,0:T(8,128)S(1)}, /*index=5*/s32[...) custom-call(s32[8]{0:T(128)} %counts_ref.5, ...), custom_call_target="tpu_custom_call" | custom-call | tf_op jit(solution)/shard_map/plan/pallas_call | solution.py:485
  63.3 3.7 %all-to-all-done.2 = f32[32,8,128]{2,1,0:T(8,128)S(1)} async-done(((f32[32,8,128]{2,1,0:T(8,128)}), f32[32,8,128]{2,1,0:T(8,128)S(1)}, u32[]{:S(2)}, u32[]{:S(2)}) %all-to-all-start.2) | async-done | bytes 131104 | tf_op jit(solution)/shard_map/all_to_all | solution.py:446
  67.0 2.1 %collective-permute-start.8 = (f32[256,128]{1,0:T(8,128)S(1)}, f32[256,128]{1,0:T(8,128)S(1)}, u32[]{:S(2)}, u32[]{:S(2)}) collective-permute-start(f32[256,128]{1,0:T(8,128)S(1)} %bitcast.14), channel_id=1, source_target_pairs={{0,32},{32,0},{1,33},{33,1},{2,34},{34,2},{3,35},{35,3},{4,36},{36... | collective-permute-start | bytes 393224 | tf_op jit(solution)/shard_map/ppermute | solution.py:448
  69.1 1.0 %collective-permute-done.8.other_ref = f32[256,128]{1,0:T(8,128)S(1)} collective-permute-done((f32[256,128]{1,0:T(8,128)S(1)}, f32[256,128]{1,0:T(8,128)S(1)}, u32[]{:S(2)}, u32[]{:S(2)}) %collective-permute-start.8) | collective-permute-done | bytes 131104 | tf_op jit(solution)/shard_map/ppermute | solution.py:448
  70.1 1.9 %finish.2 = (f32[12,2048]{1,0:T(8,128)S(1)}, f32[6,2048]{1,0:T(8,128)S(1)}) custom-call(s32[1]{0:T(128)} %get-tuple-element.268.number_ref, s32[17]{0:T(128)S(1)} %get-tuple-element.269.first_ref, s32[16,128]{1,0:T(8,128)S(1)} %get-tuple-element.270.rank_ref, s32[16,128]{1,0:T(8,128)S(1)} %get-tuple-element.271.block_ref, ...), custom_call_target="tpu_custom_call" | custom-call | tf_op jit(solution)/shard_map/finish/pallas_call | solution.py:452
  72.0 0.0 copy-start.3
  72.0 0.0 copy-start.4
  72.0 0.6 copy-done.3
  72.6 0.0 copy-done.4
  (1 shorter events, 0.0 us)
Async XLA Ops:
  24.4 11.5 %copy-start.2 = (s32[8]{0:T(128)S(1)}, s32[8]{0:T(128)}, u32[]{:S(2)}) copy-start(s32[8]{0:T(128)} %counts_ref.5) | copy-start | bytes 100
  24.4 3.6 %collective-permute-start.1 = (f32[512,128]{1,0:T(8,128)S(1)}, f32[512,128]{1,0:T(8,128)S(1)}, u32[]{:S(2)}, u32[]{:S(2)}) collective-permute-start(f32[512,128]{1,0:T(8,128)S(1)} %bitcast.10), channel_id=1, source_target_pairs={{0,32},{32,0},{1,33},{33,1},{2,34},{34,2},{3,35},{35,3},{4,36},{36... | collective-permute-start | bytes 786440 | tf_op jit(solution)/shard_map/ppermute | solution.py:448
  29.1 3.9 %collective-permute-start.4 = (f32[16,128]{1,0:T(8,128)S(1)}, f32[16,128]{1,0:T(8,128)S(1)}, u32[]{:S(2)}, u32[]{:S(2)}) collective-permute-start(f32[16,128]{1,0:T(8,128)S(1)} %extract.1.own_ref), channel_id=1, source_target_pairs={{0,24},{8,0},{16,8},{24,16},{1,25},{9,1},{17,9},{25,17},{2,26},{10... | collective-permute-start | bytes 24584 | tf_op jit(solution)/shard_map/ppermute | solution.py:438
  31.9 4.0 %collective-permute-start.3 = (f32[16,128]{1,0:T(8,128)S(1)}, f32[16,128]{1,0:T(8,128)S(1)}, u32[]{:S(2)}, u32[]{:S(2)}) collective-permute-start(f32[16,128]{1,0:T(8,128)S(1)} %extract.1.own_ref), channel_id=1, source_target_pairs={{0,16},{8,24},{16,0},{24,8},{1,17},{9,25},{17,1},{25,9},{2,18},{10... | collective-permute-start | bytes 24584 | tf_op jit(solution)/shard_map/ppermute | solution.py:438
  32.2 3.7 %collective-permute-start.2 = (f32[16,128]{1,0:T(8,128)S(1)}, f32[16,128]{1,0:T(8,128)S(1)}, u32[]{:S(2)}, u32[]{:S(2)}) collective-permute-start(f32[16,128]{1,0:T(8,128)S(1)} %extract.1.own_ref), channel_id=1, source_target_pairs={{0,8},{8,16},{16,24},{24,0},{1,9},{9,17},{17,25},{25,1},{2,10},{10... | collective-permute-start | bytes 24584 | tf_op jit(solution)/shard_map/ppermute | solution.py:438
  47.4 2.6 %collective-permute-start.7 = (f32[16,128]{1,0:T(8,128)S(1)}, f32[16,128]{1,0:T(8,128)S(1)}, u32[]{:S(2)}, u32[]{:S(2)}) collective-permute-start(f32[16,128]{1,0:T(8,128)S(1)} %pairs.1.own_ref), channel_id=1, source_target_pairs={{0,24},{8,0},{16,8},{24,16},{1,25},{9,1},{17,9},{25,17},{2,26},{10... | collective-permute-start | bytes 24584 | tf_op jit(solution)/shard_map/ppermute | solution.py:438
  48.1 4.0 %collective-permute-start.6 = (f32[16,128]{1,0:T(8,128)S(1)}, f32[16,128]{1,0:T(8,128)S(1)}, u32[]{:S(2)}, u32[]{:S(2)}) collective-permute-start(f32[16,128]{1,0:T(8,128)S(1)} %pairs.1.own_ref), channel_id=1, source_target_pairs={{0,16},{8,24},{16,0},{24,8},{1,17},{9,25},{17,1},{25,9},{2,18},{10... | collective-permute-start | bytes 24584 | tf_op jit(solution)/shard_map/ppermute | solution.py:438
  49.2 3.8 %collective-permute-start.5 = (f32[16,128]{1,0:T(8,128)S(1)}, f32[16,128]{1,0:T(8,128)S(1)}, u32[]{:S(2)}, u32[]{:S(2)}) collective-permute-start(f32[16,128]{1,0:T(8,128)S(1)} %pairs.1.own_ref), channel_id=1, source_target_pairs={{0,8},{8,16},{16,24},{24,0},{1,9},{9,17},{17,25},{25,1},{2,10},{10... | collective-permute-start | bytes 24584 | tf_op jit(solution)/shard_map/ppermute | solution.py:438
  53.7 5.4 %copy-start = (f32[12,2048]{1,0:T(8,128)S(1)}, f32[12,2048]{1,0:T(8,128)}, u32[]{:S(2)}) copy-start(f32[12,2048]{1,0:T(8,128)} %state_ref.5) | copy-start | bytes 294916
  53.7 13.3 %all-to-all-start.2 = ((f32[32,8,128]{2,1,0:T(8,128)}), f32[32,8,128]{2,1,0:T(8,128)S(1)}, u32[]{:S(2)}, u32[]{:S(2)}) async-start(f32[32,8,128]{2,1,0:T(8,128)} %get-tuple-element.109), calls=%async_computation.2 | async-start | bytes 262144 | tf_op jit(solution)/shard_map/all_to_all | solution.py:446
  57.7 1.4 %copy-start.1 = (f32[2048]{0:T(1024)S(1)}, f32[2048]{0:T(1024)}, u32[]{:S(2)}) copy-start(f32[2048]{0:T(1024)} %param.9) | copy-start | bytes 24580
  67.0 3.1 %collective-permute-start.8 = (f32[256,128]{1,0:T(8,128)S(1)}, f32[256,128]{1,0:T(8,128)S(1)}, u32[]{:S(2)}, u32[]{:S(2)}) collective-permute-start(f32[256,128]{1,0:T(8,128)S(1)} %bitcast.14), channel_id=1, source_target_pairs={{0,32},{32,0},{1,33},{33,1},{2,34},{34,2},{3,35},{35,3},{4,36},{36... | collective-permute-start | bytes 393224 | tf_op jit(solution)/shard_map/ppermute | solution.py:448
  72.0 0.7 copy-start.3
  72.0 0.7 copy-start.4

commit v8 on v7

--- a/solution.py
+++ b/solution.py
@@ -12,7 +12,7 @@
 softening_square = 0.01
 LISTS = 8
 CAP = 2048
-SHIFT = 5
+SHIFT = 6
 SHARD = 2048
 GROUPS = 64
 LANES = 128

time: 73.6 us -> 73 us (level); the launches traced: 72.7 us -> 74.1 us
  Pallas kernels: 20.1 us -> 21.9 us
  starting transfers between devices: 15 us -> 13.3 us
  waiting for transfers between devices: 11.9 us -> 13.2 us
    pallas_call x1, Pallas kernels: 11.5 us -> 13.2 us  [body(): pl.pallas_call(pair_kernel, out_shape=pltpu.VMEM((16, LANES), F32), in_sp...]
    ppermute x2, starting transfers between devices: 4.54 us -> 2.89 us  [spread(): return (in_vmem(part, lax.ppermute(part, 'c', [(0, 1), (1, 0)])), done)]
    all_to_all x1, waiting for transfers between devices: 3.72 us -> 5.06 us  [spread(): part = lax.all_to_all(part, ('z', 'x'), 0, 0).reshape(-1, LANES)]
  transfers between devices with their start and end apart: 9 -> 9, of which waited for: 7 -> 8; matrix products, arithmetic and copies ran while one was open for 1% -> 1% of each run, Pallas kernels for 6% -> 6%
where the time goes in v8:
time: 73 us; the launch traced here: 74.1 us
  blocking collectives  22.9 us (31%)
  Pallas kernels  21.9 us (30%)
  starting transfers between devices  13.3 us (18%)
  waiting for transfers between devices  13.2 us (18%)
  between operations  1.41 us (2%)
    all_to_all x1, blocking collectives, spread(): part = lax.all_to_all(part, ('z', 'x'), 0, 0).reshape(-1, LANES)  22.9 us
    pallas_call x1, Pallas kernels, body(): pl.pallas_call(pair_kernel, out_shape=pltpu.VMEM((16, LANES), F32), in_sp...  13.2 us
    ppermute x6, starting transfers between devices, exchange_y(): lax.ppermute(part, 'y', [(i, (i + k) % 4) for i in range(4)])  6.43 us
    ppermute x6, waiting for transfers between devices, exchange_y(): lax.ppermute(part, 'y', [(i, (i + k) % 4) for i in range(4)])  6 us
    all_to_all x1, waiting for transfers between devices, spread(): part = lax.all_to_all(part, ('z', 'x'), 0, 0).reshape(-1, LANES)  5.06 us
    pallas_call x1, Pallas kernels, body(): pl.pallas_call(plan_kernel, out_shape=[jax.ShapeDtypeStruct((1,), I32), j...  4.14 us
    all_to_all x1, starting transfers between devices, spread(): part = lax.all_to_all(part, ('z', 'x'), 0, 0).reshape(-1, LANES)  3.99 us
    ppermute x2, starting transfers between devices, spread(): return (in_vmem(part, lax.ppermute(part, 'c', [(0, 1), (1, 0)])), done)  2.89 us
  transfers between devices with their start and end apart: 9, of which 8 were waited for; matrix products, arithmetic and copies ran while one was open for 1% of the time, Pallas kernels for 6%

profile of v8, /device:TPU:1, one launch (start us, length us, event | category | flops | bytes accessed | tf_op | source)
XLA Modules:
  0.0 74.1 jit_solution(4280559200657756869)
XLA Ops:
  0.6 1.0 %pack.1 = f32[32,16,128]{2,1,0:T(8,128)S(1)} custom-call(f32[12,2048]{1,0:T(8,128)} %state_ref.5, f32[1,2048]{1,0:T(1,128)} %bitcast.18, f32[1,2048]{1,0:T(1,128)} %bitcast.16, s32[1,2048]{1,0:T(1,128)} %bitcast.19), custom_call_target="tpu_custom_call" | custom-call | tf_op jit(solution)/shard_map/pack/pallas_call | solution.py:468
  1.6 22.9 %all_to_all.16 = f32[32,16,128]{2,1,0:T(8,128)S(1)} all-to-all(f32[32,16,128]{2,1,0:T(8,128)S(1)} %pack.1), channel_id=1, replica_groups=mesh['x'=4,'c'=2,'y'=4,'z'=8] {'z','x'}, dimensions={0} | all-to-all | bytes 524288 | tf_op jit(solution)/shard_map/all_to_all | solution.py:446
  24.4 0.0 copy-start.2
  24.4 2.5 %collective-permute-start.1 = (f32[512,128]{1,0:T(8,128)S(1)}, f32[512,128]{1,0:T(8,128)S(1)}, u32[]{:S(2)}, u32[]{:S(2)}) collective-permute-start(f32[512,128]{1,0:T(8,128)S(1)} %bitcast.10), channel_id=1, source_target_pairs={{0,32},{32,0},{1,33},{33,1},{2,34},{34,2},{3,35},{35,3},{4,36},{36... | collective-permute-start | bytes 786440 | tf_op jit(solution)/shard_map/ppermute | solution.py:448
  26.9 1.2 %collective-permute-done.1.other_ref = f32[512,128]{1,0:T(8,128)S(1)} collective-permute-done((f32[512,128]{1,0:T(8,128)S(1)}, f32[512,128]{1,0:T(8,128)S(1)}, u32[]{:S(2)}, u32[]{:S(2)}) %collective-permute-start.1) | collective-permute-done | bytes 262176 | tf_op jit(solution)/shard_map/ppermute | solution.py:448
  28.1 1.0 %extract.1.own_ref = f32[16,128]{1,0:T(8,128)S(1)} custom-call(s32[8]{0:T(128)} %counts_ref.5, f32[512,128]{1,0:T(8,128)S(1)} %bitcast.11, f32[512,128]{1,0:T(8,128)S(1)} %collective-permute-done.1.other_ref), custom_call_target="tpu_custom_call" | custom-call | tf_op jit(solution)/shard_map/extract/pallas_call | solution.py:476
  29.1 2.8 %collective-permute-start.4 = (f32[16,128]{1,0:T(8,128)S(1)}, f32[16,128]{1,0:T(8,128)S(1)}, u32[]{:S(2)}, u32[]{:S(2)}) collective-permute-start(f32[16,128]{1,0:T(8,128)S(1)} %extract.1.own_ref), channel_id=1, source_target_pairs={{0,24},{8,0},{16,8},{24,16},{1,25},{9,1},{17,9},{25,17},{2,26},{10... | collective-permute-start | bytes 24584 | tf_op jit(solution)/shard_map/ppermute | solution.py:438
  31.9 0.3 collective-permute-start.3
  32.2 0.7 collective-permute-start.2
  32.9 0.0 collective-permute-done.4.three_ref
  32.9 3.0 %collective-permute-done.3.two_ref = f32[16,128]{1,0:T(8,128)S(1)} collective-permute-done((f32[16,128]{1,0:T(8,128)S(1)}, f32[16,128]{1,0:T(8,128)S(1)}, u32[]{:S(2)}, u32[]{:S(2)}) %collective-permute-start.3) | collective-permute-done | bytes 8224 | tf_op jit(solution)/shard_map/ppermute | solution.py:438
  35.9 0.1 collective-permute-done.2.one_ref
  36.0 0.0 copy-done.2
  36.0 13.2 %pairs.1.own_ref = f32[16,128]{1,0:T(8,128)S(1)} custom-call(s32[8]{0:T(128)S(1)} %copy-done.2, f32[16,128]{1,0:T(8,128)S(1)} %extract.1.own_ref, f32[16,128]{1,0:T(8,128)S(1)} %collective-permute-done.2.one_ref, f32[16,128]{1,0:T(8,128)S(1)} %collective-permute-done.3.two_ref, f32[16,128]{1,0:T(8,128)S(1)} %collective-permute-done.4.three_ref, ...), custom_call_target="tpu_custom_call" | custom-call | tf_op jit(solution)/shard_map/pairs/pallas_call | solution.py:494
  49.2 0.6 collective-permute-start.7
  49.8 1.2 %collective-permute-start.6 = (f32[16,128]{1,0:T(8,128)S(1)}, f32[16,128]{1,0:T(8,128)S(1)}, u32[]{:S(2)}, u32[]{:S(2)}) collective-permute-start(f32[16,128]{1,0:T(8,128)S(1)} %pairs.1.own_ref), channel_id=1, source_target_pairs={{0,16},{8,24},{16,0},{24,8},{1,17},{9,25},{17,1},{25,9},{2,18},{10... | collective-permute-start | bytes 24584 | tf_op jit(solution)/shard_map/ppermute | solution.py:438
  51.0 0.8 %collective-permute-start.5 = (f32[16,128]{1,0:T(8,128)S(1)}, f32[16,128]{1,0:T(8,128)S(1)}, u32[]{:S(2)}, u32[]{:S(2)}) collective-permute-start(f32[16,128]{1,0:T(8,128)S(1)} %pairs.1.own_ref), channel_id=1, source_target_pairs={{0,8},{8,16},{16,24},{24,0},{1,9},{9,17},{17,25},{25,1},{2,10},{10... | collective-permute-start | bytes 24584 | tf_op jit(solution)/shard_map/ppermute | solution.py:438
  51.8 0.3 collective-permute-done.7.three_ref
  52.1 1.8 %collective-permute-done.6.two_ref = f32[16,128]{1,0:T(8,128)S(1)} collective-permute-done((f32[16,128]{1,0:T(8,128)S(1)}, f32[16,128]{1,0:T(8,128)S(1)}, u32[]{:S(2)}, u32[]{:S(2)}) %collective-permute-start.6) | collective-permute-done | bytes 8224 | tf_op jit(solution)/shard_map/ppermute | solution.py:438
  53.8 0.9 %collective-permute-done.5.one_ref = f32[16,128]{1,0:T(8,128)S(1)} collective-permute-done((f32[16,128]{1,0:T(8,128)S(1)}, f32[16,128]{1,0:T(8,128)S(1)}, u32[]{:S(2)}, u32[]{:S(2)}) %collective-permute-start.5) | collective-permute-done | bytes 8224 | tf_op jit(solution)/shard_map/ppermute | solution.py:438
  54.7 0.7 combine.1
  55.4 0.0 copy-start
  55.4 4.0 %all-to-all-start.2 = ((f32[32,8,128]{2,1,0:T(8,128)}), f32[32,8,128]{2,1,0:T(8,128)S(1)}, u32[]{:S(2)}, u32[]{:S(2)}) async-start(f32[32,8,128]{2,1,0:T(8,128)} %get-tuple-element.109), calls=%async_computation.2 | async-start | bytes 262144 | tf_op jit(solution)/shard_map/all_to_all | solution.py:446
  59.4 0.0 copy-start.1
  59.4 0.7 reduce_sum.9
  60.8 0.0 copy-done
  60.8 0.0 copy-done.1
  60.8 4.1 %plan.1 = (s32[1]{0:T(128)}, s32[17]{0:T(128)S(1)}, s32[16,128]{1,0:T(8,128)S(1)}, s32[16,128]{1,0:T(8,128)S(1)}, s32[16,128]{1,0:T(8,128)S(1)}, /*index=5*/s32[...) custom-call(s32[8]{0:T(128)} %counts_ref.5, ...), custom_call_target="tpu_custom_call" | custom-call | tf_op jit(solution)/shard_map/plan/pallas_call | solution.py:485
  65.0 5.1 %all-to-all-done.2 = f32[32,8,128]{2,1,0:T(8,128)S(1)} async-done(((f32[32,8,128]{2,1,0:T(8,128)}), f32[32,8,128]{2,1,0:T(8,128)S(1)}, u32[]{:S(2)}, u32[]{:S(2)}) %all-to-all-start.2) | async-done | bytes 131104 | tf_op jit(solution)/shard_map/all_to_all | solution.py:446
  70.1 0.4 collective-permute-start.8
  70.5 1.0 %collective-permute-done.8.other_ref = f32[256,128]{1,0:T(8,128)S(1)} collective-permute-done((f32[256,128]{1,0:T(8,128)S(1)}, f32[256,128]{1,0:T(8,128)S(1)}, u32[]{:S(2)}, u32[]{:S(2)}) %collective-permute-start.8) | collective-permute-done | bytes 131104 | tf_op jit(solution)/shard_map/ppermute | solution.py:448
  71.5 1.9 %finish.2 = (f32[12,2048]{1,0:T(8,128)S(1)}, f32[6,2048]{1,0:T(8,128)S(1)}) custom-call(s32[1]{0:T(128)} %get-tuple-element.268.number_ref, s32[17]{0:T(128)S(1)} %get-tuple-element.269.first_ref, s32[16,128]{1,0:T(8,128)S(1)} %get-tuple-element.270.rank_ref, s32[16,128]{1,0:T(8,128)S(1)} %get-tuple-element.271.block_ref, ...), custom_call_target="tpu_custom_call" | custom-call | tf_op jit(solution)/shard_map/finish/pallas_call | solution.py:452
  73.4 0.0 copy-start.3
  73.4 0.0 copy-start.4
  73.4 0.6 copy-done.3
  74.0 0.0 copy-done.4
  (1 shorter events, 0.0 us)
Async XLA Ops:
  24.4 11.5 %copy-start.2 = (s32[8]{0:T(128)S(1)}, s32[8]{0:T(128)}, u32[]{:S(2)}) copy-start(s32[8]{0:T(128)} %counts_ref.5) | copy-start | bytes 100
  24.4 3.6 %collective-permute-start.1 = (f32[512,128]{1,0:T(8,128)S(1)}, f32[512,128]{1,0:T(8,128)S(1)}, u32[]{:S(2)}, u32[]{:S(2)}) collective-permute-start(f32[512,128]{1,0:T(8,128)S(1)} %bitcast.10), channel_id=1, source_target_pairs={{0,32},{32,0},{1,33},{33,1},{2,34},{34,2},{3,35},{35,3},{4,36},{36... | collective-permute-start | bytes 786440 | tf_op jit(solution)/shard_map/ppermute | solution.py:448
  29.1 3.9 %collective-permute-start.4 = (f32[16,128]{1,0:T(8,128)S(1)}, f32[16,128]{1,0:T(8,128)S(1)}, u32[]{:S(2)}, u32[]{:S(2)}) collective-permute-start(f32[16,128]{1,0:T(8,128)S(1)} %extract.1.own_ref), channel_id=1, source_target_pairs={{0,24},{8,0},{16,8},{24,16},{1,25},{9,1},{17,9},{25,17},{2,26},{10... | collective-permute-start | bytes 24584 | tf_op jit(solution)/shard_map/ppermute | solution.py:438
  31.9 4.0 %collective-permute-start.3 = (f32[16,128]{1,0:T(8,128)S(1)}, f32[16,128]{1,0:T(8,128)S(1)}, u32[]{:S(2)}, u32[]{:S(2)}) collective-permute-start(f32[16,128]{1,0:T(8,128)S(1)} %extract.1.own_ref), channel_id=1, source_target_pairs={{0,16},{8,24},{16,0},{24,8},{1,17},{9,25},{17,1},{25,9},{2,18},{10... | collective-permute-start | bytes 24584 | tf_op jit(solution)/shard_map/ppermute | solution.py:438
  32.2 3.7 %collective-permute-start.2 = (f32[16,128]{1,0:T(8,128)S(1)}, f32[16,128]{1,0:T(8,128)S(1)}, u32[]{:S(2)}, u32[]{:S(2)}) collective-permute-start(f32[16,128]{1,0:T(8,128)S(1)} %extract.1.own_ref), channel_id=1, source_target_pairs={{0,8},{8,16},{16,24},{24,0},{1,9},{9,17},{17,25},{25,1},{2,10},{10... | collective-permute-start | bytes 24584 | tf_op jit(solution)/shard_map/ppermute | solution.py:438
  49.2 2.8 %collective-permute-start.7 = (f32[16,128]{1,0:T(8,128)S(1)}, f32[16,128]{1,0:T(8,128)S(1)}, u32[]{:S(2)}, u32[]{:S(2)}) collective-permute-start(f32[16,128]{1,0:T(8,128)S(1)} %pairs.1.own_ref), channel_id=1, source_target_pairs={{0,24},{8,0},{16,8},{24,16},{1,25},{9,1},{17,9},{25,17},{2,26},{10... | collective-permute-start | bytes 24584 | tf_op jit(solution)/shard_map/ppermute | solution.py:438
  49.8 4.0 %collective-permute-start.6 = (f32[16,128]{1,0:T(8,128)S(1)}, f32[16,128]{1,0:T(8,128)S(1)}, u32[]{:S(2)}, u32[]{:S(2)}) collective-permute-start(f32[16,128]{1,0:T(8,128)S(1)} %pairs.1.own_ref), channel_id=1, source_target_pairs={{0,16},{8,24},{16,0},{24,8},{1,17},{9,25},{17,1},{25,9},{2,18},{10... | collective-permute-start | bytes 24584 | tf_op jit(solution)/shard_map/ppermute | solution.py:438
  51.0 3.7 %collective-permute-start.5 = (f32[16,128]{1,0:T(8,128)S(1)}, f32[16,128]{1,0:T(8,128)S(1)}, u32[]{:S(2)}, u32[]{:S(2)}) collective-permute-start(f32[16,128]{1,0:T(8,128)S(1)} %pairs.1.own_ref), channel_id=1, source_target_pairs={{0,8},{8,16},{16,24},{24,0},{1,9},{9,17},{17,25},{25,1},{2,10},{10... | collective-permute-start | bytes 24584 | tf_op jit(solution)/shard_map/ppermute | solution.py:438
  55.4 5.4 %copy-start = (f32[12,2048]{1,0:T(8,128)S(1)}, f32[12,2048]{1,0:T(8,128)}, u32[]{:S(2)}) copy-start(f32[12,2048]{1,0:T(8,128)} %state_ref.5) | copy-start | bytes 294916
  55.4 14.6 %all-to-all-start.2 = ((f32[32,8,128]{2,1,0:T(8,128)}), f32[32,8,128]{2,1,0:T(8,128)S(1)}, u32[]{:S(2)}, u32[]{:S(2)}) async-start(f32[32,8,128]{2,1,0:T(8,128)} %get-tuple-element.109), calls=%async_computation.2 | async-start | bytes 262144 | tf_op jit(solution)/shard_map/all_to_all | solution.py:446
  59.4 1.4 %copy-start.1 = (f32[2048]{0:T(1024)S(1)}, f32[2048]{0:T(1024)}, u32[]{:S(2)}) copy-start(f32[2048]{0:T(1024)} %param.9) | copy-start | bytes 24580
  70.1 1.4 %collective-permute-start.8 = (f32[256,128]{1,0:T(8,128)S(1)}, f32[256,128]{1,0:T(8,128)S(1)}, u32[]{:S(2)}, u32[]{:S(2)}) collective-permute-start(f32[256,128]{1,0:T(8,128)S(1)} %bitcast.14), channel_id=1, source_target_pairs={{0,32},{32,0},{1,33},{33,1},{2,34},{34,2},{3,35},{35,3},{4,36},{36... | collective-permute-start | bytes 393224 | tf_op jit(solution)/shard_map/ppermute | solution.py:448
  73.4 0.7 copy-start.3
  73.4 0.7 copy-start.4
